TPU v7x, 32 devices: a whole 2x2x4 slice. The times are simulated.
32 devices in a mesh: section: 2 (over core), dp: 16 (over z, y, x).
Axes of the slice: x: 2, y: 2, z: 4, core: 2. Of those that a mesh axis runs over, the one named last changes fastest.
Arguments:
- z_noise: float32 [96, 256, 256], P('dp'), may hold values from -6 to 6
- eps_noise: float32 [96, 256, 256], P('dp'), may hold values from -6 to 6
- levels: int32 [96], P('dp'), may hold values from 0 to 999
- counts: int32 [16], P('dp'), may hold values from 1 to 6, as said below
- gen_w: float32 [2, 6656, 256], P('section', 'dp')
- gen_m: float32 [2, 6656, 256], P('section', 'dp'), may hold values from -9.536743e-07 to 9.536743e-07
- gen_v: float32 [2, 6656, 256], P('section', 'dp'), may hold values from 1.4648437e-16 to 2.3498534e-15
- gen_ema: float32 [2, 6656, 256], P('section', 'dp')
- gen_small: float32 [2, 13, 256], P('section')
- gen_small_m: float32 [2, 13, 256], P('section'), may hold values from -3.8146973e-06 to 3.8146973e-06
- gen_small_v: float32 [2, 13, 256], P('section'), may hold values from 2.3498534e-15 to 3.753662e-14
- gen_small_ema: float32 [2, 13, 256], P('section')
- fake_w: float32 [2, 6656, 256], P('section', 'dp')
- fake_m: float32 [2, 6656, 256], P('section', 'dp'), may hold values from -9.536743e-07 to 9.536743e-07
- fake_v: float32 [2, 6656, 256], P('section', 'dp'), may hold values from 1.4648437e-16 to 2.3498534e-15
- fake_small: float32 [2, 13, 256], P('section')
- fake_small_m: float32 [2, 13, 256], P('section'), may hold values from -3.8146973e-06 to 3.8146973e-06
- fake_small_v: float32 [2, 13, 256], P('section'), may hold values from 2.3498534e-15 to 3.753662e-14
- teacher_w: bfloat16 [2, 6656, 256], P('section', 'dp')
- teacher_small: float32 [2, 13, 256], P('section')
Outputs:
- gen_w_out: float32 [2, 6656, 256], P('section', 'dp')
- gen_m_out: float32 [2, 6656, 256], P('section', 'dp')
- gen_v_out: float32 [2, 6656, 256], P('section', 'dp')
- gen_ema_out: float32 [2, 6656, 256], P('section', 'dp')
- gen_small_out: float32 [2, 13, 256], P('section')
- gen_small_m_out: float32 [2, 13, 256], P('section')
- gen_small_v_out: float32 [2, 13, 256], P('section')
- gen_small_ema_out: float32 [2, 13, 256], P('section')
- fake_w_out: float32 [2, 6656, 256], P('section', 'dp')
- fake_m_out: float32 [2, 6656, 256], P('section', 'dp')
- fake_v_out: float32 [2, 6656, 256], P('section', 'dp')
- fake_small_out: float32 [2, 13, 256], P('section')
- fake_small_m_out: float32 [2, 13, 256], P('section')
- fake_small_v_out: float32 [2, 13, 256], P('section')
- norms: float32 [2], replicated
- losses: float32 [2], replicated
Inputs may be any that keep to these rules, and one draw needn't show every extreme that they name: `counts`: some group has all 6 images counting and some group exactly one.
All inputs are finite; a program needn't handle non-finite values.
Results may differ from a plain program's by a relative error of at most 0.0093.
Values may be sent and summed in bfloat16 or wider, within the bound.
A program may use at most 192 MiB of HBM per device.

v0:
```python
import jax
import jax.numpy as jnp
from jax import lax
from jax.sharding import PartitionSpec as P

GROUPS = 32
SIDE = 16
MICRO = 3
IMG_MB = 2
LEVELS = 1000
STEP = 10


SIGMA_DATA = 0.5
SIGMA_INIT = 2.5
SIGMA_LOW = 0.05
SIGMA_HIGH = 20.0
RHO_POWER = 7.0
ALPHA_MIX = 1.2
RESIDUAL_SCALE = 0.7071067811865476
NORM_EPS = 1e-05
CLIP_NORM = 0.001
LEARN_RATE = 0.15
BETA_ONE = 0.9
BETA_TWO = 0.999
ADAM_EPS = 1e-08
WEIGHT_DECAY = 0.01


def shifted_2(array, axis, by):
    count = lax.axis_size(axis)
    pairs = [(i, i + by) for i in range(count) if 0 <= i + by < count]
    return lax.ppermute(array, axis, pairs)


def for_sending(array):
    return jax.tree.map(lambda a: a.astype(jnp.bfloat16) if a.dtype == jnp.float32 else a, array)


def spread(value, axis, source):
    kept = jnp.where(lax.axis_index(axis) == source, value, 0).astype(value.dtype)
    return lax.psum(kept, axis)


def sigma_levels(level_ids):
    fraction = level_ids.astype(jnp.float32) / (LEVELS - 1)
    top_root = SIGMA_HIGH ** (1.0 / RHO_POWER)
    bottom_root = SIGMA_LOW ** (1.0 / RHO_POWER)
    return (top_root + fraction * (bottom_root - top_root)) ** RHO_POWER


def precondition(sigma_vals):
    total = sigma_vals * sigma_vals + SIGMA_DATA**2
    return (
        lax.rsqrt(total),
        SIGMA_DATA**2 / total,
        sigma_vals * SIGMA_DATA * lax.rsqrt(total),
        total / (sigma_vals * sigma_vals * SIGMA_DATA**2),
    )


def noise_embed(sigma_vals, channel_count):
    frequency = (1.0 / 10000.0) ** (jnp.arange(channel_count, dtype=jnp.float32) / channel_count)
    angles = (jnp.log(sigma_vals) / 4.0)[..., None] * frequency
    return jnp.concatenate([jnp.cos(angles), jnp.sin(angles)], axis=-1)


def expand(values):
    return values[:, :, None, None]


def matrix_product(left, right, pattern):
    return jnp.einsum(pattern, left, right, preferred_element_type=jnp.float32)


def norm_forward(values, gain_vec, bias_vec):
    img_count, pos_count, channel_count = values.shape
    grouped = values.reshape(img_count, pos_count, GROUPS, channel_count // GROUPS)
    mean_val = jnp.mean(grouped, axis=(1, 3), keepdims=True)
    centred = grouped - mean_val
    inv_std = lax.rsqrt(jnp.mean(centred * centred, axis=(1, 3), keepdims=True) + NORM_EPS)
    normed = (centred * inv_std).reshape(values.shape)
    return (normed * gain_vec + bias_vec, normed, inv_std)


def norm_backward(grad_out, normed, inv_std, gain_vec):
    img_count, pos_count, channel_count = grad_out.shape
    split_shape = (img_count, pos_count, GROUPS, channel_count // GROUPS)
    grad_norm = (grad_out * gain_vec).reshape(split_shape)
    grouped = normed.reshape(split_shape)
    mean_grad = jnp.mean(grad_norm, axis=(1, 3), keepdims=True)
    mean_cross = jnp.mean(grad_norm * grouped, axis=(1, 3), keepdims=True)
    grad_in = (inv_std * (grad_norm - mean_grad - grouped * mean_cross)).reshape(grad_out.shape)
    return (grad_in, jnp.sum(grad_out * normed, axis=(0, 1)), jnp.sum(grad_out, axis=(0, 1)))


def silu_slope(values):
    logistic = jax.nn.sigmoid(values)
    return logistic * (1.0 + values * (1.0 - logistic))


def conv_columns(acts):
    img_count, pos_count, channel_count = acts.shape
    grid_vals = acts.reshape(img_count, SIDE, SIDE, channel_count)
    padded = jnp.pad(grid_vals, ((0, 0), (1, 1), (1, 1), (0, 0)))
    pieces = [
        padded[:, row_off : row_off + SIDE, col_off : col_off + SIDE, :]
        for row_off in range(3)
        for col_off in range(3)
    ]
    return jnp.concatenate(pieces, axis=-1).reshape(img_count, pos_count, 9 * channel_count)


def conv_transpose(grad_cols):
    img_count, pos_count, wide_chans = grad_cols.shape
    channel_count = wide_chans // 9
    pieces = grad_cols.reshape(img_count, SIDE, SIDE, 9, channel_count)
    summed = jnp.zeros((img_count, SIDE + 2, SIDE + 2, channel_count), jnp.float32)
    for row_off in range(3):
        for col_off in range(3):
            summed = summed + jnp.pad(
                pieces[:, :, :, 3 * row_off + col_off],
                ((0, 0), (row_off, 2 - row_off), (col_off, 2 - col_off), (0, 0)),
            )
    return summed[:, 1:-1, 1:-1].reshape(img_count, pos_count, channel_count)


def split_big(big_w):
    channel_count = big_w.shape[1]
    return (
        big_w[: 9 * channel_count],
        big_w[9 * channel_count : 18 * channel_count],
        big_w[18 * channel_count : 22 * channel_count].reshape(
            2 * channel_count, 2 * channel_count
        ),
        big_w[22 * channel_count : 25 * channel_count].reshape(channel_count, 3 * channel_count),
        big_w[25 * channel_count :],
    )


def layer_forward(big_w, small_w, inputs, embed_b):
    channel_count = inputs.shape[2]
    conv_one, conv_two, embed_w, qkv_w, proj_w = split_big(big_w)
    norm_one, normed_one, inv_one = norm_forward(inputs, small_w[0], small_w[1])
    columns_one = conv_columns(jax.nn.silu(norm_one).astype(jnp.bfloat16))
    hidden_one = matrix_product(columns_one, conv_one, "bpk,kc->bpc") + small_w[2]
    modul = matrix_product(embed_b, embed_w, "bk,kc->bc") + jnp.concatenate(
        [small_w[5], small_w[6]]
    )
    norm_two, normed_two, inv_two = norm_forward(hidden_one, small_w[3], small_w[4])
    pre_two = norm_two * (1.0 + modul[:, None, :channel_count]) + modul[:, None, channel_count:]
    columns_two = conv_columns(jax.nn.silu(pre_two).astype(jnp.bfloat16))
    hidden_two = matrix_product(columns_two, conv_two, "bpk,kc->bpc") + small_w[7]
    middle = (inputs + hidden_two) * RESIDUAL_SCALE
    norm_three, normed_three, inv_three = norm_forward(middle, small_w[8], small_w[9])
    attn_in = norm_three.astype(jnp.bfloat16)
    qkv_bias = jnp.concatenate([small_w[10], jnp.zeros_like(small_w[10]), small_w[11]])
    qkv_all = (matrix_product(attn_in, qkv_w, "bpc,cd->bpd") + qkv_bias).astype(jnp.bfloat16)
    query_rows = qkv_all[..., :channel_count]
    gathered_keys = qkv_all[..., channel_count : 2 * channel_count]
    gathered_values = qkv_all[..., 2 * channel_count :]
    attention_scores = matrix_product(
        query_rows, gathered_keys, "zhr,zmr->zhm"
    ) * channel_count ** (-0.5)
    attention_probabilities = jax.nn.softmax(attention_scores, axis=-1)
    lowered_probabilities = attention_probabilities.astype(jnp.bfloat16)
    attention_output = matrix_product(
        lowered_probabilities, gathered_values, "ous,osg->oug"
    ).astype(jnp.bfloat16)
    projected = matrix_product(attention_output, proj_w, "bpc,cd->bpd") + small_w[12]
    outputs = (middle + projected) * RESIDUAL_SCALE
    saved_vals = (
        normed_one,
        inv_one,
        norm_one,
        columns_one,
        modul,
        normed_two,
        inv_two,
        norm_two,
        pre_two,
        columns_two,
        normed_three,
        inv_three,
        attn_in,
        query_rows,
        gathered_keys,
        gathered_values,
        attention_probabilities,
        lowered_probabilities,
        attention_output,
    )
    return (outputs, saved_vals)


def column_sum(values):
    return jnp.sum(values.astype(jnp.float32), axis=(0, 1))


def layer_backward(big_w, small_w, embed_b, saved_vals, grad_out, want_weights):
    (
        normed_one,
        inv_one,
        norm_one,
        columns_one,
        modul,
        normed_two,
        inv_two,
        norm_two,
        pre_two,
        columns_two,
        normed_three,
        inv_three,
        attn_in,
        query_rows,
        gathered_keys,
        gathered_values,
        attention_probabilities,
        lowered_probabilities,
        attention_output,
    ) = saved_vals
    channel_count = grad_out.shape[2]
    conv_one, conv_two, embed_w, qkv_w, proj_w = split_big(big_w)
    grad_proj = (grad_out * RESIDUAL_SCALE).astype(jnp.bfloat16)
    attention_gradient = matrix_product(grad_proj, proj_w, "bpd,cd->bpc").astype(jnp.bfloat16)
    probability_gradient = matrix_product(attention_gradient, gathered_values, "zhr,zmr->zhm")
    value_gradient = matrix_product(lowered_probabilities, attention_gradient, "woz,wop->wzp")
    score_gradient = (
        attention_probabilities
        * (
            probability_gradient
            - jnp.sum(probability_gradient * attention_probabilities, axis=-1, keepdims=True)
        )
    ).astype(jnp.bfloat16)
    attention_scale = channel_count ** (-0.5)
    query_gradient = matrix_product(score_gradient, gathered_keys, "ous,osg->oug") * attention_scale
    key_gradient = matrix_product(score_gradient, query_rows, "woz,wop->wzp") * attention_scale
    grad_qkv = jnp.concatenate([query_gradient, key_gradient, value_gradient], axis=-1).astype(
        jnp.bfloat16
    )
    grad_three, gain_eight, bias_nine = norm_backward(
        matrix_product(grad_qkv, qkv_w, "bpd,cd->bpc"), normed_three, inv_three, small_w[8]
    )
    grad_middle = grad_out * RESIDUAL_SCALE + grad_three
    grad_hidden_two = (grad_middle * RESIDUAL_SCALE).astype(jnp.bfloat16)
    grad_pre_two = conv_transpose(
        matrix_product(grad_hidden_two, conv_two, "bpc,kc->bpk")
    ) * silu_slope(pre_two)
    grad_modul = jnp.concatenate(
        [jnp.sum(grad_pre_two * norm_two, axis=1), jnp.sum(grad_pre_two, axis=1)], axis=-1
    )
    grad_two, gain_three, bias_four = norm_backward(
        grad_pre_two * (1.0 + modul[:, None, :channel_count]), normed_two, inv_two, small_w[3]
    )
    grad_hidden_one = grad_two.astype(jnp.bfloat16)
    grad_norm_one = conv_transpose(
        matrix_product(grad_hidden_one, conv_one, "bpc,kc->bpk")
    ) * silu_slope(norm_one)
    grad_one, gain_zero, bias_one = norm_backward(grad_norm_one, normed_one, inv_one, small_w[0])
    grad_inputs = grad_middle * RESIDUAL_SCALE + grad_one
    if not want_weights:
        return (grad_inputs, None)
    big_grad = jnp.concatenate(
        [
            matrix_product(columns_one, grad_hidden_one, "bpk,bpc->kc"),
            matrix_product(columns_two, grad_hidden_two, "bpk,bpc->kc"),
            jnp.dot(
                embed_b.astype(jnp.float32).T, grad_modul, precision=lax.Precision.HIGHEST
            ).reshape(4 * channel_count, channel_count),
            matrix_product(attn_in, grad_qkv, "bpc,bpd->cd").reshape(
                3 * channel_count, channel_count
            ),
            matrix_product(attention_output, grad_proj, "bpc,bpd->cd"),
        ],
        axis=0,
    )
    modul_sum = jnp.sum(grad_modul, axis=0)
    bias_qkv = column_sum(grad_qkv)
    small_grad = jnp.stack(
        [
            gain_zero,
            bias_one,
            column_sum(grad_hidden_one),
            gain_three,
            bias_four,
            modul_sum[:channel_count],
            modul_sum[channel_count:],
            column_sum(grad_hidden_two),
            gain_eight,
            bias_nine,
            bias_qkv[:channel_count],
            bias_qkv[2 * channel_count :],
            column_sum(grad_proj),
        ]
    )
    return (grad_inputs, (big_grad, small_grad))


def forward_pass(nets, sources, embeds, section_idx):
    net_count = len(nets)

    def forward_tick(incoming, tick_index):
        index_mb = jnp.clip(tick_index - section_idx, 0, MICRO - 1)
        first_input = sources[jnp.minimum(tick_index, MICRO - 1)]
        fed_inputs = jnp.where(
            section_idx == 0, jnp.broadcast_to(first_input[None], incoming.shape), incoming
        )
        outputs = jnp.stack(
            [
                layer_forward(
                    nets[net_index][0], nets[net_index][1], fed_inputs[net_index], embeds[index_mb]
                )[0]
                for net_index in range(net_count)
            ]
        )
        shifted = shifted_2(outputs.astype(jnp.bfloat16), "section", 1).astype(outputs.dtype)
        return (shifted, (fed_inputs, outputs))

    initial = jnp.zeros((net_count,) + sources.shape[1:], jnp.float32)
    final_carry, (fed_all, out_all) = lax.scan(forward_tick, initial, jnp.arange(MICRO + 1))
    kept_in = lax.dynamic_slice_in_dim(fed_all, section_idx, MICRO, 0)
    return (kept_in, out_all[1:])


def backward_pass(nets, kept_in, embeds, cot_stack, job_list, section_idx):

    def backward_tick(carry, tick_index):
        incoming, totals = carry
        mb_offset = tick_index - 1 + section_idx
        index_mb = jnp.clip(mb_offset, 0, MICRO - 1)
        live_tick = ((mb_offset >= 0) & (mb_offset < MICRO)).astype(jnp.float32)
        fed_grads = jnp.where(
            section_idx == 1, cot_stack[jnp.minimum(tick_index, MICRO - 1)], incoming
        )
        saved_all = [
            layer_forward(
                nets[net_index][0],
                nets[net_index][1],
                kept_in[index_mb, net_index],
                embeds[index_mb],
            )[1]
            for net_index in range(len(nets))
        ]
        grad_list = []
        new_totals = []
        for job_index, (net_index, want_weights) in enumerate(job_list):
            grad_in, weight_grads = layer_backward(
                nets[net_index][0],
                nets[net_index][1],
                embeds[index_mb],
                saved_all[net_index],
                fed_grads[job_index],
                want_weights,
            )
            grad_list.append(grad_in)
            if want_weights:
                running = totals[len(new_totals)]
                new_totals.append(
                    tuple(
                        (held + live_tick * addend for held, addend in zip(running, weight_grads))
                    )
                )
        stacked = jnp.stack(grad_list)
        shifted = shifted_2(for_sending(stacked), "section", -1).astype(stacked.dtype)
        return ((shifted, tuple(new_totals)), stacked)

    initial_totals = tuple(
        (
            (
                jnp.zeros(nets[net_index][0].shape, jnp.float32),
                jnp.zeros(nets[net_index][1].shape, jnp.float32),
            )
            for net_index, want_weights in job_list
            if want_weights
        )
    )
    initial = (jnp.zeros(cot_stack.shape[1:], jnp.float32), initial_totals)
    (final_grads, totals), grads_all = lax.scan(backward_tick, initial, jnp.arange(MICRO + 1))
    return (totals, grads_all[1:])


def adam_step(master, first_mom, second_mom, grad):
    first_new = BETA_ONE * first_mom + (1.0 - BETA_ONE) * grad
    second_new = BETA_TWO * second_mom + (1.0 - BETA_TWO) * grad * grad
    direction = (
        first_new
        / (1.0 - BETA_ONE**STEP)
        / (jnp.sqrt(second_new / (1.0 - BETA_TWO**STEP)) + ADAM_EPS)
    )
    return (master - LEARN_RATE * (direction + WEIGHT_DECAY * master), first_new, second_new)


def shards(
    z_noise,
    eps_noise,
    levels,
    counts,
    gen_w,
    gen_m,
    gen_v,
    gen_ema,
    gen_small,
    gen_small_m,
    gen_small_v,
    gen_small_ema,
    fake_w,
    fake_m,
    fake_v,
    fake_small,
    fake_small_m,
    fake_small_v,
    teacher_w,
    teacher_small,
):
    section_idx = lax.axis_index("section")
    dp_index = lax.axis_index("dp")
    num_points = z_noise.shape[1]
    channel_count = z_noise.shape[2]
    grid_shape = (MICRO, IMG_MB, num_points, channel_count)
    ema_rate = 0.5 ** (20.0 / STEP)
    local_count = counts[0]
    valid_mask = (
        (jnp.arange(MICRO * IMG_MB) < local_count).astype(jnp.float32).reshape(MICRO, IMG_MB)
    )
    count_total = lax.psum(local_count.astype(jnp.float32), "dp")
    init_sigma = jnp.full((MICRO, IMG_MB), SIGMA_INIT, jnp.float32)
    gen_terms = precondition(init_sigma)
    raw_gen = SIGMA_INIT * z_noise.reshape(grid_shape)
    gen_embed = noise_embed(init_sigma, channel_count).astype(jnp.bfloat16)
    sigma_vals = sigma_levels(levels).reshape(MICRO, IMG_MB)
    score_terms = precondition(sigma_vals)
    score_embed = noise_embed(sigma_vals, channel_count).astype(jnp.bfloat16)
    eps_grid = eps_noise.reshape(grid_shape)
    rows_local = gen_w.shape[1]
    elements = num_points * channel_count
    gen_big, fake_big, teacher_big = (
        lax.all_gather(gen_w[0].astype(jnp.bfloat16), "dp", axis=0, tiled=True),
        lax.all_gather(fake_w[0].astype(jnp.bfloat16), "dp", axis=0, tiled=True),
        lax.all_gather(teacher_w[0], "dp", axis=0, tiled=True),
    )
    gen_net = (gen_big, gen_small[0])
    fake_net = (fake_big, fake_small[0])
    teacher_net = (teacher_big, teacher_small[0])
    gen_in, gen_skip, gen_out = (expand(gen_terms[0]), expand(gen_terms[1]), expand(gen_terms[2]))
    gen_kept, gen_result = forward_pass((gen_net,), gen_in * raw_gen, gen_embed, section_idx)
    samples = gen_skip * raw_gen + gen_out * gen_result[:, 0]
    samples = spread(samples.astype(jnp.bfloat16), "section", 1).astype(samples.dtype)
    score_in, score_skip, score_out, weight_lam = [expand(term) for term in score_terms]
    noisy_in = samples + expand(sigma_vals) * eps_grid
    score_kept, score_result = forward_pass(
        (teacher_net, fake_net), score_in * noisy_in, score_embed, section_idx
    )
    teacher_den = score_skip * noisy_in + score_out * score_result[:, 0]
    fake_den = score_skip * noisy_in + score_out * score_result[:, 1]
    factor = expand(valid_mask) * weight_lam / elements
    gap_den = teacher_den - fake_den
    miss_den = fake_den - samples
    on_last = (section_idx == 1).astype(jnp.float32)
    loss_gen = on_last * jnp.sum(
        factor * ((1.0 - ALPHA_MIX) * gap_den * gap_den + gap_den * miss_den)
    )
    loss_fake = on_last * jnp.sum(factor * miss_den * miss_den)
    grad_teacher = factor * (2.0 * (1.0 - ALPHA_MIX) * gap_den + miss_den)
    grad_fake = factor * (gap_den - 2.0 * (1.0 - ALPHA_MIX) * gap_den - miss_den)
    direct = score_skip * (grad_teacher + grad_fake) - factor * gap_den
    cot_stack = jnp.stack(
        [score_out * grad_teacher, score_out * 2.0 * factor * miss_den, score_out * grad_fake],
        axis=1,
    )
    fake_sums, score_grads = backward_pass(
        (teacher_net, fake_net),
        score_kept,
        score_embed,
        cot_stack,
        ((0, False), (1, True), (1, False)),
        section_idx,
    )
    back_noisy = score_in * (score_grads[:, 0] + score_grads[:, 2])
    back_noisy = spread(for_sending(back_noisy), "section", 0).astype(back_noisy.dtype)
    gen_cot = gen_out * (direct + back_noisy)
    gen_sums, gen_input_grads = backward_pass(
        (gen_net,), gen_kept, gen_embed, gen_cot[:, None], ((0, True),), section_idx
    )
    gen_big_g, gen_small_g = gen_sums[0]
    fake_big_g, fake_small_g = fake_sums[0]
    whole_gen, whole_fake = lax.psum((gen_big_g, fake_big_g), "dp")
    gen_shard = lax.dynamic_slice_in_dim(whole_gen, dp_index * rows_local, rows_local, 0)
    fake_shard = lax.dynamic_slice_in_dim(whole_fake, dp_index * rows_local, rows_local, 0)
    gen_small_sum, fake_small_sum = lax.psum((gen_small_g, fake_small_g), "dp")
    first_dp = (dp_index == 0).astype(jnp.float32)
    square_gen = jnp.sum(gen_shard * gen_shard) + first_dp * jnp.sum(gen_small_sum * gen_small_sum)
    square_fake = jnp.sum(fake_shard * fake_shard) + first_dp * jnp.sum(
        fake_small_sum * fake_small_sum
    )
    square_gen_all, square_fake_all, gen_total, fake_total = lax.psum(
        (square_gen, square_fake, loss_gen, loss_fake), ("section", "dp")
    )
    norm_gen = jnp.sqrt(square_gen_all) / count_total
    norm_fake = jnp.sqrt(square_fake_all) / count_total
    scale_gen = jnp.minimum(1.0, CLIP_NORM / norm_gen) / count_total
    scale_fake = jnp.minimum(1.0, CLIP_NORM / norm_fake) / count_total
    gen_w_out, gen_m_out, gen_v_out = adam_step(gen_w[0], gen_m[0], gen_v[0], gen_shard * scale_gen)
    gen_small_out, gen_small_m_out, gen_small_v_out = adam_step(
        gen_small[0], gen_small_m[0], gen_small_v[0], gen_small_sum * scale_gen
    )
    fake_w_out, fake_m_out, fake_v_out = adam_step(
        fake_w[0], fake_m[0], fake_v[0], fake_shard * scale_fake
    )
    fake_small_out, fake_small_m_out, fake_small_v_out = adam_step(
        fake_small[0], fake_small_m[0], fake_small_v[0], fake_small_sum * scale_fake
    )
    gen_ema_out = ema_rate * gen_ema[0] + (1.0 - ema_rate) * gen_w_out
    gen_small_ema_out = ema_rate * gen_small_ema[0] + (1.0 - ema_rate) * gen_small_out
    norms = jnp.stack([norm_gen, norm_fake])
    losses = jnp.stack([gen_total, fake_total]) / count_total
    return (
        gen_w_out[None],
        gen_m_out[None],
        gen_v_out[None],
        gen_ema_out[None],
        gen_small_out[None],
        gen_small_m_out[None],
        gen_small_v_out[None],
        gen_small_ema_out[None],
        fake_w_out[None],
        fake_m_out[None],
        fake_v_out[None],
        fake_small_out[None],
        fake_small_m_out[None],
        fake_small_v_out[None],
        norms,
        losses,
    )


def solution(mesh):
    return jax.shard_map(
        shards,
        mesh=mesh,
        in_specs=(
            P("dp", None, None),
            P("dp", None, None),
            P("dp"),
            P("dp"),
            P("section", "dp", None),
            P("section", "dp", None),
            P("section", "dp", None),
            P("section", "dp", None),
            P("section", None, None),
            P("section", None, None),
            P("section", None, None),
            P("section", None, None),
            P("section", "dp", None),
            P("section", "dp", None),
            P("section", "dp", None),
            P("section", None, None),
            P("section", None, None),
            P("section", None, None),
            P("section", "dp", None),
            P("section", None, None),
        ),
        out_specs=(
            P("section", "dp", None),
            P("section", "dp", None),
            P("section", "dp", None),
            P("section", "dp", None),
            P("section", None, None),
            P("section", None, None),
            P("section", None, None),
            P("section", None, None),
            P("section", "dp", None),
            P("section", "dp", None),
            P("section", "dp", None),
            P("section", None, None),
            P("section", None, None),
            P("section", None, None),
            P(),
            P(),
        ),
        check_vma=False,
    )
```

profile of v0, /device:TPU:0, one launch (start us, length us, event | category | flops | bytes accessed | tf_op | source)
XLA Modules:
  0.0 2305.2 jit_solution(16277880812409428424)
XLA Ops:
  14.4 69.9 %all-gather.5.cloned.1.call-done = bf16[6656,256]{1,0:T(8,128)(2,1)} async-done(((bf16[416,256]{1,0:T(8,128)(2,1)}), bf16[6656,256]{1,0:T(8,128)(2,1)}) %all-gather.5.cloned.1.call-update) | async-done | bytes 3407888 | tf_op jit(solution)/shard_map/all_gather | solution.py:437
  84.9 88.4 %while.70 = (s32[]{:T(128)}, f32[1,2,256,256]{3,2,1,0:T(8,128)S(1)}, f32[4,1,2,256,256]{4,3,2,1,0:T(8,128)}, f32[4,1,2,256,256]{4,3,2,1,0:T(8,128)}, pred[]{:T(5...) while((s32[]{:T(128)}, ...), condition=%wide.region_15.16_spmd.clone, body=%wide.region_0.15_spmd.clone.sunk | while | flops 1689522304 | bytes 41352020 | solution.py:320
  181.5 13.4 all-reduce.91.cloned.1.call-done
  197.5 72.6 %all-gather.7.cloned.1.call-done = bf16[6656,256]{1,0:T(8,128)(2,1)} async-done(((bf16[416,256]{1,0:T(8,128)(2,1)}), bf16[6656,256]{1,0:T(8,128)(2,1)}) %all-gather.7.cloned.1.call-update) | async-done | bytes 3407888 | tf_op jit(solution)/shard_map/all_gather | solution.py:438
  270.1 71.8 %all-gather.9.cloned.1.call-done = bf16[1,6656,256]{2,1,0:T(8,128)(2,1)} async-done(((bf16[1,416,256]{2,1,0:T(8,128)(2,1)}), bf16[1,6656,256]{2,1,0:T(8,128)(2,1)}) %all-gather.9.cloned.1.call-update) | async-done | bytes 3407888 | tf_op jit(solution)/shard_map/all_gather | solution.py:439
  341.9 236.2 %while.71 = (s32[]{:T(128)}, f32[2,2,256,256]{3,2,1,0:T(8,128)}, f32[4,2,2,256,256]{4,3,2,1,0:T(8,128)}, f32[4,2,2,256,256]{4,3,2,0,1:T(8,128)}, pred[]{:T(512)}...) while((s32[]{:T(128)}, f32[2,2,256,256]{3,2,1,0:T(8,128)}, ...), condition=%wide.region_46.47_spmd.clone, body=%wide.region_17.46_spmd.clone.sunk | while | flops 3379307008 | bytes 98101408 | solution.py:320
  590.0 959.6 %while.72 = (s32[]{:T(128)}, f32[3,2,256,256]{3,2,1,0:T(8,128)}, f32[6656,256]{1,0:T(8,128)}, f32[13,256]{1,0:T(8,128)}, f32[4,3,2,256,256]{4,3,2,0,1:T(8,128)},...) while((s32[]{:T(128)}, f32[3,2,256,256]{3,2,1,0:T(8,128)}, ...), condition=%wide.region_128.129_spmd.clone, body=%wide.region_47.128_spmd.clone.sunk | while | flops 10023246848 | bytes 414936608 | solution.py:378
  617.9 4.3 fusion.888
  814.4 6.6 select_add_fusion.8
  853.0 4.3 fusion.888
  1049.5 8.5 select_add_fusion.8
  1090.1 4.3 fusion.888
  1286.6 8.5 select_add_fusion.8
  1327.4 4.3 fusion.888
  1523.9 8.5 select_add_fusion.8
  1555.6 19.6 all-reduce.93.cloned.1.call-done
  1578.7 268.4 %while.73 = (s32[]{:T(128)}, f32[1,2,256,256]{3,2,1,0:T(8,128)S(1)}, f32[6656,256]{1,0:T(8,128)}, f32[13,256]{1,0:T(8,128)}, pred[]{:T(512)}, /*index=5*/s32[4]{...) while((s32[]{:T(128)}, ...), condition=%wide.region_171.172_spmd.clone, body=%wide.region_130.171_spmd.clone.sunk | while | flops 4880486400 | bytes 207928336 | solution.py:378
  1636.7 6.7 select_add_fusion.10
  1702.4 8.6 select_add_fusion.10
  1769.9 8.6 select_add_fusion.10
  1837.5 8.6 select_add_fusion.10
  1848.8 81.7 %all-reduce.85 = (f32[]{:T(128)}, f32[13,256]{1,0:T(8,128)S(1)}, f32[13,256]{1,0:T(8,128)S(1)}) all-reduce(f32[]{:T(128)S(6)} %convert_element_type.652, f32[13,256]{1,0:T(8,128)S(1)} %copy-done.115, f32[13,256]{1,0:T(8,128)S(1)} %copy-done.112), channel_id=1, replica_groups=mesh['section'=2,'dp'=16] {'dp'}, use_global_device_ids=true, to_apply=%region_173.174 | all-reduce | flops 6657 | bytes 53256 | tf_op jit(solution)/shard_map/psum | solution.py:425
  1933.7 302.1 %all-reduce.95.cloned.1.call-done = (f32[6656,256]{1,0:T(8,128)}, f32[6656,256]{1,0:T(8,128)}) async-done(((f32[6656,256]{1,0:T(8,128)}, f32[6656,256]{1,0:T(8,128)}), (f32[6656,256]{1,0:T(8,128)}, f32[6656,256]{1,0:T(8,128)})) %all-reduce.95.cloned.1.call-update) | async-done | bytes 13631504 | tf_op jit(solution)/shard_map/psum | solution.py:486
  2240.5 40.7 %all-reduce.84 = (f32[]{:T(128)}, f32[]{:T(128)}, f32[1]{0:T(128)}, f32[1]{0:T(128)}) all-reduce(f32[]{:T(128)S(6)} %add.2358, f32[]{:T(128)S(6)} %add.2369, f32[1]{0:T(128)} %bitcast.42, f32[1]{0:T(128)} %bitcast.41), channel_id=1, replica_groups=mesh['section'=2,'dp'=16] {'section','dp'}, use_global_device_ids=true, to_apply=%region_177.178 | all-reduce | flops 4 | bytes 32 | tf_op jit(solution)/shard_map/psum | solution.py:495
  (4294 shorter events, 1473.8 us)
Async XLA Ops:
  7.2 77.2 %all-gather.5.cloned.1.call-start = ((), (), s32[]{:S(2)}) async-start(), calls=%async_computation | async-start | bytes 3620864 | tf_op jit(solution)/shard_map/all_gather | solution.py:437
  9.0 185.9 %all-reduce.91.cloned.1.call-start = ((), (), s32[]{:S(2)}) async-start(), calls=%async_computation.1 | async-start | bytes 1572864 | tf_op jit(solution)/shard_map/psum | solution.py:42
  103.8 2.4 collective-permute-start
  125.1 3.4 collective-permute-start
  147.5 3.4 collective-permute-start
  169.8 3.4 collective-permute-start
  176.6 93.5 %all-gather.7.cloned.1.call-start = ((), (), s32[]{:S(2)}) async-start(), calls=%async_computation.2 | async-start | bytes 3620864 | tf_op jit(solution)/shard_map/all_gather | solution.py:438
  177.4 164.5 %all-gather.9.cloned.1.call-start = ((), (), s32[]{:S(2)}) async-start(), calls=%async_computation.4 | async-start | bytes 3620864 | tf_op jit(solution)/shard_map/all_gather | solution.py:439
  178.0 1397.2 %all-reduce.93.cloned.1.call-start = ((), (), s32[]{:S(2)}) async-start(), calls=%async_computation.3 | async-start | bytes 1572864 | tf_op jit(solution)/shard_map/psum | solution.py:42
  395.5 2.8 collective-permute-start.1
  454.1 3.8 collective-permute-start.1
  513.7 3.8 collective-permute-start.1
  573.2 3.8 collective-permute-start.1
  793.6 28.8 %collective-permute-start.2 = (bf16[3,2,256,256]{3,2,1,0:T(8,128)(2,1)}, bf16[3,2,256,256]{3,2,1,0:T(8,128)(2,1)}, u32[]{:S(2)}, u32[]{:S(2)}) collective-permute-start(bf16[3,2,256,256]{3,2,1,0:T(8,128)(2,1)} %fusion.908), channel_id=1, source_target_pairs={{16,0},{17,1},{18,2},{19,3},{20,4},{21,5},{22,6},{23,7},{24,8},{25... | collective-permute-start | bytes 2359304 | tf_op jit(solution)/shard_map/while/body/eval_jaxpr/ppermute | solution.py:33
  1029.0 30.6 %collective-permute-start.2 = (bf16[3,2,256,256]{3,2,1,0:T(8,128)(2,1)}, bf16[3,2,256,256]{3,2,1,0:T(8,128)(2,1)}, u32[]{:S(2)}, u32[]{:S(2)}) collective-permute-start(bf16[3,2,256,256]{3,2,1,0:T(8,128)(2,1)} %fusion.908), channel_id=1, source_target_pairs={{16,0},{17,1},{18,2},{19,3},{20,4},{21,5},{22,6},{23,7},{24,8},{25... | collective-permute-start | bytes 2359304 | tf_op jit(solution)/shard_map/while/body/eval_jaxpr/ppermute | solution.py:33
  1266.0 30.6 %collective-permute-start.2 = (bf16[3,2,256,256]{3,2,1,0:T(8,128)(2,1)}, bf16[3,2,256,256]{3,2,1,0:T(8,128)(2,1)}, u32[]{:S(2)}, u32[]{:S(2)}) collective-permute-start(bf16[3,2,256,256]{3,2,1,0:T(8,128)(2,1)} %fusion.908), channel_id=1, source_target_pairs={{16,0},{17,1},{18,2},{19,3},{20,4},{21,5},{22,6},{23,7},{24,8},{25... | collective-permute-start | bytes 2359304 | tf_op jit(solution)/shard_map/while/body/eval_jaxpr/ppermute | solution.py:33
  1503.1 30.8 %collective-permute-start.2 = (bf16[3,2,256,256]{3,2,1,0:T(8,128)(2,1)}, bf16[3,2,256,256]{3,2,1,0:T(8,128)(2,1)}, u32[]{:S(2)}, u32[]{:S(2)}) collective-permute-start(bf16[3,2,256,256]{3,2,1,0:T(8,128)(2,1)} %fusion.908), channel_id=1, source_target_pairs={{16,0},{17,1},{18,2},{19,3},{20,4},{21,5},{22,6},{23,7},{24,8},{25... | collective-permute-start | bytes 2359304 | tf_op jit(solution)/shard_map/while/body/eval_jaxpr/ppermute | solution.py:33
  1552.7 683.1 %all-reduce.95.cloned.1.call-start = ((), (), s32[]{:S(2)}) async-start(), calls=%async_computation.5 | async-start | bytes 27262976 | tf_op jit(solution)/shard_map/psum | solution.py:486
  1621.8 21.7 collective-permute-start.3
  1687.5 23.7 %collective-permute-start.3 = (bf16[1,2,256,256]{3,2,1,0:T(8,128)(2,1)}, bf16[1,2,256,256]{3,2,1,0:T(8,128)(2,1)S(1)}, u32[]{:S(2)}, u32[]{:S(2)}) collective-permute-start(bf16[1,2,256,256]{3,2,1,0:T(8,128)(2,1)} %bitcast.1788), channel_id=1, source_target_pairs={{16,0},{17,1},{18,2},{19,3},{20,4},{21,5},{22,6},{23,7},{24,8},{25... | collective-permute-start | bytes 786440 | tf_op jit(solution)/shard_map/while/body/eval_jaxpr/ppermute | solution.py:33
  1755.0 23.7 %collective-permute-start.3 = (bf16[1,2,256,256]{3,2,1,0:T(8,128)(2,1)}, bf16[1,2,256,256]{3,2,1,0:T(8,128)(2,1)S(1)}, u32[]{:S(2)}, u32[]{:S(2)}) collective-permute-start(bf16[1,2,256,256]{3,2,1,0:T(8,128)(2,1)} %bitcast.1788), channel_id=1, source_target_pairs={{16,0},{17,1},{18,2},{19,3},{20,4},{21,5},{22,6},{23,7},{24,8},{25... | collective-permute-start | bytes 786440 | tf_op jit(solution)/shard_map/while/body/eval_jaxpr/ppermute | solution.py:33
  1822.6 23.7 %collective-permute-start.3 = (bf16[1,2,256,256]{3,2,1,0:T(8,128)(2,1)}, bf16[1,2,256,256]{3,2,1,0:T(8,128)(2,1)S(1)}, u32[]{:S(2)}, u32[]{:S(2)}) collective-permute-start(bf16[1,2,256,256]{3,2,1,0:T(8,128)(2,1)} %bitcast.1788), channel_id=1, source_target_pairs={{16,0},{17,1},{18,2},{19,3},{20,4},{21,5},{22,6},{23,7},{24,8},{25... | collective-permute-start | bytes 786440 | tf_op jit(solution)/shard_map/while/body/eval_jaxpr/ppermute | solution.py:33
  1847.3 448.1 %copy-start.69 = (f32[1,416,256]{2,1,0:T(8,128)S(1)}, f32[1,416,256]{2,1,0:T(8,128)}, u32[]{:S(2)}) copy-start(f32[1,416,256]{2,1,0:T(8,128)} %param.32) | copy-start | bytes 1277956
  1847.3 448.1 %copy-start.130 = (f32[1,416,256]{2,1,0:T(8,128)S(1)}, f32[1,416,256]{2,1,0:T(8,128)}, u32[]{:S(2)}) copy-start(f32[1,416,256]{2,1,0:T(8,128)} %param.35) | copy-start | bytes 1277956
  (788 other events, 8703.4 us)
Sparse Core Ops, SparseCore 0:
  11.3 73.0 all-gather.4
  176.7 18.1 all-reduce.90
  198.5 71.4 all-gather.6
  273.0 68.8 all-gather.8
  1552.8 22.3 all-reduce.92
  1847.4 388.3 all-reduce.94
where the time goes:
time: 2330 us; the launch traced here: 2310 us
  waiting for transfers between devices  556 us (24%)
  local copies, waits for them, and re-layouts  551 us (24%)
  other arithmetic  494 us (21%)
  matrix products  476 us (20%)
  blocking collectives  122 us (5%)
  loops' own time  52.8 us (2%)
  starting transfers between devices  28.6 us (1%)
  between operations  24.8 us (1%)
    dot_general x280, matrix products, matrix_product(): return jnp.einsum(pattern, left, right, preferred_element_type=jnp.float32)  443 us
    psum x1, waiting for transfers between devices, shards(): whole_gen, whole_fake = lax.psum((gen_big_g, fake_big_g), 'dp')  302 us
    psum x1, blocking collectives, shards(): count_total = lax.psum(local_count.astype(jnp.float32), 'dp')  81.7 us
    while x1852, local copies, waits for them, and re-layouts  79.8 us
    all_gather x1, waiting for transfers between devices, shards(): lax.all_gather(fake_w[0].astype(jnp.bfloat16), 'dp', axis=0, tiled=True)  72.6 us
    all_gather x1, waiting for transfers between devices, shards(): lax.all_gather(teacher_w[0], 'dp', axis=0, tiled=True)  71.8 us
    all_gather x1, waiting for transfers between devices, shards(): lax.all_gather(gen_w[0].astype(jnp.bfloat16), 'dp', axis=0, tiled=True)  69.9 us
    add x16, other arithmetic, backward_tick(): held + live_tick * addend  64.8 us

commit v1 on v0

v1 whole, which is shorter than its diff:
```python
import functools

import jax
import jax.numpy as jnp
from jax import lax
from jax.experimental import pallas as pl
from jax.experimental.pallas import tpu as pltpu
from jax.sharding import PartitionSpec as P

GROUPS = 32
SIDE = 16
LEVELS = 1000
STEP = 10

SIGMA_DATA = 0.5
SIGMA_INIT = 2.5
SIGMA_LOW = 0.05
SIGMA_HIGH = 20.0
RHO_POWER = 7.0
ALPHA_MIX = 1.2
RS = 0.7071067811865476
NORM_EPS = 1e-05
CLIP_NORM = 0.001
LEARN_RATE = 0.15
BETA_ONE = 0.9
BETA_TWO = 0.999
ADAM_EPS = 1e-08
WEIGHT_DECAY = 0.01

C = 256
HALF = 128
POS = 256
ROWS = 26 * C
CHUNK = 64
PAD = SIDE
F32 = jnp.float32
BF16 = jnp.bfloat16
VMEM_LIMIT = 58 * 2**20

R_CONV1, R_CONV2, R_EMB, R_QKV, R_PROJ = 0, 9 * C, 18 * C, 22 * C, 25 * C
S_M1, S_I1, S_M2, S_I2, S_M3, S_I3, S_MA, S_MB = range(8)


def sigma_levels(level_ids):
    fraction = level_ids.astype(F32) / (LEVELS - 1)
    top_root = SIGMA_HIGH ** (1.0 / RHO_POWER)
    bottom_root = SIGMA_LOW ** (1.0 / RHO_POWER)
    return (top_root + fraction * (bottom_root - top_root)) ** RHO_POWER


def precondition(sigma_vals):
    total = sigma_vals * sigma_vals + SIGMA_DATA**2
    return (
        lax.rsqrt(total),
        SIGMA_DATA**2 / total,
        sigma_vals * SIGMA_DATA * lax.rsqrt(total),
        total / (sigma_vals * sigma_vals * SIGMA_DATA**2),
    )


def noise_embed(sigma_vals, channel_count):
    frequency = (1.0 / 10000.0) ** (jnp.arange(channel_count, dtype=F32) / channel_count)
    angles = (jnp.log(sigma_vals) / 4.0)[..., None] * frequency
    return jnp.concatenate([jnp.cos(angles), jnp.sin(angles)], axis=-1)


def spread_embed(sigma_vals):
    emb = noise_embed(sigma_vals, C).astype(BF16)
    images = emb.shape[0]
    zero = jnp.zeros_like(emb)
    low = jnp.stack([emb, zero], axis=-1).reshape(images, 4 * C)
    high = jnp.stack([zero, emb], axis=-1).reshape(images, 4 * C)
    fill = jnp.zeros((4 - images, 4 * C), BF16)
    return jnp.concatenate([low, fill, high, fill], axis=0)


def dot_nn(a, b):
    return lax.dot_general(a, b, (((1,), (0,)), ((), ())), preferred_element_type=F32)


def dot_nt(a, b):
    return lax.dot_general(a, b, (((1,), (1,)), ((), ())), preferred_element_type=F32)


def dot_tn(a, b):
    return lax.dot_general(a, b, (((0,), (0,)), ((), ())), preferred_element_type=F32)


def group_mean(row):
    v = jnp.broadcast_to(row, (8, C))
    lane = lax.broadcasted_iota(jnp.int32, (8, C), 1)
    for sh in (1, 2, 4):
        v = v + jnp.where((lane & sh) != 0, pltpu.roll(v, sh, 1), pltpu.roll(v, C - sh, 1))
    return v[0:1] * (1.0 / (POS * 8))


def colsum(v):
    return jnp.sum(v, axis=0, keepdims=True)


def norm_stats(ref, *at):
    x = ref[at]
    mean = group_mean(colsum(x))
    d = x - mean
    inv = lax.rsqrt(group_mean(colsum(d * d)) + NORM_EPS)
    return mean, inv


def put_shifted(bufs, i, r, v):
    rows = v.shape[0]
    col = lax.broadcasted_iota(jnp.int32, (rows, C), 0) & (SIDE - 1)
    at = pl.ds(PAD + r, rows)
    bufs[0, i, at, :] = jnp.where(col == 0, 0.0, pltpu.roll(v, 1, 0)).astype(BF16)
    bufs[1, i, at, :] = v.astype(BF16)
    bufs[2, i, at, :] = jnp.where(col == SIDE - 1, 0.0, pltpu.roll(v, rows - 1, 0)).astype(BF16)


def taps(bufs, flip):
    images = bufs.shape[1]
    out = []
    for dr in (-1, 0, 1):
        for dc in (-1, 0, 1):
            sr, sc = (-dr, -dc) if flip else (dr, dc)
            piece = bufs[sc + 1, :, PAD + SIDE * sr : PAD + SIDE * sr + POS, :]
            out.append(piece.reshape(images * POS, C))
    return out


def conv_forward(bufs, w, l, row):
    return dot_nn(jnp.concatenate(taps(bufs, False), axis=1), w[l, row : row + 9 * C, :])


def conv_input_grad(bufs, w, l, row):
    parts = [w[l, row + t * C : row + (t + 1) * C, :] for t in range(9)]
    return dot_nt(jnp.concatenate(taps(bufs, True), axis=1), jnp.concatenate(parts, axis=1))


def conv_weight_grad(act_t, bufs, grad, l, row):
    left = act_t[...]
    for t, piece in enumerate(taps(bufs, True)):
        grad[l, row + t * C : row + (t + 1) * C, :] = dot_nn(left, piece)


def silu(v):
    h = 0.5 * v
    return h + h * jnp.tanh(h)


def silu_parts(v):
    s = 0.5 + 0.5 * jnp.tanh(0.5 * v)
    return s, s * (1.0 + v * (1.0 - s))


def clear_pads(bufs):
    zero = jnp.zeros(bufs.shape[:2] + (PAD, C), BF16)
    bufs[:, :, 0:PAD, :] = zero
    bufs[:, :, PAD + POS :, :] = zero


def split_qkv(w, l, qkvw, tmp):
    for h in range(2):
        tmp[h] = w[l, R_QKV : R_QKV + 3 * C, h * HALF : (h + 1) * HALF].astype(F32)
    for j in range(3):
        for h in range(2):
            at = j * C + h * HALF
            qkvw[:, at : at + HALF] = tmp[h, pl.ds(j, C, stride=3), :].astype(BF16)


def layer_forward(l, w, small, eo, xs, h1, y, qkv, att, o, st, bufs, nbuf, qkvw, tmp):
    images = h1.shape[1]
    flat = images * POS
    split_qkv(w, l, qkvw, tmp)
    mod = dot_nn(eo[...], w[l, R_EMB : R_EMB + 4 * C, :])
    ma = mod[0:4] + small[l, 5:6, :]
    mb = mod[4:8] + small[l, 6:7, :]
    for i in range(images):
        st[l, i, S_MA : S_MA + 1, :] = ma[i : i + 1]
        st[l, i, S_MB : S_MB + 1, :] = mb[i : i + 1]

    def first(i, _):
        mean, inv = norm_stats(xs, l, i)
        st[l, i, S_M1 : S_M1 + 1, :] = mean
        st[l, i, S_I1 : S_I1 + 1, :] = inv
        a = inv * small[l, 0:1, :]
        b = small[l, 1:2, :]
        for r in range(0, POS, CHUNK):
            put_shifted(bufs, i, r, silu((xs[l, i, r : r + CHUNK, :] - mean) * a + b))
        return 0

    lax.fori_loop(0, images, first, 0)
    h1[l] = (conv_forward(bufs, w, l, R_CONV1) + small[l, 2:3, :]).reshape(images, POS, C)

    def second(i, _):
        mean, inv = norm_stats(h1, l, i)
        st[l, i, S_M2 : S_M2 + 1, :] = mean
        st[l, i, S_I2 : S_I2 + 1, :] = inv
        gain = 1.0 + st[l, i, S_MA : S_MA + 1, :]
        a = inv * small[l, 3:4, :] * gain
        b = small[l, 4:5, :] * gain + st[l, i, S_MB : S_MB + 1, :]
        for r in range(0, POS, CHUNK):
            put_shifted(bufs, i, r, silu((h1[l, i, r : r + CHUNK, :] - mean) * a + b))
        return 0

    lax.fori_loop(0, images, second, 0)
    h2 = conv_forward(bufs, w, l, R_CONV2) + small[l, 7:8, :]
    y[l] = (xs[l] + h2.reshape(images, POS, C)) * RS

    def third(i, _):
        mean, inv = norm_stats(y, l, i)
        st[l, i, S_M3 : S_M3 + 1, :] = mean
        st[l, i, S_I3 : S_I3 + 1, :] = inv
        a = inv * small[l, 8:9, :]
        b = small[l, 9:10, :]
        for r in range(0, POS, CHUNK):
            nbuf[i, r : r + CHUNK, :] = ((y[l, i, r : r + CHUNK, :] - mean) * a + b).astype(BF16)
        return 0

    lax.fori_loop(0, images, third, 0)
    n = nbuf[...].reshape(flat, C)
    for j, row in ((0, 10), (1, None), (2, 11)):
        part = dot_nn(n, qkvw[:, j * C : (j + 1) * C])
        if row is not None:
            part = part + small[l, row : row + 1, :]
        qkv[l, :, :, j * C : (j + 1) * C] = part.astype(BF16).reshape(images, POS, C)

    def attend(i, _):
        s = dot_nt(qkv[l, i, :, 0:C], qkv[l, i, :, C : 2 * C])
        e = jnp.exp((s - jnp.max(s, axis=1, keepdims=True)) * (C**-0.5))
        p = (e * (1.0 / jnp.sum(e, axis=1, keepdims=True))).astype(BF16)
        att[l, i] = p
        o[l, i] = dot_nn(p, qkv[l, i, :, 2 * C :]).astype(BF16)
        return 0

    lax.fori_loop(0, images, attend, 0)
    out = dot_nn(o[l].reshape(flat, C), w[l, R_PROJ:, :]) + small[l, 12:13, :]
    xs[l + 1] = (y[l] + out.reshape(images, POS, C)) * RS


def layer_backward(
    l, w, small, eot, xs, h1, y, qkv, att, o, st, g, bufs, nbuf, qkvw, tmp, dn, dqkv, act_t,
    grad, sgrad,
):
    want = grad is not None
    images = h1.shape[1]
    flat = images * POS
    scale = C**-0.5
    zrow = jnp.zeros((1, C), F32)
    split_qkv(w, l, qkvw, tmp)
    gp = (g[...] * RS).astype(BF16).reshape(flat, C)
    nbuf[...] = dot_nt(gp, w[l, R_PROJ:, :]).astype(BF16).reshape(images, POS, C)
    if want:
        grad[l, R_PROJ:, :] = dot_tn(o[l].reshape(flat, C), gp)
        sgrad[l, 12:13, :] = colsum(gp.astype(F32))

    def attend(i, _):
        p = att[l, i]
        pf = p.astype(F32)
        do = nbuf[i]
        dp = dot_nt(do, qkv[l, i, :, 2 * C :])
        ds = (pf * (dp - jnp.sum(dp * pf, axis=1, keepdims=True))).astype(BF16)
        dqkv[i, :, 0:C] = (dot_nn(ds, qkv[l, i, :, C : 2 * C]) * scale).astype(BF16)
        dqkv[i, :, C : 2 * C] = (dot_tn(ds, qkv[l, i, :, 0:C]) * scale).astype(BF16)
        dqkv[i, :, 2 * C :] = dot_tn(p, do).astype(BF16)
        return 0

    lax.fori_loop(0, images, attend, 0)
    dq = dqkv[...].reshape(flat, 3 * C)
    dn[...] = dot_nt(dq, qkvw[...]).reshape(images, POS, C)

    def third(i, carry):
        db7, dg8, db9 = carry
        mean, inv = st[l, i, S_M3 : S_M3 + 1, :], st[l, i, S_I3 : S_I3 + 1, :]
        gain = small[l, 8:9, :]
        nh = (y[l, i] - mean) * inv
        c1 = colsum(dn[i])
        c2 = colsum(dn[i] * nh)
        mg = group_mean(gain * c1)
        mc = group_mean(gain * c2)
        for r in range(0, POS, CHUNK):
            nhr = (y[l, i, r : r + CHUNK, :] - mean) * inv
            gm = g[i, r : r + CHUNK, :] * RS + inv * (
                gain * dn[i, r : r + CHUNK, :] - mg - nhr * mc
            )
            gm = gm * RS
            g[i, r : r + CHUNK, :] = gm
            put_shifted(bufs, i, r, gm)
            if want:
                nbuf[i, r : r + CHUNK, :] = (nhr * gain + small[l, 9:10, :]).astype(BF16)
                db7 = db7 + colsum(gm.astype(BF16).astype(F32))
        return db7, dg8 + c2, db9 + c1

    db7, dg8, db9 = lax.fori_loop(0, images, third, (zrow, zrow, zrow))
    if want:
        sgrad[l, 7:8, :] = db7
        sgrad[l, 8:9, :] = dg8
        sgrad[l, 9:10, :] = db9
        act_t[...] = nbuf[...].reshape(flat, C).T
        for j in range(3):
            dj = dqkv[:, :, j * C : (j + 1) * C].reshape(flat, C)
            wide = dot_nn(act_t[...], dj)
            for h in range(2):
                tmp[h, pl.ds(j, C, stride=3), :] = wide[:, h * HALF : (h + 1) * HALF]
            if j != 1:
                sgrad[l, 10 + j // 2 : 11 + j // 2, :] = colsum(dj.astype(F32))
        for h in range(2):
            grad[l, R_QKV : R_QKV + 3 * C, h * HALF : (h + 1) * HALF] = tmp[h]
    dn[...] = conv_input_grad(bufs, w, l, R_CONV2).reshape(images, POS, C)

    def second_a(i, _):
        mean, inv = st[l, i, S_M2 : S_M2 + 1, :], st[l, i, S_I2 : S_I2 + 1, :]
        gain = 1.0 + st[l, i, S_MA : S_MA + 1, :]
        a = inv * small[l, 3:4, :] * gain
        b = small[l, 4:5, :] * gain + st[l, i, S_MB : S_MB + 1, :]
        for r in range(0, POS, CHUNK):
            pre = (h1[l, i, r : r + CHUNK, :] - mean) * a + b
            s, slope = silu_parts(pre)
            dn[i, r : r + CHUNK, :] = dn[i, r : r + CHUNK, :] * slope
            if want:
                nbuf[i, r : r + CHUNK, :] = (pre * s).astype(BF16)
        return 0

    lax.fori_loop(0, images, second_a, 0)
    if want:
        act_t[...] = nbuf[...].reshape(flat, C).T
        conv_weight_grad(act_t, bufs, grad, l, R_CONV2)
    row8 = lax.broadcasted_iota(jnp.int32, (8, C), 0)

    def second_b(i, carry):
        db2, dg3, db4, dm = carry
        mean, inv = st[l, i, S_M2 : S_M2 + 1, :], st[l, i, S_I2 : S_I2 + 1, :]
        modgain = 1.0 + st[l, i, S_MA : S_MA + 1, :]
        gain = small[l, 3:4, :]
        nh = (h1[l, i] - mean) * inv
        p1 = colsum(dn[i])
        p2 = colsum(dn[i] * nh)
        full = gain * modgain
        mg = group_mean(full * p1)
        mc = group_mean(full * p2)
        for r in range(0, POS, CHUNK):
            nhr = (h1[l, i, r : r + CHUNK, :] - mean) * inv
            dh = inv * (full * dn[i, r : r + CHUNK, :] - mg - nhr * mc)
            put_shifted(bufs, i, r, dh)
            if want:
                db2 = db2 + colsum(dh.astype(BF16).astype(F32))
        dma = gain * p2 + small[l, 4:5, :] * p1
        dm = jnp.where(row8 == i, dma, jnp.where(row8 == i + 4, p1, dm))
        return db2, dg3 + modgain * p2, db4 + modgain * p1, dm

    db2, dg3, db4, dm = lax.fori_loop(
        0, images, second_b, (zrow, zrow, zrow, jnp.zeros((8, C), F32))
    )
    if want:
        sgrad[l, 2:3, :] = db2
        sgrad[l, 3:4, :] = dg3
        sgrad[l, 4:5, :] = db4
        sgrad[l, 5:6, :] = colsum(dm[0:4])
        sgrad[l, 6:7, :] = colsum(dm[4:8])
        grad[l, R_EMB : R_EMB + 4 * C, :] = lax.dot_general(
            eot[...], dm, (((1,), (0,)), ((), ())),
            precision=lax.Precision.HIGHEST, preferred_element_type=F32,
        )
    dn[...] = conv_input_grad(bufs, w, l, R_CONV1).reshape(images, POS, C)

    def first(i, carry):
        dg0, db1 = carry
        mean, inv = st[l, i, S_M1 : S_M1 + 1, :], st[l, i, S_I1 : S_I1 + 1, :]
        gain = small[l, 0:1, :]
        b = small[l, 1:2, :]
        c1, c2 = zrow, zrow
        for r in range(0, POS, CHUNK):
            nhr = (xs[l, i, r : r + CHUNK, :] - mean) * inv
            pre = nhr * gain + b
            s, slope = silu_parts(pre)
            d = dn[i, r : r + CHUNK, :] * slope
            dn[i, r : r + CHUNK, :] = d
            c1 = c1 + colsum(d)
            c2 = c2 + colsum(d * nhr)
            if want:
                nbuf[i, r : r + CHUNK, :] = (pre * s).astype(BF16)
        mg = group_mean(gain * c1)
        mc = group_mean(gain * c2)
        for r in range(0, POS, CHUNK):
            nhr = (xs[l, i, r : r + CHUNK, :] - mean) * inv
            dx = inv * (gain * dn[i, r : r + CHUNK, :] - mg - nhr * mc)
            g[i, r : r + CHUNK, :] = g[i, r : r + CHUNK, :] + dx
        return dg0 + c2, db1 + c1

    dg0, db1 = lax.fori_loop(0, images, first, (zrow, zrow))
    if want:
        sgrad[l, 0:1, :] = dg0
        sgrad[l, 1:2, :] = db1
        act_t[...] = nbuf[...].reshape(flat, C).T
        conv_weight_grad(act_t, bufs, grad, l, R_CONV1)


def saved_shapes(images):
    return [
        jax.ShapeDtypeStruct((3, images, POS, C), F32),
        jax.ShapeDtypeStruct((2, images, POS, C), F32),
        jax.ShapeDtypeStruct((2, images, POS, C), F32),
        jax.ShapeDtypeStruct((2, images, POS, 3 * C), BF16),
        jax.ShapeDtypeStruct((2, images, POS, POS), BF16),
        jax.ShapeDtypeStruct((2, images, POS, C), BF16),
        jax.ShapeDtypeStruct((2, images, 8, C), F32),
    ]


def forward_kernel(x0, w, small, eo, xs, h1, y, qkv, att, o, st, bufs, nbuf, qkvw, tmp):
    clear_pads(bufs)
    xs[0] = x0[...]

    def body(l, _):
        layer_forward(l, w, small, eo, xs, h1, y, qkv, att, o, st, bufs, nbuf, qkvw, tmp)
        return 0

    lax.fori_loop(0, 2, body, 0)


def backward_kernel(want, *refs):
    cot, w, small, eot, xs, h1, y, qkv, att, o, st, g = refs[:12]
    refs = refs[12:]
    if want:
        grad, sgrad = refs[:2]
        refs = refs[2:]
    else:
        grad, sgrad = None, None
    bufs, nbuf, qkvw, tmp, dn, dqkv, act_t = refs
    clear_pads(bufs)
    g[...] = cot[...]
    if want:
        sgrad[...] = jnp.zeros(sgrad.shape, F32)

    def body(k, _):
        layer_backward(
            1 - k, w, small, eot, xs, h1, y, qkv, att, o, st, g, bufs, nbuf, qkvw, tmp, dn,
            dqkv, act_t, grad, sgrad,
        )
        return 0

    lax.fori_loop(0, 2, body, 0)


def vm(n):
    return [pl.BlockSpec(memory_space=pltpu.VMEM)] * n


def scratch_forward(images):
    return [
        pltpu.VMEM((3, images, POS + 2 * PAD, C), BF16),
        pltpu.VMEM((images, POS, C), BF16),
        pltpu.VMEM((C, 3 * C), BF16),
        pltpu.VMEM((2, 3 * C, HALF), F32),
    ]


def run_forward(x0, w, small, eo):
    images = x0.shape[0]
    return pl.pallas_call(
        forward_kernel,
        out_shape=saved_shapes(images),
        in_specs=vm(4),
        out_specs=vm(7),
        scratch_shapes=scratch_forward(images),
        compiler_params=pltpu.CompilerParams(vmem_limit_bytes=VMEM_LIMIT),
    )(x0, w, small, eo)


def run_backward(cot, w, small, eot, saved, want):
    images = cot.shape[0]
    outs = [jax.ShapeDtypeStruct(cot.shape, F32)]
    if want:
        outs += [
            jax.ShapeDtypeStruct((2, ROWS, C), F32),
            jax.ShapeDtypeStruct((2, 16, C), F32),
        ]
    return pl.pallas_call(
        functools.partial(backward_kernel, want),
        out_shape=outs,
        in_specs=vm(11),
        out_specs=vm(len(outs)),
        scratch_shapes=scratch_forward(images)
        + [
            pltpu.VMEM((images, POS, C), F32),
            pltpu.VMEM((images, POS, 3 * C), BF16),
            pltpu.VMEM((C, images * POS), BF16),
        ],
        compiler_params=pltpu.CompilerParams(vmem_limit_bytes=VMEM_LIMIT),
    )(cot, w, small, eot, *saved)


def adam_step(master, first_mom, second_mom, grad):
    first_new = BETA_ONE * first_mom + (1.0 - BETA_ONE) * grad
    second_new = BETA_TWO * second_mom + (1.0 - BETA_TWO) * grad * grad
    direction = (
        first_new
        / (1.0 - BETA_ONE**STEP)
        / (jnp.sqrt(second_new / (1.0 - BETA_TWO**STEP)) + ADAM_EPS)
    )
    return (master - LEARN_RATE * (direction + WEIGHT_DECAY * master), first_new, second_new)


def gather_net(shard, small):
    rows = lax.all_gather(shard.astype(BF16), "dp", axis=1, tiled=True)
    return (
        lax.all_gather(rows, "section", axis=0, tiled=True),
        lax.all_gather(small, "section", axis=0, tiled=True),
    )


def shards(
    z_noise, eps_noise, levels, counts,
    gen_w, gen_m, gen_v, gen_ema, gen_small, gen_small_m, gen_small_v, gen_small_ema,
    fake_w, fake_m, fake_v, fake_small, fake_small_m, fake_small_v,
    teacher_w, teacher_small,
):
    section_idx = lax.axis_index("section")
    sections = lax.axis_size("section")
    per_group = z_noise.shape[0]
    images = per_group // sections
    start = section_idx * images
    elements = POS * C
    ema_rate = 0.5 ** (20.0 / STEP)

    def mine(a):
        return lax.dynamic_slice_in_dim(a, start, images, 0)

    def wide(a):
        return a[:, None, None]

    z = mine(z_noise)
    eps = mine(eps_noise)
    local_count = counts[0]
    valid = ((start + jnp.arange(images)) < local_count).astype(F32)
    sigma = sigma_levels(mine(levels))
    s_in, s_skip, s_out, s_lam = [wide(t) for t in precondition(sigma)]
    init = jnp.full((images,), SIGMA_INIT, F32)
    g_in, g_skip, g_out, _ = [wide(t) for t in precondition(init)]
    gen_eo, score_eo = spread_embed(init), spread_embed(sigma)
    gen_eot, score_eot = gen_eo.astype(F32).T, score_eo.astype(F32).T

    gw, gs = gather_net(gen_w, gen_small)
    fw, fs = gather_net(fake_w, fake_small)
    tw, ts = gather_net(teacher_w, teacher_small)

    raw = SIGMA_INIT * z
    gen_saved = run_forward(g_in * raw, gw, gs, gen_eo)
    samples = g_skip * raw + g_out * gen_saved[0][2]
    noisy = samples + wide(sigma) * eps
    x0 = s_in * noisy
    fake_saved = run_forward(x0, fw, fs, score_eo)
    fake_den = s_skip * noisy + s_out * fake_saved[0][2]
    factor = wide(valid) * s_lam / elements
    miss = fake_den - samples
    _, fake_g, fake_sg = run_backward(s_out * 2.0 * factor * miss, fw, fs, score_eot, fake_saved, True)
    teacher_saved = run_forward(x0, tw, ts, score_eo)
    teacher_den = s_skip * noisy + s_out * teacher_saved[0][2]
    gap = teacher_den - fake_den
    loss_gen = jnp.sum(factor * ((1.0 - ALPHA_MIX) * gap * gap + gap * miss))
    loss_fake = jnp.sum(factor * miss * miss)
    grad_teacher = factor * (2.0 * (1.0 - ALPHA_MIX) * gap + miss)
    grad_fake = factor * (gap - 2.0 * (1.0 - ALPHA_MIX) * gap - miss)
    direct = s_skip * (grad_teacher + grad_fake) - factor * gap
    (back_t,) = run_backward(s_out * grad_teacher, tw, ts, score_eot, teacher_saved, False)
    (back_f,) = run_backward(s_out * grad_fake, fw, fs, score_eot, fake_saved, False)
    gen_cot = g_out * (direct + s_in * (back_t + back_f))
    _, gen_g, gen_sg = run_backward(gen_cot, gw, gs, gen_eot, gen_saved, True)

    def reduce_net(big, small):
        own = lax.psum_scatter(big, "section", scatter_dimension=0, tiled=True)
        own = lax.psum_scatter(own, "dp", scatter_dimension=1, tiled=True)
        small = lax.psum_scatter(small, "section", scatter_dimension=0, tiled=True)
        return own[0], lax.psum(small, "dp")[0, :13]

    fake_shard, fake_small_sum = reduce_net(fake_g, fake_sg)
    gen_shard, gen_small_sum = reduce_net(gen_g, gen_sg)
    first_dp = (lax.axis_index("dp") == 0).astype(F32)
    square_gen = jnp.sum(gen_shard * gen_shard) + first_dp * jnp.sum(gen_small_sum * gen_small_sum)
    square_fake = jnp.sum(fake_shard * fake_shard) + first_dp * jnp.sum(
        fake_small_sum * fake_small_sum
    )
    on_first = (section_idx == 0).astype(F32)
    sums = jnp.stack(
        [square_gen, square_fake, loss_gen, loss_fake, on_first * local_count.astype(F32)]
    )
    square_gen, square_fake, gen_total, fake_total, count_total = lax.psum(sums, ("section", "dp"))
    norm_gen = jnp.sqrt(square_gen) / count_total
    norm_fake = jnp.sqrt(square_fake) / count_total
    scale_gen = jnp.minimum(1.0, CLIP_NORM / norm_gen) / count_total
    scale_fake = jnp.minimum(1.0, CLIP_NORM / norm_fake) / count_total
    gw_o, gm_o, gv_o = adam_step(gen_w[0], gen_m[0], gen_v[0], gen_shard * scale_gen)
    gs_o, gsm_o, gsv_o = adam_step(
        gen_small[0], gen_small_m[0], gen_small_v[0], gen_small_sum * scale_gen
    )
    fw_o, fm_o, fv_o = adam_step(fake_w[0], fake_m[0], fake_v[0], fake_shard * scale_fake)
    fs_o, fsm_o, fsv_o = adam_step(
        fake_small[0], fake_small_m[0], fake_small_v[0], fake_small_sum * scale_fake
    )
    ge_o = ema_rate * gen_ema[0] + (1.0 - ema_rate) * gw_o
    gse_o = ema_rate * gen_small_ema[0] + (1.0 - ema_rate) * gs_o
    norms = jnp.stack([norm_gen, norm_fake])
    losses = jnp.stack([gen_total, fake_total]) / count_total
    outs = (gw_o, gm_o, gv_o, ge_o, gs_o, gsm_o, gsv_o, gse_o, fw_o, fm_o, fv_o, fs_o, fsm_o, fsv_o)
    return tuple(a[None] for a in outs) + (norms, losses)


def solution(mesh):
    images = P("dp", None, None)
    big = P("section", "dp", None)
    small = P("section", None, None)
    return jax.shard_map(
        shards,
        mesh=mesh,
        in_specs=(images, images, P("dp"), P("dp"))
        + (big,) * 4 + (small,) * 4 + (big,) * 3 + (small,) * 3 + (big, small),
        out_specs=(big,) * 4 + (small,) * 4 + (big,) * 3 + (small,) * 3 + (P(), P()),
        check_vma=False,
    )
```

time: 2330 us -> 916 us (0.39)
  local copies, waits for them, and re-layouts: 551 us -> 14 us
  matrix products: 476 us -> 0 us
  other arithmetic: 494 us -> 26.2 us
  Pallas kernels: 0 us -> 238 us
  waiting for transfers between devices: 556 us -> 482 us
  loops' own time: 52.8 us -> 0 us
  starting transfers between devices: 28.6 us -> 0.47 us
    dot_general x288 -> x0, matrix products: 454 us -> none  [the longest x280 443 us: matrix_product(): return jnp.einsum(pattern, left, right, preferred_element_type=jnp.float32)]
    psum x3 -> x0, waiting for transfers between devices: 335 us -> none  [the longest x1 302 us: shards(): whole_gen, whole_fake = lax.psum((gen_big_g, fake_big_g), 'dp')]
    reduce_scatter x0 -> x6, waiting for transfers between devices: none -> 261 us  [the longest x2 217 us: reduce_net(): own = lax.psum_scatter(own, 'dp', scatter_dimension=1, tiled=True)]
    pallas_call x0 -> x7, Pallas kernels: none -> 238 us  [the longest x4 142 us: run_backward(): pl.pallas_call(functools.partial(backward_kernel, want), out_shape=outs,...]
    reduce_sum x385 -> x1, other arithmetic: 204 us -> 2.73 us  [shards(): loss_fake = jnp.sum(factor * miss * miss)]
    slice x147 -> x0, local copies, waits for them, and re-layouts: 119 us -> none  [the longest x24 30 us: split_big(): big_w[18 * channel_count:22 * channel_count]]
    reduce_sum x240 -> x0, local copies, waits for them, and re-layouts: 101 us -> none  [the longest x48 32.8 us: norm_backward(): mean_grad = jnp.mean(grad_norm, axis=(1, 3), keepdims=True)]
    add x97 -> x2, other arithmetic: 92.5 us -> 1.46 us  [the longest x1 1.42 us: shards(): ge_o = ema_rate * gen_ema[0] + (1.0 - ema_rate) * gw_o]
where the time goes in v1:
time: 916 us; the launch traced here: 912 us
  waiting for transfers between devices  482 us (53%)
  Pallas kernels  238 us (26%)
  blocking collectives  128 us (14%)
  other arithmetic  26.2 us (3%)
  between operations  23 us (3%)
  local copies, waits for them, and re-layouts  14 us (2%)
    reduce_scatter x2, waiting for transfers between devices, reduce_net(): own = lax.psum_scatter(own, 'dp', scatter_dimension=1, tiled=True)  217 us
    all_gather x3, waiting for transfers between devices, gather_net(): rows = lax.all_gather(shard.astype(BF16), 'dp', axis=1, tiled=True)  216 us
    pallas_call x4, Pallas kernels, run_backward(): pl.pallas_call(functools.partial(backward_kernel, want), out_shape=outs,...  142 us
    pallas_call x3, Pallas kernels, run_forward(): pl.pallas_call(forward_kernel, out_shape=saved_shapes(images), in_specs=v...  96 us
    psum x1, blocking collectives, reduce_net(): return (own[0], lax.psum(small, 'dp')[0, :13])  80.9 us
    psum x1, blocking collectives, shards(): lax.psum(sums, ('section', 'dp'))  41.2 us
    reduce_scatter x2, waiting for transfers between devices, reduce_net(): small = lax.psum_scatter(small, 'section', scatter_dimension=0, tiled=True)  22.4 us
    reduce_scatter x2, waiting for transfers between devices, reduce_net(): own = lax.psum_scatter(big, 'section', scatter_dimension=0, tiled=True)  21.9 us
  transfers between devices with their start and end apart: 12, of which 9 were waited for; matrix products, arithmetic and copies ran while one was open for 2% of the time, Pallas kernels for 12%

profile of v1, /device:TPU:0, one launch (start us, length us, event | category | flops | bytes accessed | tf_op | source)
XLA Modules:
  0.0 912.2 jit_solution(2673033710629529783)
XLA Ops:
  11.5 72.8 %all-gather.7.cloned.1.call-done = bf16[1,6656,256]{2,1,0:T(8,128)(2,1)} async-done(((bf16[1,416,256]{2,1,0:T(8,128)(2,1)}), bf16[1,6656,256]{2,1,0:T(8,128)(2,1)}) %all-gather.7.cloned.1.call-update) | async-done | bytes 3407888 | tf_op jit(solution)/shard_map/all_gather | solution.py:503
  84.4 72.1 %all-gather.15.cloned.1.call-done = bf16[1,6656,256]{2,1,0:T(8,128)(2,1)} async-done(((bf16[1,416,256]{2,1,0:T(8,128)(2,1)}), bf16[1,6656,256]{2,1,0:T(8,128)(2,1)}) %all-gather.15.cloned.1.call-update) | async-done | bytes 3407888 | tf_op jit(solution)/shard_map/all_gather | solution.py:503
  156.6 71.5 %all-gather.11.cloned.1.call-done = bf16[1,6656,256]{2,1,0:T(8,128)(2,1)} async-done(((bf16[1,416,256]{2,1,0:T(8,128)(2,1)}), bf16[1,6656,256]{2,1,0:T(8,128)(2,1)}) %all-gather.11.cloned.1.call-update) | async-done | bytes 3407888 | tf_op jit(solution)/shard_map/all_gather | solution.py:503
  236.7 2.0 all_gather.29.small.refs_2_
  238.7 1.9 all_gather.35.small.refs_2_
  240.6 2.5 all_gather.32.small.refs_2_
  245.6 32.4 %shard_map.315 = (f32[3,3,256,256]{3,2,1,0:T(8,128)}, f32[2,3,256,256]{3,2,1,0:T(8,128)}, f32[2,3,256,256]{3,2,1,0:T(8,128)}, bf16[2,3,256,768]{3,2,1,0:T(8,128)...) custom-call(f32[3,256,256]{2,1,0:T(8,128)} %dynamic-slice_multiply_fusion.x0, ...), custom_call_target="tpu_custom_call" | custom-call | tf_op jit(solution)/shard_map/pallas_call | solution.py:458
  278.0 2.4 broadcast_multiply_fusion.1
  280.4 32.2 %shard_map.317 = (f32[3,3,256,256]{3,2,1,0:T(8,128)}, f32[2,3,256,256]{3,2,1,0:T(8,128)}, f32[2,3,256,256]{3,2,1,0:T(8,128)}, bf16[2,3,256,768]{3,2,1,0:T(8,128)...) custom-call(f32[3,256,256]{2,1,0:T(8,128)} %get-tuple-element.154.x0, ...), custom_call_target="tpu_custom_call" | custom-call | tf_op jit(solution)/shard_map/pallas_call | solution.py:458
  312.6 31.4 %shard_map.316 = (f32[3,3,256,256]{3,2,1,0:T(8,128)}, f32[2,3,256,256]{3,2,1,0:T(8,128)}, f32[2,3,256,256]{3,2,1,0:T(8,128)}, bf16[2,3,256,768]{3,2,1,0:T(8,128)...) custom-call(f32[3,256,256]{2,1,0:T(8,128)} %get-tuple-element.154.x0, ...), custom_call_target="tpu_custom_call" | custom-call | tf_op jit(solution)/shard_map/pallas_call | solution.py:458
  344.0 2.7 fusion.3
  348.5 29.0 %shard_map.318 = f32[3,256,256]{2,1,0:T(8,128)} custom-call(f32[3,256,256]{2,1,0:T(8,128)} %get-tuple-element.157.refs_0_, bf16[2,6656,256]{2,1,0:T(8,128)(2,1)} %all-gather.13.cloned.1.call-done.w.refs_1_, f32[2,13,256]{2,1,0:T(8,128)} %all_gather.32.small.refs_2_, f32[1024,8]{1,0:T(8,128)} %bitcast.44, f32[3,3,256,256]{3,2,1,0:T(8,128)} %get-tuple-element.42.refs_4_, ...), custom_call_target="tpu_custom_call" | custom-call | tf_op jit(solution)/shard_map/pallas_call | solution.py:476
  377.5 28.6 %shard_map.319 = f32[3,256,256]{2,1,0:T(8,128)} custom-call(f32[3,256,256]{2,1,0:T(8,128)} %get-tuple-element.156.refs_0_, bf16[2,6656,256]{2,1,0:T(8,128)(2,1)} %all-gather.17.cloned.1.call-done.w.refs_1_, f32[2,13,256]{2,1,0:T(8,128)} %all_gather.35.small.refs_2_, f32[1024,8]{1,0:T(8,128)} %bitcast.45, f32[3,3,256,256]{3,2,1,0:T(8,128)} %get-tuple-element.43.refs_4_, ...), custom_call_target="tpu_custom_call" | custom-call | tf_op jit(solution)/shard_map/pallas_call | solution.py:476
  406.1 2.4 add_multiply_fusion.refs_0_
  408.5 42.3 %shard_map.320 = (f32[3,256,256]{2,1,0:T(8,128)}, f32[2,6656,256]{2,1,0:T(8,128)}, f32[2,16,256]{2,1,0:T(8,128)}) custom-call(f32[3,256,256]{2,1,0:T(8,128)} %add_multiply_fusion.refs_0_, bf16[2,6656,256]{2,1,0:T(8,128)(2,1)} %all-gather.9.cloned.1.call-done.w.refs_1_, f32[2,13,256]{2,1,0:T(8,128)} %all_gather.29.small.refs_2_, f32[1024,8]{1,0:T(8,128)} %bitcast.47, ...), custom_call_target="tpu_custom_call" | custom-call | tf_op jit(solution)/shard_map/pallas_call | solution.py:476
  450.9 42.3 %shard_map.321 = (f32[3,256,256]{2,1,0:T(8,128)}, f32[2,6656,256]{2,1,0:T(8,128)}, f32[2,16,256]{2,1,0:T(8,128)}) custom-call(f32[3,256,256]{2,1,0:T(8,128)} %get-tuple-element.158.refs_0_, bf16[2,6656,256]{2,1,0:T(8,128)(2,1)} %all-gather.17.cloned.1.call-done.w.refs_1_, f32[2,13,256]{2,1,0:T(8,128)} %all_gather.35.small.refs_2_, f32[1024,8]{1,0:T(8,128)} %bitcast.46, ...), custom_call_target="tpu_custom_call" | custom-call | tf_op jit(solution)/shard_map/pallas_call | solution.py:476
  495.3 21.9 %reduce-scatter.13.cloned.1.call-done = f32[1,6656,256]{2,1,0:T(8,128)} async-done(((f32[2,6656,256]{2,1,0:T(8,128)}), f32[1,6656,256]{2,1,0:T(8,128)}) %reduce-scatter.13.cloned.1.call-update) | async-done | bytes 6815760 | tf_op jit(solution)/shard_map/reduce_scatter | solution.py:569
  517.4 11.2 %reduce-scatter.11.cloned.1.call-done = f32[1,16,256]{2,1,0:T(8,128)} async-done(((f32[2,16,256]{2,1,0:T(8,128)}), f32[1,16,256]{2,1,0:T(8,128)}) %reduce-scatter.11.cloned.1.call-update) | async-done | bytes 16400 | tf_op jit(solution)/shard_map/reduce_scatter | solution.py:571
  528.6 11.2 %reduce-scatter.17.cloned.1.call-done = f32[1,16,256]{2,1,0:T(8,128)} async-done(((f32[2,16,256]{2,1,0:T(8,128)}), f32[1,16,256]{2,1,0:T(8,128)}) %reduce-scatter.17.cloned.1.call-update) | async-done | bytes 16400 | tf_op jit(solution)/shard_map/reduce_scatter | solution.py:571
  539.9 80.9 %all-reduce.4 = (f32[1,16,256]{2,1,0:T(8,128)S(1)}, f32[1,16,256]{2,1,0:T(8,128)S(1)}) all-reduce(f32[1,16,256]{2,1,0:T(8,128)} %reduce-scatter.11.cloned.1.call-done, f32[1,16,256]{2,1,0:T(8,128)} %reduce-scatter.17.cloned.1.call-done), channel_id=1, replica_groups=mesh['section'=2,'dp'=16] {'dp'}, use_global_device_ids=true, to_apply=%region_4.0 | all-reduce | flops 8192 | bytes 65536 | tf_op jit(solution)/shard_map/psum | solution.py:572
  623.3 68.9 %reduce-scatter.9.cloned.1.call-done = f32[1,416,256]{2,1,0:T(8,128)} async-done(((f32[1,6656,256]{2,1,0:T(8,128)}), f32[1,416,256]{2,1,0:T(8,128)}) %reduce-scatter.9.cloned.1.call-update) | async-done | bytes 426000 | tf_op jit(solution)/shard_map/reduce_scatter | solution.py:570
  694.6 148.2 %reduce-scatter.15.cloned.1.call-done = f32[1,416,256]{2,1,0:T(8,128)} async-done(((f32[1,6656,256]{2,1,0:T(8,128)}), f32[1,416,256]{2,1,0:T(8,128)}) %reduce-scatter.15.cloned.1.call-update) | async-done | bytes 426000 | tf_op jit(solution)/shard_map/reduce_scatter | solution.py:570
  847.1 41.2 %psum.23 = f32[5]{0:T(128)} all-reduce(f32[5]{0:T(128)} %stack.55), channel_id=1, replica_groups=mesh['section'=2,'dp'=16] {'section','dp'}, use_global_device_ids=true, to_apply=%region_14.0 | all-reduce | flops 5 | bytes 40 | tf_op jit(solution)/shard_map/psum | solution.py:585
  901.4 2.2 multiply_subtract_fusion.1
  (120 shorter events, 34.9 us)
Async XLA Ops:
  7.2 77.2 %all-gather.7.cloned.1.call-start = ((), (), s32[]{:S(2)}) async-start(), calls=%async_computation.6 | async-start | bytes 3620864 | tf_op jit(solution)/shard_map/all_gather | solution.py:503
  9.0 147.5 %all-gather.15.cloned.1.call-start = ((), (), s32[]{:S(2)}) async-start(), calls=%async_computation.10 | async-start | bytes 3620864 | tf_op jit(solution)/shard_map/all_gather | solution.py:503
  10.8 217.3 %all-gather.11.cloned.1.call-start = ((), (), s32[]{:S(2)}) async-start(), calls=%async_computation.8 | async-start | bytes 3620864 | tf_op jit(solution)/shard_map/all_gather | solution.py:503
  11.5 234.1 %all-gather.9.cloned.1.call-start = ((), (), s32[]{:S(2)}) async-start(), calls=%async_computation.7 | async-start | bytes 10223616 | tf_op jit(solution)/shard_map/all_gather | solution.py:505
  84.4 196.0 %all-gather.17.cloned.1.call-start = ((), (), s32[]{:S(2)}) async-start(), calls=%async_computation.11 | async-start | bytes 10223616 | tf_op jit(solution)/shard_map/all_gather | solution.py:505
  156.5 156.1 %all-gather.13.cloned.1.call-start = ((), (), s32[]{:S(2)}) async-start(), calls=%async_computation.9 | async-start | bytes 10223616 | tf_op jit(solution)/shard_map/all_gather | solution.py:505
  228.1 266.5 %reduce-scatter.7.cloned.1.call-start = ((), (), s32[]{:S(2)}) async-start(), calls=%async_computation.12 | async-start | bytes 20447232 | tf_op jit(solution)/shard_map/reduce_scatter | solution.py:569
  450.8 66.4 %reduce-scatter.13.cloned.1.call-start = ((), (), s32[]{:S(2)}) async-start(), calls=%async_computation.15 | async-start | bytes 20447232 | tf_op jit(solution)/shard_map/reduce_scatter | solution.py:569
  493.2 35.4 %reduce-scatter.11.cloned.1.call-start = ((), (), s32[]{:S(2)}) async-start(), calls=%async_computation.14 | async-start | bytes 49152 | tf_op jit(solution)/shard_map/reduce_scatter | solution.py:571
  494.0 45.9 %reduce-scatter.17.cloned.1.call-start = ((), (), s32[]{:S(2)}) async-start(), calls=%async_computation.17 | async-start | bytes 49152 | tf_op jit(solution)/shard_map/reduce_scatter | solution.py:571
  494.5 197.6 %reduce-scatter.9.cloned.1.call-start = ((), (), s32[]{:S(2)}) async-start(), calls=%async_computation.13 | async-start | bytes 7241728 | tf_op jit(solution)/shard_map/reduce_scatter | solution.py:570
  495.3 347.5 %reduce-scatter.15.cloned.1.call-start = ((), (), s32[]{:S(2)}) async-start(), calls=%async_computation.16 | async-start | bytes 7241728 | tf_op jit(solution)/shard_map/reduce_scatter | solution.py:570
  517.2 378.5 %copy-start.15 = (f32[1,13,256]{2,0,1:T(1,128)S(1)}, f32[1,13,256]{2,0,1:T(1,128)}, u32[]{:S(2)}) copy-start(f32[1,13,256]{2,0,1:T(1,128)} %param.29) | copy-start | bytes 39940
  517.3 378.5 %copy-start.16 = (f32[1,13,256]{2,0,1:T(1,128)S(1)}, f32[1,13,256]{2,0,1:T(1,128)}, u32[]{:S(2)}) copy-start(f32[1,13,256]{2,0,1:T(1,128)} %param.30) | copy-start | bytes 39940
  517.3 381.7 %copy-start.13 = (f32[1,13,256]{2,0,1:T(1,128)S(1)}, f32[1,13,256]{2,0,1:T(1,128)}, u32[]{:S(2)}) copy-start(f32[1,13,256]{2,0,1:T(1,128)} %param.35) | copy-start | bytes 39940
  517.3 381.7 %copy-start.17 = (f32[1,13,256]{2,0,1:T(1,128)S(1)}, f32[1,13,256]{2,0,1:T(1,128)}, u32[]{:S(2)}) copy-start(f32[1,13,256]{2,0,1:T(1,128)} %param.36) | copy-start | bytes 39940
  517.3 381.7 %copy-start.18 = (f32[1,13,256]{2,0,1:T(1,128)S(1)}, f32[1,13,256]{2,0,1:T(1,128)}, u32[]{:S(2)}) copy-start(f32[1,13,256]{2,0,1:T(1,128)} %param.37) | copy-start | bytes 39940
  517.3 384.1 %copy-start.2 = (f32[1,416,256]{2,1,0:T(8,128)S(1)}, f32[1,416,256]{2,1,0:T(8,128)}, u32[]{:S(2)}) copy-start(f32[1,416,256]{2,1,0:T(8,128)} %param.32) | copy-start | bytes 1277956
  517.3 384.1 %copy-start.5 = (f32[1,416,256]{2,1,0:T(8,128)S(1)}, f32[1,416,256]{2,1,0:T(8,128)}, u32[]{:S(2)}) copy-start(f32[1,416,256]{2,1,0:T(8,128)} %param.33) | copy-start | bytes 1277956
  517.3 384.1 %copy-start.6 = (f32[1,416,256]{2,1,0:T(8,128)S(1)}, f32[1,416,256]{2,1,0:T(8,128)}, u32[]{:S(2)}) copy-start(f32[1,416,256]{2,1,0:T(8,128)} %param.34) | copy-start | bytes 1277956
  517.3 386.3 %copy-start.3 = (f32[1,416,256]{2,1,0:T(8,128)S(1)}, f32[1,416,256]{2,1,0:T(8,128)}, u32[]{:S(2)}) copy-start(f32[1,416,256]{2,1,0:T(8,128)} %param.24) | copy-start | bytes 1277956
  517.4 386.3 %copy-start.7 = (f32[1,416,256]{2,1,0:T(8,128)S(1)}, f32[1,416,256]{2,1,0:T(8,128)}, u32[]{:S(2)}) copy-start(f32[1,416,256]{2,1,0:T(8,128)} %param.27) | copy-start | bytes 1277956
  517.4 386.3 %copy-start.8 = (f32[1,416,256]{2,1,0:T(8,128)S(1)}, f32[1,416,256]{2,1,0:T(8,128)}, u32[]{:S(2)}) copy-start(f32[1,416,256]{2,1,0:T(8,128)} %param.25) | copy-start | bytes 1277956
  517.4 386.3 %copy-start.9 = (f32[1,416,256]{2,1,0:T(8,128)S(1)}, f32[1,416,256]{2,1,0:T(8,128)}, u32[]{:S(2)}) copy-start(f32[1,416,256]{2,1,0:T(8,128)} %param.26) | copy-start | bytes 1277956
  (12 other events, 1266.2 us)
Sparse Core Ops, SparseCore 0:
  11.3 73.0 all-gather.6
  87.6 68.8 all-gather.14
  159.2 68.8 all-gather.10
  229.4 16.0 all-gather.8
  246.9 18.6 all-gather.16
  267.1 18.7 all-gather.12
  450.9 23.8 reduce-scatter.6
  493.3 23.8 reduce-scatter.12
  520.0 8.5 reduce-scatter.10
  531.2 8.5 reduce-scatter.16
  542.2 149.9 reduce-scatter.8
  694.3 148.4 reduce-scatter.14

commit v2 on v1

--- a/solution.py
+++ b/solution.py
@@ -138,7 +138,7 @@
 def conv_weight_grad(act_t, bufs, grad, l, row):
     left = act_t[...]
     for t, piece in enumerate(taps(bufs, True)):
-        grad[l, row + t * C : row + (t + 1) * C, :] = dot_nn(left, piece)
+        grad[l, row + t * C : row + (t + 1) * C, :] = dot_nn(left, piece).astype(BF16)
 
 
 def silu(v):
@@ -249,7 +249,7 @@
     gp = (g[...] * RS).astype(BF16).reshape(flat, C)
     nbuf[...] = dot_nt(gp, w[l, R_PROJ:, :]).astype(BF16).reshape(images, POS, C)
     if want:
-        grad[l, R_PROJ:, :] = dot_tn(o[l].reshape(flat, C), gp)
+        grad[l, R_PROJ:, :] = dot_tn(o[l].reshape(flat, C), gp).astype(BF16)
         sgrad[l, 12:13, :] = colsum(gp.astype(F32))
 
     def attend(i, _):
@@ -303,7 +303,7 @@
             if j != 1:
                 sgrad[l, 10 + j // 2 : 11 + j // 2, :] = colsum(dj.astype(F32))
         for h in range(2):
-            grad[l, R_QKV : R_QKV + 3 * C, h * HALF : (h + 1) * HALF] = tmp[h]
+            grad[l, R_QKV : R_QKV + 3 * C, h * HALF : (h + 1) * HALF] = tmp[h].astype(BF16)
     dn[...] = conv_input_grad(bufs, w, l, R_CONV2).reshape(images, POS, C)
 
     def second_a(i, _):
@@ -358,7 +358,7 @@
         grad[l, R_EMB : R_EMB + 4 * C, :] = lax.dot_general(
             eot[...], dm, (((1,), (0,)), ((), ())),
             precision=lax.Precision.HIGHEST, preferred_element_type=F32,
-        )
+        ).astype(BF16)
     dn[...] = conv_input_grad(bufs, w, l, R_CONV1).reshape(images, POS, C)
 
     def first(i, carry):
@@ -470,7 +470,7 @@
     outs = [jax.ShapeDtypeStruct(cot.shape, F32)]
     if want:
         outs += [
-            jax.ShapeDtypeStruct((2, ROWS, C), F32),
+            jax.ShapeDtypeStruct((2, ROWS, C), BF16),
             jax.ShapeDtypeStruct((2, 16, C), F32),
         ]
     return pl.pallas_call(
@@ -488,6 +488,357 @@
     )(cot, w, small, eot, *saved)
 
 
+PLANES, PLANE = 4, 4
+MESH = pl.DeviceIdType.MESH
+
+
+class Place:
+    def __init__(self):
+        self.sec = lax.axis_index("section")
+        self.d = lax.axis_index("dp")
+        self.x = lax.rem(self.d, 2)
+        self.y = lax.rem(self.d // 2, 2)
+        self.z = self.d // PLANE
+        self.sib = {"section": 1 - self.sec}
+        self.xn = {"dp": self.d + 1 - 2 * self.x}
+        self.yn = {"dp": self.d + 2 - 4 * self.y}
+
+    def plane(self, j):
+        return lax.rem(self.z + j + PLANES, PLANES)
+
+    def zpeer(self, j):
+        return {"dp": self.plane(j) * PLANE + lax.rem(self.d, PLANE)}
+
+    def meet(self):
+        barrier = pltpu.get_barrier_semaphore()
+        others = [self.sib, self.xn, self.yn] + [self.zpeer(j) for j in (1, 2, 3)]
+        for other in others:
+            pl.semaphore_signal(barrier, inc=1, device_id=other, device_id_type=MESH)
+        pl.semaphore_wait(barrier, len(others))
+
+
+def remote(src, dst, send, recv, target):
+    return pltpu.make_async_remote_copy(
+        src_ref=src, dst_ref=dst, send_sem=send, recv_sem=recv,
+        device_id=target, device_id_type=MESH,
+    )
+
+
+Z1, X1, Y1, X2, Y2, S_OWN, S_X, S_Y, S_DA, S_DB = 0, 3, 7, 11, 15, 19, 23, 27, 31, 35
+SLOTS = 39
+
+
+def gather_kernel(*refs):
+    nets = (len(refs) - 4) // 2
+    ws, outs = refs[:nets], refs[nets : 2 * nets]
+    stage, local_sem, send_sem, recv_sem = refs[2 * nets :]
+    part = stage.shape[1]
+    half = part // 2
+    me = Place()
+    for n in range(nets):
+        stage[n] = ws[n][...].astype(BF16)
+    me.meet()
+
+    def rows(plane, y, x, lo, count):
+        at = me.sec * ROWS + (plane * PLANE + y * 2 + x) * part + lo
+        return pl.ds(pl.multiple_of(at, 16), count)
+
+    sends = []
+
+    def send(n, slot, where, target, src=None):
+        piece = outs[n].at[where]
+        copy = remote(
+            piece if src is None else src, piece, send_sem.at[n, slot], recv_sem.at[n, slot], target
+        )
+        copy.start()
+        sends.append(copy)
+
+    def arrived(n, slot, where):
+        piece = outs[n].at[where]
+        remote(piece, piece, send_sem.at[n, slot], recv_sem.at[n, slot], me.sib).wait_recv()
+
+    def own(j):
+        return rows(me.plane(-j), me.y, me.x, 0, part)
+
+    def begin(n):
+        for j in (1, 2, 3):
+            send(n, Z1 + j - 1, own(0), me.zpeer(j), stage.at[n])
+        for slot, target in ((X1, me.xn), (Y1, me.yn), (S_OWN, me.sib)):
+            send(n, slot, own(0), target, stage.at[n])
+        copy = pltpu.make_async_copy(stage.at[n], outs[n].at[own(0)], local_sem.at[n])
+        copy.start()
+        return copy
+
+    def phase1(n):
+        for j in (1, 2, 3):
+            arrived(n, Z1 + j - 1, own(j))
+            for slot, target in ((X1, me.xn), (Y1, me.yn), (S_OWN, me.sib)):
+                send(n, slot + j, own(j), target)
+
+    def phase2(n):
+        for j in range(PLANES):
+            plane = me.plane(-j)
+            arrived(n, X1 + j, rows(plane, me.y, 1 - me.x, 0, part))
+            send(n, Y2 + j, rows(plane, me.y, 1 - me.x, 0, half), me.yn)
+            send(n, S_X + j, rows(plane, me.y, 1 - me.x, 0, part), me.sib)
+            arrived(n, Y1 + j, rows(plane, 1 - me.y, me.x, 0, part))
+            send(n, X2 + j, rows(plane, 1 - me.y, me.x, half, half), me.xn)
+            send(n, S_Y + j, rows(plane, 1 - me.y, me.x, 0, part), me.sib)
+
+    def phase3(n):
+        for j in range(PLANES):
+            plane = me.plane(-j)
+            for slot, to, lo in ((Y2, S_DA, 0), (X2, S_DB, half)):
+                where = rows(plane, 1 - me.y, 1 - me.x, lo, half)
+                arrived(n, slot + j, where)
+                send(n, to + j, where, me.sib)
+
+    def finish(n):
+        for slot in range(S_OWN, SLOTS):
+            arrived(n, slot, pl.ds(0, part if slot < S_DA else half))
+
+    locals_ = [begin(n) for n in range(nets)]
+    phase1(0)
+    phase2(0)
+    for n in range(1, nets):
+        phase1(n)
+        phase3(n - 1)
+        phase2(n)
+    phase3(nets - 1)
+    for n in range(nets):
+        finish(n)
+    for copy in locals_:
+        copy.wait()
+    for copy in sends:
+        copy.wait_send()
+
+
+def gather_nets(*ws):
+    part = ws[0].shape[0]
+    nets = len(ws)
+    outs = pl.pallas_call(
+        gather_kernel,
+        out_shape=[jax.ShapeDtypeStruct((2 * ROWS, C), BF16)] * nets,
+        in_specs=vm(nets),
+        out_specs=[pl.BlockSpec(memory_space=pl.ANY)] * nets,
+        scratch_shapes=[
+            pltpu.VMEM((nets, part, C), BF16),
+            pltpu.SemaphoreType.DMA((nets,)),
+            pltpu.SemaphoreType.DMA((nets, SLOTS)),
+            pltpu.SemaphoreType.DMA((nets, SLOTS)),
+        ],
+        compiler_params=pltpu.CompilerParams(
+            collective_id=0, has_side_effects=True, vmem_limit_bytes=VMEM_LIMIT
+        ),
+    )(*ws)
+    return [a.reshape(2, ROWS, C) for a in outs]
+
+
+A_SLOT, B_SLOT, C_SLOT, D_SLOT = 0, 4, 20, 28
+R_SLOTS = 31
+
+
+def reduce_kernel(*refs):
+    nets = 2
+    gb, sg = refs[:nets], refs[nets]
+    shard, stot, sqtot = refs[nets + 1 : nets + 4]
+    own, sib, rb, rc, rd, sbuf, srecv, qbuf, qrecv, lsem, ssem, rsem, tsem, urem = refs[nets + 4 :]
+    part = shard.shape[1]
+    half = part // 2
+    span = PLANE * part
+    me = Place()
+    me.meet()
+    sends = []
+
+    def send(src, dst, s, r, target):
+        copy = remote(src, dst, s, r, target)
+        copy.start()
+        sends.append(copy)
+
+    def arrived(dst, s, r):
+        remote(dst, dst, s, r, me.sib).wait_recv()
+
+    def zt(k):
+        return me.plane(1 + k)
+
+    def block(base, k):
+        return pl.ds(pl.multiple_of(base + zt(k) * span, 16), span)
+
+    def piece(k, y, x, lo, count):
+        at = (zt(k) * PLANE + y * 2 + x) * part + lo
+        return pl.ds(pl.multiple_of(at, 16), count)
+
+    loads = {}
+    for n in range(nets):
+        for k in range(PLANES):
+            there, here = block((1 - me.sec) * ROWS, k), block(me.sec * ROWS, k)
+            slot = A_SLOT + k
+            send(
+                gb[n].at[there], sib.at[n, block(0, k)], ssem.at[n, slot], rsem.at[n, slot], me.sib
+            )
+            copy = pltpu.make_async_copy(gb[n].at[here], own.at[n, block(0, k)], lsem.at[n, k])
+            copy.start()
+            loads[n, k] = copy
+
+    def totals(buf, recv, sem_s, sem_r, base, first):
+        steps = ((0, me.sib), (1, me.xn), (2, me.yn))
+        for slot, target in steps:
+            if slot == 0 and first is not None:
+                src = first
+            else:
+                src = buf.at[slot]
+            send(src, recv.at[slot], sem_s.at[base + slot], sem_r.at[base + slot], target)
+            arrived(recv.at[slot], sem_s.at[base + slot], sem_r.at[base + slot])
+            buf[slot + 1] = buf[slot] + recv[slot]
+        recv[3 + me.z] = buf[3]
+        for j in (1, 2, 3):
+            at = base + 2 + j
+            send(buf.at[3], recv.at[3 + me.z], sem_s.at[at], sem_r.at[at], me.zpeer(j))
+        for j in (1, 2, 3):
+            at = base + 2 + j
+            arrived(recv.at[3 + me.plane(-j)], sem_s.at[at], sem_r.at[at])
+        return (recv[3] + recv[4]) + (recv[5] + recv[6])
+
+    def add_rows(dst, src, n_rows, step):
+        def body(i, _):
+            r = pl.multiple_of(i * step, 16)
+            a, at = dst(r, step)
+            b, bt = src(r, step)
+            a[at] = (a[at].astype(F32) + b[bt].astype(F32)).astype(BF16)
+            return 0
+
+        lax.fori_loop(0, n_rows // step, body, 0)
+
+    def stage_a(n, k):
+        slot = A_SLOT + k
+        loads[n, k].wait()
+        arrived(sib.at[n, block(0, k)], ssem.at[n, slot], rsem.at[n, slot])
+        base = zt(k) * span
+        step = part
+
+        def at(ref):
+            return lambda r, c: (ref, (n, pl.ds(pl.multiple_of(base + r, 16), c), slice(None)))
+
+        add_rows(at(own), at(sib), span, step)
+        for j in range(2):
+            slot = B_SLOT + 4 * k + j
+            send(
+                own.at[n, piece(k, 1 - me.y, j, 0, half)], rb.at[n, k, j],
+                ssem.at[n, slot], rsem.at[n, slot], me.yn,
+            )
+            slot = B_SLOT + 4 * k + 2 + j
+            send(
+                own.at[n, piece(k, j, 1 - me.x, half, half)], rb.at[n, k, 2 + j],
+                ssem.at[n, slot], rsem.at[n, slot], me.xn,
+            )
+
+    def join(n, where, recv_ref, at):
+        own[(n, where, slice(None))] = (
+            own[(n, where, slice(None))].astype(F32) + recv_ref[at].astype(F32)
+        ).astype(BF16)
+
+    def stage_c(n, k):
+        for j in range(4):
+            slot = B_SLOT + 4 * k + j
+            arrived(rb.at[n, k, j], ssem.at[n, slot], rsem.at[n, slot])
+            where = piece(k, me.y, j, 0, half) if j < 2 else piece(k, j - 2, me.x, half, half)
+            join(n, where, rb, (n, k, j))
+        slot = C_SLOT + 2 * k
+        send(
+            own.at[n, piece(k, me.y, 1 - me.x, 0, half)], rc.at[n, k, 0],
+            ssem.at[n, slot], rsem.at[n, slot], me.xn,
+        )
+        slot += 1
+        send(
+            own.at[n, piece(k, 1 - me.y, me.x, half, half)], rc.at[n, k, 1],
+            ssem.at[n, slot], rsem.at[n, slot], me.yn,
+        )
+
+    def stage_d(n, k):
+        for j in range(2):
+            slot = C_SLOT + 2 * k + j
+            arrived(rc.at[n, k, j], ssem.at[n, slot], rsem.at[n, slot])
+            where = piece(k, me.y, me.x, j * half, half)
+            if k < PLANES - 1:
+                join(n, where, rc, (n, k, j))
+            else:
+                shard[n, j * half : (j + 1) * half, :] = (
+                    own[(n, where, slice(None))].astype(F32) + rc[n, k, j].astype(F32)
+                )
+        if k < PLANES - 1:
+            slot = D_SLOT + k
+            send(
+                own.at[n, piece(k, me.y, me.x, 0, part)], rd.at[n, k],
+                ssem.at[n, slot], rsem.at[n, slot], me.zpeer(1 + k),
+            )
+
+    def stage_e(n):
+        for k in range(PLANES - 1):
+            slot = D_SLOT + k
+            arrived(rd.at[n, k], ssem.at[n, slot], rsem.at[n, slot])
+        shard[n] = (
+            shard[n] + rd[n, 0].astype(F32) + (rd[n, 1].astype(F32) + rd[n, 2].astype(F32))
+        )
+
+    order = [(n, k) for n in range(nets) for k in range(PLANES)]
+    lag_c, lag_d = 1, 2
+    for t in range(len(order) + lag_d):
+        if t < len(order):
+            stage_a(*order[t])
+        if 0 <= t - lag_c < len(order):
+            stage_c(*order[t - lag_c])
+        if 0 <= t - lag_d < len(order):
+            stage_d(*order[t - lag_d])
+    sbuf[0] = sg[me.sec]
+    stot[...] = totals(sbuf, srecv, tsem, urem, 0, sg.at[1 - me.sec])
+    for n in range(nets):
+        stage_e(n)
+    lane = lax.broadcasted_iota(jnp.int32, (8, HALF), 1)
+    tile = jnp.zeros((8, HALF), F32)
+    for n in range(nets):
+        big = jnp.sum(shard[n] * shard[n])
+        low = jnp.sum(stot[16 * n : 16 * n + 13, :] * stot[16 * n : 16 * n + 13, :])
+        tile = jnp.where(lane == n, big + jnp.where(me.d == 0, low, 0.0), tile)
+    qbuf[0] = tile
+    sqtot[...] = totals(qbuf, qrecv, tsem, urem, 6, None)
+    for copy in sends:
+        copy.wait_send()
+
+
+def reduce_nets(bigs, small, part):
+    nets = len(bigs)
+    half = part // 2
+    return pl.pallas_call(
+        reduce_kernel,
+        out_shape=[
+            jax.ShapeDtypeStruct((nets, part, C), F32),
+            jax.ShapeDtypeStruct(small.shape[1:], F32),
+            jax.ShapeDtypeStruct((8, HALF), F32),
+        ],
+        in_specs=[pl.BlockSpec(memory_space=pl.ANY)] * nets + vm(1),
+        out_specs=vm(3),
+        scratch_shapes=[
+            pltpu.VMEM((nets, ROWS, C), BF16),
+            pltpu.VMEM((nets, ROWS, C), BF16),
+            pltpu.VMEM((nets, PLANES, 4, half, C), BF16),
+            pltpu.VMEM((nets, PLANES, 2, half, C), BF16),
+            pltpu.VMEM((nets, PLANES - 1, part, C), BF16),
+            pltpu.VMEM((4,) + small.shape[1:], F32),
+            pltpu.VMEM((7,) + small.shape[1:], F32),
+            pltpu.VMEM((4, 8, HALF), F32),
+            pltpu.VMEM((7, 8, HALF), F32),
+            pltpu.SemaphoreType.DMA((nets, PLANES)),
+            pltpu.SemaphoreType.DMA((nets, R_SLOTS)),
+            pltpu.SemaphoreType.DMA((nets, R_SLOTS)),
+            pltpu.SemaphoreType.DMA((12,)),
+            pltpu.SemaphoreType.DMA((12,)),
+        ],
+        compiler_params=pltpu.CompilerParams(
+            collective_id=1, has_side_effects=True, vmem_limit_bytes=VMEM_LIMIT
+        ),
+    )(*[b.reshape(2 * ROWS, C) for b in bigs], small)
+
+
 def adam_step(master, first_mom, second_mom, grad):
     first_new = BETA_ONE * first_mom + (1.0 - BETA_ONE) * grad
     second_new = BETA_TWO * second_mom + (1.0 - BETA_TWO) * grad * grad
@@ -499,12 +850,69 @@
     return (master - LEARN_RATE * (direction + WEIGHT_DECAY * master), first_new, second_new)
 
 
-def gather_net(shard, small):
+EMA_RATE = 0.5 ** (20.0 / STEP)
+
+
+def update_kernel(shard, stot, sqtot, *refs):
+    ins, outs = refs[:14], refs[14:]
+    nums = outs[14]
+    count = stot[15:16, 0:1]
+    sq = sqtot[0:1, :]
+    lane = lax.broadcasted_iota(jnp.int32, sq.shape, 1)
+    total = jnp.zeros_like(sq)
+    scales = []
+    for n in range(2):
+        norm = jnp.sqrt(jnp.sum(jnp.where(lane == n, sq, 0.0), axis=1, keepdims=True)) / count
+        scales.append(jnp.minimum(1.0, CLIP_NORM / norm) / count)
+        total = jnp.where(lane == n, norm, total)
+        total = jnp.where(lane == 2 + n, stot[13 + n : 14 + n, 0:1] / count, total)
+    nums[...] = jnp.broadcast_to(total, nums.shape)
+
+    def one(scale, grad, w, m, v, ema, ow, om, ov, oe):
+        new, first, second = adam_step(w[0], m[0], v[0], grad * scale)
+        ow[0] = new
+        om[0] = first
+        ov[0] = second
+        if ema is not None:
+            oe[0] = EMA_RATE * ema[0] + (1.0 - EMA_RATE) * new
+
+    one(scales[0], shard[0], *ins[0:4], *outs[0:4])
+    one(scales[0], stot[0:13], *ins[4:8], *outs[4:8])
+    one(scales[1], shard[1], *ins[8:11], None, *outs[8:11], None)
+    one(scales[1], stot[16:29], *ins[11:14], None, *outs[11:14], None)
+
+
+def update_nets(shard, stot, sqtot, states):
+    res = pl.pallas_call(
+        update_kernel,
+        out_shape=[jax.ShapeDtypeStruct(a.shape, F32) for a in states]
+        + [jax.ShapeDtypeStruct((8, HALF), F32)],
+        in_specs=vm(3 + len(states)),
+        out_specs=vm(len(states) + 1),
+        compiler_params=pltpu.CompilerParams(vmem_limit_bytes=VMEM_LIMIT),
+    )(shard, stot, sqtot, *states)
+    nums = res[-1]
+    return tuple(res[:-1]) + (nums[0, 0:2], nums[0, 2:4])
+
+
+def gather_plain(shard):
     rows = lax.all_gather(shard.astype(BF16), "dp", axis=1, tiled=True)
-    return (
-        lax.all_gather(rows, "section", axis=0, tiled=True),
-        lax.all_gather(small, "section", axis=0, tiled=True),
-    )
+    return lax.all_gather(rows, "section", axis=0, tiled=True)
+
+
+def reduce_plain(bigs, small):
+    shards_, squares = [], []
+    own = lax.psum_scatter(small, "section", scatter_dimension=0, tiled=True)
+    stot = lax.psum(own, "dp")[0]
+    first = lax.axis_index("dp") == 0
+    for n, big in enumerate(bigs):
+        own = lax.psum_scatter(big, "section", scatter_dimension=0, tiled=True)
+        own = lax.psum_scatter(own, "dp", scatter_dimension=1, tiled=True)[0].astype(F32)
+        shards_.append(own)
+        low = jnp.sum(jnp.square(stot[16 * n : 16 * n + 13]))
+        squares.append(jnp.sum(own * own) + jnp.where(first, low, 0.0))
+    sq = lax.psum(jnp.stack(squares), ("section", "dp"))
+    return jnp.stack(shards_), stot, jnp.zeros((8, HALF), F32).at[:, 0:2].set(sq)
 
 
 def shards(
@@ -515,11 +923,11 @@
 ):
     section_idx = lax.axis_index("section")
     sections = lax.axis_size("section")
+    custom = lax.axis_size("dp") == PLANES * PLANE
     per_group = z_noise.shape[0]
     images = per_group // sections
     start = section_idx * images
     elements = POS * C
-    ema_rate = 0.5 ** (20.0 / STEP)
 
     def mine(a):
         return lax.dynamic_slice_in_dim(a, start, images, 0)
@@ -538,9 +946,14 @@
     gen_eo, score_eo = spread_embed(init), spread_embed(sigma)
     gen_eot, score_eot = gen_eo.astype(F32).T, score_eo.astype(F32).T
 
-    gw, gs = gather_net(gen_w, gen_small)
-    fw, fs = gather_net(fake_w, fake_small)
-    tw, ts = gather_net(teacher_w, teacher_small)
+    smalls = lax.all_gather(
+        jnp.concatenate([gen_small, fake_small, teacher_small]), "section", axis=0
+    )
+    gs, fs, ts = smalls[:, 0], smalls[:, 1], smalls[:, 2]
+    if custom:
+        gw, fw, tw = gather_nets(gen_w[0], fake_w[0], teacher_w[0])
+    else:
+        gw, fw, tw = gather_plain(gen_w), gather_plain(fake_w), gather_plain(teacher_w)
 
     raw = SIGMA_INIT * z
     gen_saved = run_forward(g_in * raw, gw, gs, gen_eo)
@@ -565,42 +978,21 @@
     gen_cot = g_out * (direct + s_in * (back_t + back_f))
     _, gen_g, gen_sg = run_backward(gen_cot, gw, gs, gen_eot, gen_saved, True)
 
-    def reduce_net(big, small):
-        own = lax.psum_scatter(big, "section", scatter_dimension=0, tiled=True)
-        own = lax.psum_scatter(own, "dp", scatter_dimension=1, tiled=True)
-        small = lax.psum_scatter(small, "section", scatter_dimension=0, tiled=True)
-        return own[0], lax.psum(small, "dp")[0, :13]
-
-    fake_shard, fake_small_sum = reduce_net(fake_g, fake_sg)
-    gen_shard, gen_small_sum = reduce_net(gen_g, gen_sg)
-    first_dp = (lax.axis_index("dp") == 0).astype(F32)
-    square_gen = jnp.sum(gen_shard * gen_shard) + first_dp * jnp.sum(gen_small_sum * gen_small_sum)
-    square_fake = jnp.sum(fake_shard * fake_shard) + first_dp * jnp.sum(
-        fake_small_sum * fake_small_sum
+    scalars = jnp.broadcast_to(jnp.stack([loss_gen, loss_fake, jnp.sum(valid)])[:, None], (3, C))
+    small_sums = jnp.concatenate(
+        [gen_sg[:, :13], jnp.broadcast_to(scalars, (2, 3, C)), fake_sg], axis=1
     )
-    on_first = (section_idx == 0).astype(F32)
-    sums = jnp.stack(
-        [square_gen, square_fake, loss_gen, loss_fake, on_first * local_count.astype(F32)]
+    if custom:
+        reduced = reduce_nets((gen_g, fake_g), small_sums, gen_w.shape[1])
+    else:
+        reduced = reduce_plain((gen_g, fake_g), small_sums)
+    return update_nets(
+        *reduced,
+        (
+            gen_w, gen_m, gen_v, gen_ema, gen_small, gen_small_m, gen_small_v, gen_small_ema,
+            fake_w, fake_m, fake_v, fake_small, fake_small_m, fake_small_v,
+        ),
     )
-    square_gen, square_fake, gen_total, fake_total, count_total = lax.psum(sums, ("section", "dp"))
-    norm_gen = jnp.sqrt(square_gen) / count_total
-    norm_fake = jnp.sqrt(square_fake) / count_total
-    scale_gen = jnp.minimum(1.0, CLIP_NORM / norm_gen) / count_total
-    scale_fake = jnp.minimum(1.0, CLIP_NORM / norm_fake) / count_total
-    gw_o, gm_o, gv_o = adam_step(gen_w[0], gen_m[0], gen_v[0], gen_shard * scale_gen)
-    gs_o, gsm_o, gsv_o = adam_step(
-        gen_small[0], gen_small_m[0], gen_small_v[0], gen_small_sum * scale_gen
-    )
-    fw_o, fm_o, fv_o = adam_step(fake_w[0], fake_m[0], fake_v[0], fake_shard * scale_fake)
-    fs_o, fsm_o, fsv_o = adam_step(
-        fake_small[0], fake_small_m[0], fake_small_v[0], fake_small_sum * scale_fake
-    )
-    ge_o = ema_rate * gen_ema[0] + (1.0 - ema_rate) * gw_o
-    gse_o = ema_rate * gen_small_ema[0] + (1.0 - ema_rate) * gs_o
-    norms = jnp.stack([norm_gen, norm_fake])
-    losses = jnp.stack([gen_total, fake_total]) / count_total
-    outs = (gw_o, gm_o, gv_o, ge_o, gs_o, gsm_o, gsv_o, gse_o, fw_o, fm_o, fv_o, fs_o, fsm_o, fsv_o)
-    return tuple(a[None] for a in outs) + (norms, losses)
 
 
 def solution(mesh):

time: 916 us -> 467 us (0.51)
  waiting for transfers between devices: 482 us -> 0 us
  Pallas kernels: 238 us -> 422 us
  blocking collectives: 128 us -> 2.09 us
  between operations: 23 us -> 1.77 us
  other arithmetic: 26.2 us -> 16.8 us
    reduce_scatter x6 -> x0, waiting for transfers between devices: 261 us -> none  [the longest x2 217 us: reduce_net(): own = lax.psum_scatter(own, 'dp', scatter_dimension=1, tiled=True)]
    all_gather x6 -> x0, waiting for transfers between devices: 218 us -> none  [the longest x3 216 us: gather_net(): rows = lax.all_gather(shard.astype(BF16), 'dp', axis=1, tiled=True)]
    pallas_call x0 -> x3, Pallas kernels: none -> 190 us  [the longest x1 95 us: gather_nets(): pl.pallas_call(gather_kernel, out_shape=[jax.ShapeDtypeStruct((2 * ROWS,...]
    psum x2 -> x0, blocking collectives: 122 us -> none  [the longest x1 80.9 us: reduce_net(): return (own[0], lax.psum(small, 'dp')[0, :13])]
  transfers between devices with their start and end apart: 12 -> 0, of which waited for: 9 -> 0; matrix products, arithmetic and copies ran while one was open for 2% -> 0% of each run, Pallas kernels for 12% -> 0%
where the time goes in v2:
time: 467 us; the launch traced here: 462 us
  Pallas kernels  422 us (90%)
  local copies, waits for them, and re-layouts  19.3 us (4%)
  other arithmetic  16.8 us (4%)
    pallas_call x4, Pallas kernels, run_backward(): pl.pallas_call(functools.partial(backward_kernel, want), out_shape=outs,...  138 us
    pallas_call x1, Pallas kernels, gather_nets(): pl.pallas_call(gather_kernel, out_shape=[jax.ShapeDtypeStruct((2 * ROWS,...  95 us
    pallas_call x3, Pallas kernels, run_forward(): pl.pallas_call(forward_kernel, out_shape=saved_shapes(images), in_specs=v...  94.1 us
    pallas_call x1, Pallas kernels, reduce_nets(): pl.pallas_call(reduce_kernel, out_shape=[jax.ShapeDtypeStruct((nets, part...  90.5 us
    unnamed x44, local copies, waits for them, and re-layouts  12.6 us

profile of v2, /device:TPU:0, one launch (start us, length us, event | category | flops | bytes accessed | tf_op | source)
XLA Modules:
  0.0 462.0 jit_solution(4746554835054102734)
XLA Ops:
  1.4 1.3 multiply_multiply_fusion.2
  2.7 2.1 dynamic-slice_multiply_fusion.x0
  4.8 95.0 %shard_map.315 = (bf16[13312,256]{1,0:T(8,128)(2,1)}, bf16[13312,256]{1,0:T(8,128)(2,1)}, bf16[13312,256]{1,0:T(8,128)(2,1)}) custom-call(f32[416,256]{1,0:T(8,128)} %bitcast.75, f32[416,256]{1,0:T(8,128)} %bitcast.76, bf16[416,256]{1,0:T(8,128)(2,1)} %bitcast.78), custom_call_target="tpu_custom_call" | custom-call | tf_op jit(solution)/shard_map/pallas_call | solution.py:619
  99.9 2.1 all-gather
  106.5 31.6 %shard_map.316 = (f32[3,3,256,256]{3,2,1,0:T(8,128)}, f32[2,3,256,256]{3,2,1,0:T(8,128)}, f32[2,3,256,256]{3,2,1,0:T(8,128)}, bf16[2,3,256,768]{3,2,1,0:T(8,128)...) custom-call(f32[3,256,256]{2,1,0:T(8,128)} %dynamic-slice_multiply_fusion.x0, ...), custom_call_target="tpu_custom_call" | custom-call | tf_op jit(solution)/shard_map/pallas_call | solution.py:458
  138.1 2.3 broadcast_multiply_fusion.1
  140.4 31.3 %shard_map.318 = (f32[3,3,256,256]{3,2,1,0:T(8,128)}, f32[2,3,256,256]{3,2,1,0:T(8,128)}, f32[2,3,256,256]{3,2,1,0:T(8,128)}, bf16[2,3,256,768]{3,2,1,0:T(8,128)...) custom-call(f32[3,256,256]{2,1,0:T(8,128)} %get-tuple-element.180.x0, ...), custom_call_target="tpu_custom_call" | custom-call | tf_op jit(solution)/shard_map/pallas_call | solution.py:458
  171.7 31.2 %shard_map.317 = (f32[3,3,256,256]{3,2,1,0:T(8,128)}, f32[2,3,256,256]{3,2,1,0:T(8,128)}, f32[2,3,256,256]{3,2,1,0:T(8,128)}, bf16[2,3,256,768]{3,2,1,0:T(8,128)...) custom-call(f32[3,256,256]{2,1,0:T(8,128)} %get-tuple-element.180.x0, ...), custom_call_target="tpu_custom_call" | custom-call | tf_op jit(solution)/shard_map/pallas_call | solution.py:458
  202.9 2.7 fusion.7
  205.6 1.6 fusion.10
  208.2 28.9 %shard_map.319 = f32[3,256,256]{2,1,0:T(8,128)} custom-call(f32[3,256,256]{2,1,0:T(8,128)} %get-tuple-element.183.refs_0_, bf16[2,6656,256]{2,1,0:T(8,128)(2,1)} %bitcast.68, f32[2,13,256]{2,1,0:T(8,128)} %get-tuple-element.189.small.refs_2_, f32[1024,8]{1,0:T(8,128)} %bitcast.69, f32[3,3,256,256]{3,2,1,0:T(8,128)} %get-tuple-element.65.refs_4_, ...), custom_call_target="tpu_custom_call" | custom-call | tf_op jit(solution)/shard_map/pallas_call | solution.py:476
  237.1 28.7 %shard_map.320 = f32[3,256,256]{2,1,0:T(8,128)} custom-call(f32[3,256,256]{2,1,0:T(8,128)} %get-tuple-element.182.refs_0_, bf16[2,6656,256]{2,1,0:T(8,128)(2,1)} %bitcast.63, f32[2,13,256]{2,1,0:T(8,128)} %get-tuple-element.191.small.refs_2_, f32[1024,8]{1,0:T(8,128)} %bitcast.70, f32[3,3,256,256]{3,2,1,0:T(8,128)} %get-tuple-element.67.refs_4_, ...), custom_call_target="tpu_custom_call" | custom-call | tf_op jit(solution)/shard_map/pallas_call | solution.py:476
  265.8 2.4 add_multiply_fusion.refs_0_
  269.3 40.1 %shard_map.321 = (f32[3,256,256]{2,1,0:T(8,128)}, bf16[2,6656,256]{2,1,0:T(8,128)(2,1)}, f32[2,16,256]{2,1,0:T(8,128)}) custom-call(f32[3,256,256]{2,1,0:T(8,128)} %add_multiply_fusion.refs_0_, bf16[2,6656,256]{2,1,0:T(8,128)(2,1)} %bitcast.66, f32[2,13,256]{2,1,0:T(8,128)} %get-tuple-element.190.small.refs_2_, f32[1024,8]{1,0:T(8,128)} %bitcast.74, ...), custom_call_target="tpu_custom_call" | custom-call | tf_op jit(solution)/shard_map/pallas_call | solution.py:476
  309.4 40.4 %shard_map.322 = (f32[3,256,256]{2,1,0:T(8,128)}, bf16[2,6656,256]{2,1,0:T(8,128)(2,1)}, f32[2,16,256]{2,1,0:T(8,128)}) custom-call(f32[3,256,256]{2,1,0:T(8,128)} %get-tuple-element.184.refs_0_, bf16[2,6656,256]{2,1,0:T(8,128)(2,1)} %bitcast.64, f32[2,13,256]{2,1,0:T(8,128)} %get-tuple-element.191.small.refs_2_, f32[1024,8]{1,0:T(8,128)} %bitcast.71, ...), custom_call_target="tpu_custom_call" | custom-call | tf_op jit(solution)/shard_map/pallas_call | solution.py:476
  349.8 2.0 pad_maximum_fusion.8
  351.8 1.5 pad_maximum_fusion.refs_2_
  353.3 90.5 %shard_map.323 = (f32[2,416,256]{2,1,0:T(8,128)}, f32[32,256]{1,0:T(8,128)}, f32[8,128]{1,0:T(8,128)}) custom-call(bf16[13312,256]{1,0:T(8,128)(2,1)} %bitcast.72, bf16[13312,256]{1,0:T(8,128)(2,1)} %bitcast.73, f32[2,32,256]{2,1,0:T(8,128)} %pad_maximum_fusion.refs_2_), custom_call_target="tpu_custom_call" | custom-call | tf_op jit(solution)/shard_map/pallas_call | solution.py:811
  446.8 4.4 shard_map.324
  451.2 1.3 copy.120
  452.5 1.3 copy.121
  453.9 1.3 copy.122
  455.2 1.3 copy.123
  460.5 1.3 slice_bitcast_fusion.3
  (59 shorter events, 13.5 us)
Async XLA Ops:
  0.6 99.2 %copy-start.6 = (f32[1,13,256]{2,0,1:T(1,128)S(1)}, f32[1,13,256]{2,0,1:T(1,128)}, u32[]{:S(2)}) copy-start(f32[1,13,256]{2,0,1:T(1,128)} %param.39) | copy-start | bytes 39940
  0.7 99.2 %copy-start.7 = (f32[1,13,256]{2,0,1:T(1,128)S(1)}, f32[1,13,256]{2,0,1:T(1,128)}, u32[]{:S(2)}) copy-start(f32[1,13,256]{2,0,1:T(1,128)} %param.35) | copy-start | bytes 39940
  0.7 99.2 %copy-start.8 = (f32[1,13,256]{2,0,1:T(1,128)S(1)}, f32[1,13,256]{2,0,1:T(1,128)}, u32[]{:S(2)}) copy-start(f32[1,13,256]{2,0,1:T(1,128)} %param.28) | copy-start | bytes 39940
  99.9 5.4 %copy-start.3 = (f32[1,13,256]{2,1,0:T(8,128)}, f32[1,13,256]{2,1,0:T(8,128)S(1)}, u32[]{:S(2)}) copy-start(f32[1,13,256]{2,1,0:T(8,128)S(1)} %copy.102.refs_11_) | copy-start | bytes 39940
  99.9 5.4 %copy-start.4 = (f32[1,13,256]{2,1,0:T(8,128)}, f32[1,13,256]{2,1,0:T(8,128)S(1)}, u32[]{:S(2)}) copy-start(f32[1,13,256]{2,1,0:T(8,128)S(1)} %copy.101.refs_4_) | copy-start | bytes 39940
  106.5 31.6 %copy-start = (f32[6,256,256]{2,1,0:T(8,128)S(1)}, f32[6,256,256]{2,1,0:T(8,128)}, u32[]{:S(2)}) copy-start(f32[6,256,256]{2,1,0:T(8,128)} %param.20) | copy-start | bytes 4718596
  106.5 31.6 %copy-start.2 = (f32[6,256,256]{2,1,0:T(8,128)S(1)}, f32[6,256,256]{2,1,0:T(8,128)}, u32[]{:S(2)}) copy-start(f32[6,256,256]{2,1,0:T(8,128)} %param.21) | copy-start | bytes 4718596
  237.1 28.7 %copy-start.1 = (f32[3,256,256]{2,1,0:T(8,128)S(1)}, f32[3,256,256]{2,1,0:T(8,128)}, u32[]{:S(2)}) copy-start(f32[3,256,256]{2,1,0:T(8,128)} %shard_map.319) | copy-start | bytes 2359300
  309.4 42.5 %copy-start.5 = (f32[2,16,256]{2,1,0:T(8,128)S(1)}, f32[2,16,256]{2,1,0:T(8,128)}, u32[]{:S(2)}) copy-start(f32[2,16,256]{2,1,0:T(8,128)} %get-tuple-element.88) | copy-start | bytes 98308
  353.3 90.5 %copy-start.9 = (f32[1,13,256]{2,0,1:T(1,128)S(1)}, f32[1,13,256]{2,0,1:T(1,128)}, u32[]{:S(2)}) copy-start(f32[1,13,256]{2,0,1:T(1,128)} %param.29) | copy-start | bytes 39940
  353.3 91.1 %copy-start.10 = (f32[1,13,256]{2,0,1:T(1,128)S(1)}, f32[1,13,256]{2,0,1:T(1,128)}, u32[]{:S(2)}) copy-start(f32[1,13,256]{2,0,1:T(1,128)} %param.30) | copy-start | bytes 39940
  353.3 91.7 %copy-start.11 = (f32[1,13,256]{2,0,1:T(1,128)S(1)}, f32[1,13,256]{2,0,1:T(1,128)}, u32[]{:S(2)}) copy-start(f32[1,13,256]{2,0,1:T(1,128)} %param.31) | copy-start | bytes 39940
  353.3 92.3 %copy-start.12 = (f32[1,13,256]{2,0,1:T(1,128)S(1)}, f32[1,13,256]{2,0,1:T(1,128)}, u32[]{:S(2)}) copy-start(f32[1,13,256]{2,0,1:T(1,128)} %param.36) | copy-start | bytes 39940
  353.3 92.9 %copy-start.13 = (f32[1,13,256]{2,0,1:T(1,128)S(1)}, f32[1,13,256]{2,0,1:T(1,128)}, u32[]{:S(2)}) copy-start(f32[1,13,256]{2,0,1:T(1,128)} %param.37) | copy-start | bytes 39940

commit v3 on v2

--- a/solution.py
+++ b/solution.py
@@ -86,24 +86,15 @@
     return lax.dot_general(a, b, (((0,), (0,)), ((), ())), preferred_element_type=F32)
 
 
-def group_mean(row):
-    v = jnp.broadcast_to(row, (8, C))
+def group_mean(v):
     lane = lax.broadcasted_iota(jnp.int32, (8, C), 1)
     for sh in (1, 2, 4):
         v = v + jnp.where((lane & sh) != 0, pltpu.roll(v, sh, 1), pltpu.roll(v, C - sh, 1))
-    return v[0:1] * (1.0 / (POS * 8))
+    return v * (1.0 / (POS * 8))
 
 
 def colsum(v):
     return jnp.sum(v, axis=0, keepdims=True)
-
-
-def norm_stats(ref, *at):
-    x = ref[at]
-    mean = group_mean(colsum(x))
-    d = x - mean
-    inv = lax.rsqrt(group_mean(colsum(d * d)) + NORM_EPS)
-    return mean, inv
 
 
 def put_shifted(bufs, i, r, v):
@@ -166,9 +157,27 @@
             qkvw[:, at : at + HALF] = tmp[h, pl.ds(j, C, stride=3), :].astype(BF16)
 
 
-def layer_forward(l, w, small, eo, xs, h1, y, qkv, att, o, st, bufs, nbuf, qkvw, tmp):
+def norm_stats(views):
+    fill = [jnp.zeros((8 - len(views), C), F32)]
+    sums = jnp.concatenate([colsum(x) for x in views] + fill, axis=0)
+    mean = group_mean(sums)
+    squares = [colsum(jnp.square(x - mean[i : i + 1])) for i, x in enumerate(views)]
+    return mean, lax.rsqrt(group_mean(jnp.concatenate(squares + fill, axis=0)) + NORM_EPS)
+
+
+def tap_rows(bufs, flip, which):
+    out = []
+    for dr in (-1, 0, 1):
+        for dc in (-1, 0, 1):
+            sr, sc = (-dr, -dc) if flip else (dr, dc)
+            at = slice(PAD + SIDE * sr, PAD + SIDE * sr + POS)
+            piece = jnp.concatenate([bufs[sc + 1, i, at, :] for i in which], axis=0)
+            out.append(piece)
+    return out
+
+
+def layer_forward(l, w, small, eo, xs, h1, y, qkv, att, o, st, bufs, nbuf, qkvw, tmp, staged):
     images = h1.shape[1]
-    flat = images * POS
     split_qkv(w, l, qkvw, tmp)
     mod = dot_nn(eo[...], w[l, R_EMB : R_EMB + 4 * C, :])
     ma = mod[0:4] + small[l, 5:6, :]
@@ -177,63 +186,90 @@
         st[l, i, S_MA : S_MA + 1, :] = ma[i : i + 1]
         st[l, i, S_MB : S_MB + 1, :] = mb[i : i + 1]
 
-    def first(i, _):
-        mean, inv = norm_stats(xs, l, i)
-        st[l, i, S_M1 : S_M1 + 1, :] = mean
-        st[l, i, S_I1 : S_I1 + 1, :] = inv
-        a = inv * small[l, 0:1, :]
-        b = small[l, 1:2, :]
-        for r in range(0, POS, CHUNK):
-            put_shifted(bufs, i, r, silu((xs[l, i, r : r + CHUNK, :] - mean) * a + b))
-        return 0
-
-    lax.fori_loop(0, images, first, 0)
-    h1[l] = (conv_forward(bufs, w, l, R_CONV1) + small[l, 2:3, :]).reshape(images, POS, C)
-
-    def second(i, _):
-        mean, inv = norm_stats(h1, l, i)
-        st[l, i, S_M2 : S_M2 + 1, :] = mean
-        st[l, i, S_I2 : S_I2 + 1, :] = inv
-        gain = 1.0 + st[l, i, S_MA : S_MA + 1, :]
-        a = inv * small[l, 3:4, :] * gain
-        b = small[l, 4:5, :] * gain + st[l, i, S_MB : S_MB + 1, :]
-        for r in range(0, POS, CHUNK):
-            put_shifted(bufs, i, r, silu((h1[l, i, r : r + CHUNK, :] - mean) * a + b))
-        return 0
-
-    lax.fori_loop(0, images, second, 0)
-    h2 = conv_forward(bufs, w, l, R_CONV2) + small[l, 7:8, :]
-    y[l] = (xs[l] + h2.reshape(images, POS, C)) * RS
-
-    def third(i, _):
-        mean, inv = norm_stats(y, l, i)
-        st[l, i, S_M3 : S_M3 + 1, :] = mean
-        st[l, i, S_I3 : S_I3 + 1, :] = inv
-        a = inv * small[l, 8:9, :]
-        b = small[l, 9:10, :]
-        for r in range(0, POS, CHUNK):
-            nbuf[i, r : r + CHUNK, :] = ((y[l, i, r : r + CHUNK, :] - mean) * a + b).astype(BF16)
-        return 0
-
-    lax.fori_loop(0, images, third, 0)
-    n = nbuf[...].reshape(flat, C)
-    for j, row in ((0, 10), (1, None), (2, 11)):
-        part = dot_nn(n, qkvw[:, j * C : (j + 1) * C])
-        if row is not None:
-            part = part + small[l, row : row + 1, :]
-        qkv[l, :, :, j * C : (j + 1) * C] = part.astype(BF16).reshape(images, POS, C)
-
-    def attend(i, _):
-        s = dot_nt(qkv[l, i, :, 0:C], qkv[l, i, :, C : 2 * C])
-        e = jnp.exp((s - jnp.max(s, axis=1, keepdims=True)) * (C**-0.5))
-        p = (e * (1.0 / jnp.sum(e, axis=1, keepdims=True))).astype(BF16)
-        att[l, i] = p
-        o[l, i] = dot_nn(p, qkv[l, i, :, 2 * C :]).astype(BF16)
-        return 0
-
-    lax.fori_loop(0, images, attend, 0)
-    out = dot_nn(o[l].reshape(flat, C), w[l, R_PROJ:, :]) + small[l, 12:13, :]
-    xs[l + 1] = (y[l] + out.reshape(images, POS, C)) * RS
+    def row(k):
+        return small[l, k : k + 1, :]
+
+    def keep(which, mean, inv, at):
+        for k, i in enumerate(which):
+            st[l, i, at : at + 1, :] = mean[k : k + 1]
+            st[l, i, at + 1 : at + 2, :] = inv[k : k + 1]
+
+    def first(which):
+        mean, inv = norm_stats([xs[l, i] for i in which])
+        keep(which, mean, inv, S_M1)
+        for k, i in enumerate(which):
+            a = inv[k : k + 1] * row(0)
+            for r in range(0, POS, CHUNK):
+                v = (xs[l, i, r : r + CHUNK, :] - mean[k : k + 1]) * a + row(1)
+                put_shifted(bufs, i, r, silu(v))
+
+    def conv(which, at):
+        left = jnp.concatenate(tap_rows(bufs, False, which), axis=1)
+        return dot_nn(left, w[l, at : at + 9 * C, :])
+
+    def conv_one(which):
+        out = conv(which, R_CONV1) + row(2)
+        for k, i in enumerate(which):
+            h1[l, i] = out[k * POS : (k + 1) * POS]
+
+    def second(which):
+        mean, inv = norm_stats([h1[l, i] for i in which])
+        keep(which, mean, inv, S_M2)
+        for k, i in enumerate(which):
+            gain = 1.0 + ma[i : i + 1]
+            a = inv[k : k + 1] * row(3) * gain
+            b = row(4) * gain + mb[i : i + 1]
+            for r in range(0, POS, CHUNK):
+                v = (h1[l, i, r : r + CHUNK, :] - mean[k : k + 1]) * a + b
+                put_shifted(bufs, i, r, silu(v))
+
+    def conv_two(which):
+        out = conv(which, R_CONV2) + row(7)
+        for k, i in enumerate(which):
+            y[l, i] = (xs[l, i] + out[k * POS : (k + 1) * POS]) * RS
+
+    def third(which):
+        mean, inv = norm_stats([y[l, i] for i in which])
+        keep(which, mean, inv, S_M3)
+        for k, i in enumerate(which):
+            a = inv[k : k + 1] * row(8)
+            for r in range(0, POS, CHUNK):
+                v = (y[l, i, r : r + CHUNK, :] - mean[k : k + 1]) * a + row(9)
+                nbuf[i, r : r + CHUNK, :] = v.astype(BF16)
+
+    def project_in(which):
+        n = jnp.concatenate([nbuf[i] for i in which], axis=0)
+        for j, at in ((0, 10), (1, None), (2, 11)):
+            part = dot_nn(n, qkvw[:, j * C : (j + 1) * C])
+            if at is not None:
+                part = part + row(at)
+            part = part.astype(BF16)
+            for k, i in enumerate(which):
+                qkv[l, i, :, j * C : (j + 1) * C] = part[k * POS : (k + 1) * POS]
+
+    def attend(which):
+        scores = [dot_nt(qkv[l, i, :, 0:C], qkv[l, i, :, C : 2 * C]) for i in which]
+        for s, i in zip(scores, which):
+            e = jnp.exp((s - jnp.max(s, axis=1, keepdims=True)) * (C**-0.5))
+            p = (e * (1.0 / jnp.sum(e, axis=1, keepdims=True))).astype(BF16)
+            att[l, i] = p
+            o[l, i] = dot_nn(p, qkv[l, i, :, 2 * C :]).astype(BF16)
+
+    def project_out(which):
+        left = jnp.concatenate([o[l, i] for i in which], axis=0)
+        out = dot_nn(left, w[l, R_PROJ:, :]) + row(12)
+        for k, i in enumerate(which):
+            xs[l + 1, i] = (y[l, i] + out[k * POS : (k + 1) * POS]) * RS
+
+    steps = (first, conv_one, second, conv_two, third, project_in, attend, project_out)
+    if not staged:
+        for step in steps:
+            step(range(images))
+    else:
+        for t in range(len(steps) + images - 1):
+            for i in range(images):
+                if 0 <= t - i < len(steps):
+                    steps[t - i]([i])
 
 
 def layer_backward(
@@ -242,155 +278,155 @@
 ):
     want = grad is not None
     images = h1.shape[1]
+    which = range(images)
     flat = images * POS
     scale = C**-0.5
-    zrow = jnp.zeros((1, C), F32)
     split_qkv(w, l, qkvw, tmp)
+
+    def row(k):
+        return small[l, k : k + 1, :]
+
+    def rows8(rows):
+        return jnp.concatenate(list(rows) + [jnp.zeros((8 - len(rows), C), F32)], axis=0)
+
+    def stat(at):
+        return [(st[l, i, at : at + 1, :], st[l, i, at + 1 : at + 2, :]) for i in which]
+
     gp = (g[...] * RS).astype(BF16).reshape(flat, C)
     nbuf[...] = dot_nt(gp, w[l, R_PROJ:, :]).astype(BF16).reshape(images, POS, C)
     if want:
         grad[l, R_PROJ:, :] = dot_tn(o[l].reshape(flat, C), gp).astype(BF16)
         sgrad[l, 12:13, :] = colsum(gp.astype(F32))
-
-    def attend(i, _):
+    dps = [dot_nt(nbuf[i], qkv[l, i, :, 2 * C :]) for i in which]
+    for i, dp in zip(which, dps):
         p = att[l, i]
         pf = p.astype(F32)
-        do = nbuf[i]
-        dp = dot_nt(do, qkv[l, i, :, 2 * C :])
         ds = (pf * (dp - jnp.sum(dp * pf, axis=1, keepdims=True))).astype(BF16)
         dqkv[i, :, 0:C] = (dot_nn(ds, qkv[l, i, :, C : 2 * C]) * scale).astype(BF16)
         dqkv[i, :, C : 2 * C] = (dot_tn(ds, qkv[l, i, :, 0:C]) * scale).astype(BF16)
-        dqkv[i, :, 2 * C :] = dot_tn(p, do).astype(BF16)
-        return 0
-
-    lax.fori_loop(0, images, attend, 0)
-    dq = dqkv[...].reshape(flat, 3 * C)
-    dn[...] = dot_nt(dq, qkvw[...]).reshape(images, POS, C)
-
-    def third(i, carry):
-        db7, dg8, db9 = carry
-        mean, inv = st[l, i, S_M3 : S_M3 + 1, :], st[l, i, S_I3 : S_I3 + 1, :]
-        gain = small[l, 8:9, :]
-        nh = (y[l, i] - mean) * inv
-        c1 = colsum(dn[i])
-        c2 = colsum(dn[i] * nh)
-        mg = group_mean(gain * c1)
-        mc = group_mean(gain * c2)
+        dqkv[i, :, 2 * C :] = dot_tn(p, nbuf[i]).astype(BF16)
+    dn[...] = dot_nt(dqkv[...].reshape(flat, 3 * C), qkvw[...]).reshape(images, POS, C)
+
+    stats = stat(S_M3)
+    c1 = rows8([colsum(dn[i]) for i in which])
+    c2 = rows8([colsum(dn[i] * ((y[l, i] - stats[i][0]) * stats[i][1])) for i in which])
+    mg = group_mean(row(8) * c1)
+    mc = group_mean(row(8) * c2)
+    db7 = jnp.zeros((1, C), F32)
+    for i in which:
+        mean, inv = stats[i]
         for r in range(0, POS, CHUNK):
-            nhr = (y[l, i, r : r + CHUNK, :] - mean) * inv
+            nh = (y[l, i, r : r + CHUNK, :] - mean) * inv
             gm = g[i, r : r + CHUNK, :] * RS + inv * (
-                gain * dn[i, r : r + CHUNK, :] - mg - nhr * mc
+                row(8) * dn[i, r : r + CHUNK, :] - mg[i : i + 1] - nh * mc[i : i + 1]
             )
             gm = gm * RS
             g[i, r : r + CHUNK, :] = gm
             put_shifted(bufs, i, r, gm)
             if want:
-                nbuf[i, r : r + CHUNK, :] = (nhr * gain + small[l, 9:10, :]).astype(BF16)
-                db7 = db7 + colsum(gm.astype(BF16).astype(F32))
-        return db7, dg8 + c2, db9 + c1
-
-    db7, dg8, db9 = lax.fori_loop(0, images, third, (zrow, zrow, zrow))
+                nbuf[i, r : r + CHUNK, :] = (nh * row(8) + row(9)).astype(BF16)
+                db7 = db7 + colsum(gm)
     if want:
         sgrad[l, 7:8, :] = db7
-        sgrad[l, 8:9, :] = dg8
-        sgrad[l, 9:10, :] = db9
+        sgrad[l, 8:9, :] = colsum(c2)
+        sgrad[l, 9:10, :] = colsum(c1)
         act_t[...] = nbuf[...].reshape(flat, C).T
         for j in range(3):
             dj = dqkv[:, :, j * C : (j + 1) * C].reshape(flat, C)
-            wide = dot_nn(act_t[...], dj)
+            part = dot_nn(act_t[...], dj)
             for h in range(2):
-                tmp[h, pl.ds(j, C, stride=3), :] = wide[:, h * HALF : (h + 1) * HALF]
+                tmp[h, pl.ds(j, C, stride=3), :] = part[:, h * HALF : (h + 1) * HALF]
             if j != 1:
                 sgrad[l, 10 + j // 2 : 11 + j // 2, :] = colsum(dj.astype(F32))
         for h in range(2):
             grad[l, R_QKV : R_QKV + 3 * C, h * HALF : (h + 1) * HALF] = tmp[h].astype(BF16)
     dn[...] = conv_input_grad(bufs, w, l, R_CONV2).reshape(images, POS, C)
 
-    def second_a(i, _):
-        mean, inv = st[l, i, S_M2 : S_M2 + 1, :], st[l, i, S_I2 : S_I2 + 1, :]
-        gain = 1.0 + st[l, i, S_MA : S_MA + 1, :]
-        a = inv * small[l, 3:4, :] * gain
-        b = small[l, 4:5, :] * gain + st[l, i, S_MB : S_MB + 1, :]
+    stats = stat(S_M2)
+    gains = [1.0 + st[l, i, S_MA : S_MA + 1, :] for i in which]
+    p1, p2 = [], []
+    for i in which:
+        mean, inv = stats[i]
+        a = row(3) * gains[i]
+        b = row(4) * gains[i] + st[l, i, S_MB : S_MB + 1, :]
+        s1 = jnp.zeros((1, C), F32)
+        s2 = jnp.zeros((1, C), F32)
         for r in range(0, POS, CHUNK):
-            pre = (h1[l, i, r : r + CHUNK, :] - mean) * a + b
+            nh = (h1[l, i, r : r + CHUNK, :] - mean) * inv
+            pre = nh * a + b
             s, slope = silu_parts(pre)
-            dn[i, r : r + CHUNK, :] = dn[i, r : r + CHUNK, :] * slope
+            d = dn[i, r : r + CHUNK, :] * slope
+            dn[i, r : r + CHUNK, :] = d
+            s1 = s1 + colsum(d)
+            s2 = s2 + colsum(d * nh)
             if want:
                 nbuf[i, r : r + CHUNK, :] = (pre * s).astype(BF16)
-        return 0
-
-    lax.fori_loop(0, images, second_a, 0)
+        p1.append(s1)
+        p2.append(s2)
     if want:
         act_t[...] = nbuf[...].reshape(flat, C).T
         conv_weight_grad(act_t, bufs, grad, l, R_CONV2)
-    row8 = lax.broadcasted_iota(jnp.int32, (8, C), 0)
-
-    def second_b(i, carry):
-        db2, dg3, db4, dm = carry
-        mean, inv = st[l, i, S_M2 : S_M2 + 1, :], st[l, i, S_I2 : S_I2 + 1, :]
-        modgain = 1.0 + st[l, i, S_MA : S_MA + 1, :]
-        gain = small[l, 3:4, :]
-        nh = (h1[l, i] - mean) * inv
-        p1 = colsum(dn[i])
-        p2 = colsum(dn[i] * nh)
-        full = gain * modgain
-        mg = group_mean(full * p1)
-        mc = group_mean(full * p2)
+    full = rows8([row(3) * gains[i] for i in which])
+    p18, p28 = rows8(p1), rows8(p2)
+    mg = group_mean(full * p18)
+    mc = group_mean(full * p28)
+    db2 = jnp.zeros((1, C), F32)
+    for i in which:
+        mean, inv = stats[i]
         for r in range(0, POS, CHUNK):
-            nhr = (h1[l, i, r : r + CHUNK, :] - mean) * inv
-            dh = inv * (full * dn[i, r : r + CHUNK, :] - mg - nhr * mc)
+            nh = (h1[l, i, r : r + CHUNK, :] - mean) * inv
+            dh = inv * (full[i : i + 1] * dn[i, r : r + CHUNK, :] - mg[i : i + 1] - nh * mc[i : i + 1])
             put_shifted(bufs, i, r, dh)
             if want:
-                db2 = db2 + colsum(dh.astype(BF16).astype(F32))
-        dma = gain * p2 + small[l, 4:5, :] * p1
-        dm = jnp.where(row8 == i, dma, jnp.where(row8 == i + 4, p1, dm))
-        return db2, dg3 + modgain * p2, db4 + modgain * p1, dm
-
-    db2, dg3, db4, dm = lax.fori_loop(
-        0, images, second_b, (zrow, zrow, zrow, jnp.zeros((8, C), F32))
-    )
+                db2 = db2 + colsum(dh)
     if want:
+        modgain = rows8(gains)
+        dma = row(3) * p28 + row(4) * p18
+        dm = jnp.concatenate([dma[0:4], p18[0:4]], axis=0)
         sgrad[l, 2:3, :] = db2
-        sgrad[l, 3:4, :] = dg3
-        sgrad[l, 4:5, :] = db4
-        sgrad[l, 5:6, :] = colsum(dm[0:4])
-        sgrad[l, 6:7, :] = colsum(dm[4:8])
+        sgrad[l, 3:4, :] = colsum(modgain * p28)
+        sgrad[l, 4:5, :] = colsum(modgain * p18)
+        sgrad[l, 5:6, :] = colsum(dma)
+        sgrad[l, 6:7, :] = colsum(p18)
         grad[l, R_EMB : R_EMB + 4 * C, :] = lax.dot_general(
             eot[...], dm, (((1,), (0,)), ((), ())),
             precision=lax.Precision.HIGHEST, preferred_element_type=F32,
         ).astype(BF16)
     dn[...] = conv_input_grad(bufs, w, l, R_CONV1).reshape(images, POS, C)
 
-    def first(i, carry):
-        dg0, db1 = carry
-        mean, inv = st[l, i, S_M1 : S_M1 + 1, :], st[l, i, S_I1 : S_I1 + 1, :]
-        gain = small[l, 0:1, :]
-        b = small[l, 1:2, :]
-        c1, c2 = zrow, zrow
+    stats = stat(S_M1)
+    p1, p2 = [], []
+    for i in which:
+        mean, inv = stats[i]
+        s1 = jnp.zeros((1, C), F32)
+        s2 = jnp.zeros((1, C), F32)
         for r in range(0, POS, CHUNK):
-            nhr = (xs[l, i, r : r + CHUNK, :] - mean) * inv
-            pre = nhr * gain + b
+            nh = (xs[l, i, r : r + CHUNK, :] - mean) * inv
+            pre = nh * row(0) + row(1)
             s, slope = silu_parts(pre)
             d = dn[i, r : r + CHUNK, :] * slope
             dn[i, r : r + CHUNK, :] = d
-            c1 = c1 + colsum(d)
-            c2 = c2 + colsum(d * nhr)
+            s1 = s1 + colsum(d)
+            s2 = s2 + colsum(d * nh)
             if want:
                 nbuf[i, r : r + CHUNK, :] = (pre * s).astype(BF16)
-        mg = group_mean(gain * c1)
-        mc = group_mean(gain * c2)
-        for r in range(0, POS, CHUNK):
-            nhr = (xs[l, i, r : r + CHUNK, :] - mean) * inv
-            dx = inv * (gain * dn[i, r : r + CHUNK, :] - mg - nhr * mc)
-            g[i, r : r + CHUNK, :] = g[i, r : r + CHUNK, :] + dx
-        return dg0 + c2, db1 + c1
-
-    dg0, db1 = lax.fori_loop(0, images, first, (zrow, zrow))
+        p1.append(s1)
+        p2.append(s2)
     if want:
-        sgrad[l, 0:1, :] = dg0
-        sgrad[l, 1:2, :] = db1
         act_t[...] = nbuf[...].reshape(flat, C).T
         conv_weight_grad(act_t, bufs, grad, l, R_CONV1)
+    c1, c2 = rows8(p1), rows8(p2)
+    mg = group_mean(row(0) * c1)
+    mc = group_mean(row(0) * c2)
+    for i in which:
+        mean, inv = stats[i]
+        for r in range(0, POS, CHUNK):
+            nh = (xs[l, i, r : r + CHUNK, :] - mean) * inv
+            dx = inv * (row(0) * dn[i, r : r + CHUNK, :] - mg[i : i + 1] - nh * mc[i : i + 1])
+            g[i, r : r + CHUNK, :] = g[i, r : r + CHUNK, :] + dx
+    if want:
+        sgrad[l, 0:1, :] = colsum(c2)
+        sgrad[l, 1:2, :] = colsum(c1)
 
 
 def saved_shapes(images):
@@ -405,12 +441,14 @@
     ]
 
 
-def forward_kernel(x0, w, small, eo, xs, h1, y, qkv, att, o, st, bufs, nbuf, qkvw, tmp):
+def forward_kernel(staged, x0, w, small, eo, xs, h1, y, qkv, att, o, st, bufs, nbuf, qkvw, tmp):
     clear_pads(bufs)
     xs[0] = x0[...]
 
     def body(l, _):
-        layer_forward(l, w, small, eo, xs, h1, y, qkv, att, o, st, bufs, nbuf, qkvw, tmp)
+        layer_forward(
+            l, w, small, eo, xs, h1, y, qkv, att, o, st, bufs, nbuf, qkvw, tmp, staged
+        )
         return 0
 
     lax.fori_loop(0, 2, body, 0)
@@ -453,10 +491,10 @@
     ]
 
 
-def run_forward(x0, w, small, eo):
+def run_forward(x0, w, small, eo, staged=False):
     images = x0.shape[0]
     return pl.pallas_call(
-        forward_kernel,
+        functools.partial(forward_kernel, staged),
         out_shape=saved_shapes(images),
         in_specs=vm(4),
         out_specs=vm(7),
@@ -851,6 +889,7 @@
 
 
 EMA_RATE = 0.5 ** (20.0 / STEP)
+SMALL_STATES = (4, 5, 6, 7, 11, 12, 13)
 
 
 def update_kernel(shard, stot, sqtot, *refs):
@@ -868,21 +907,26 @@
         total = jnp.where(lane == 2 + n, stot[13 + n : 14 + n, 0:1] / count, total)
     nums[...] = jnp.broadcast_to(total, nums.shape)
 
-    def one(scale, grad, w, m, v, ema, ow, om, ov, oe):
-        new, first, second = adam_step(w[0], m[0], v[0], grad * scale)
-        ow[0] = new
-        om[0] = first
-        ov[0] = second
+    def one(at, grad, w, m, v, ema, ow, om, ov, oe):
+        new, first, second = adam_step(w[at], m[at], v[at], grad)
+        ow[at] = new
+        om[at] = first
+        ov[at] = second
         if ema is not None:
-            oe[0] = EMA_RATE * ema[0] + (1.0 - EMA_RATE) * new
-
-    one(scales[0], shard[0], *ins[0:4], *outs[0:4])
-    one(scales[0], stot[0:13], *ins[4:8], *outs[4:8])
-    one(scales[1], shard[1], *ins[8:11], None, *outs[8:11], None)
-    one(scales[1], stot[16:29], *ins[11:14], None, *outs[11:14], None)
+            oe[at] = EMA_RATE * ema[at] + (1.0 - EMA_RATE) * new
+
+    one(0, shard[0] * scales[0], *ins[0:4], *outs[0:4])
+    one(0, shard[1] * scales[1], *ins[8:11], None, *outs[8:11], None)
+    for k in range(13):
+        one(k, stot[k : k + 1, :] * scales[0], *ins[4:8], *outs[4:8])
+        one(k, stot[16 + k : 17 + k, :] * scales[1], *ins[11:14], None, *outs[11:14], None)
 
 
 def update_nets(shard, stot, sqtot, states):
+    def turned(arrays):
+        return [a.swapaxes(0, 1) if k in SMALL_STATES else a for k, a in enumerate(arrays)]
+
+    states = turned(states)
     res = pl.pallas_call(
         update_kernel,
         out_shape=[jax.ShapeDtypeStruct(a.shape, F32) for a in states]
@@ -892,7 +936,7 @@
         compiler_params=pltpu.CompilerParams(vmem_limit_bytes=VMEM_LIMIT),
     )(shard, stot, sqtot, *states)
     nums = res[-1]
-    return tuple(res[:-1]) + (nums[0, 0:2], nums[0, 2:4])
+    return tuple(turned(res[:-1])) + (nums[0, 0:2], nums[0, 2:4])
 
 
 def gather_plain(shard):
@@ -956,7 +1000,7 @@
         gw, fw, tw = gather_plain(gen_w), gather_plain(fake_w), gather_plain(teacher_w)
 
     raw = SIGMA_INIT * z
-    gen_saved = run_forward(g_in * raw, gw, gs, gen_eo)
+    gen_saved = run_forward(g_in * raw, gw, gs, gen_eo, True)
     samples = g_skip * raw + g_out * gen_saved[0][2]
     noisy = samples + wide(sigma) * eps
     x0 = s_in * noisy

time: 467 us -> 378 us (0.81)
  Pallas kernels: 422 us -> 345 us
  local copies, waits for them, and re-layouts: 19.3 us -> 6.9 us
    pallas_call x4, Pallas kernels: 138 us -> 95.4 us  [run_backward(): pl.pallas_call(functools.partial(backward_kernel, want), out_shape=outs,...]
    pallas_call x3, Pallas kernels: 94.1 us -> 59.6 us  [run_forward(): pl.pallas_call(functools.partial(forward_kernel, staged), out_shape=saved...]
    unnamed x44 -> x18, local copies, waits for them, and re-layouts: 12.6 us -> 0.3 us
where the time goes in v3:
time: 378 us; the launch traced here: 373 us
  Pallas kernels  345 us (91%)
  other arithmetic  16.8 us (4%)
  local copies, waits for them, and re-layouts  6.9 us (2%)
    pallas_call x4, Pallas kernels, run_backward(): pl.pallas_call(functools.partial(backward_kernel, want), out_shape=outs,...  95.4 us
    pallas_call x1, Pallas kernels, gather_nets(): pl.pallas_call(gather_kernel, out_shape=[jax.ShapeDtypeStruct((2 * ROWS,...  95 us
    pallas_call x1, Pallas kernels, reduce_nets(): pl.pallas_call(reduce_kernel, out_shape=[jax.ShapeDtypeStruct((nets, part...  90.4 us
    pallas_call x3, Pallas kernels, run_forward(): pl.pallas_call(functools.partial(forward_kernel, staged), out_shape=saved...  59.6 us

profile of v3, /device:TPU:0, one launch (start us, length us, event | category | flops | bytes accessed | tf_op | source)
XLA Modules:
  0.0 372.7 jit_solution(8875233966568481026)
XLA Ops:
  1.3 1.3 multiply_multiply_fusion.2
  2.7 2.1 dynamic-slice_multiply_fusion.x0
  4.8 95.0 %shard_map.315 = (bf16[13312,256]{1,0:T(8,128)(2,1)}, bf16[13312,256]{1,0:T(8,128)(2,1)}, bf16[13312,256]{1,0:T(8,128)(2,1)}) custom-call(f32[416,256]{1,0:T(8,128)} %bitcast.89, f32[416,256]{1,0:T(8,128)} %bitcast.90, bf16[416,256]{1,0:T(8,128)(2,1)} %bitcast.92), custom_call_target="tpu_custom_call" | custom-call | tf_op jit(solution)/shard_map/pallas_call | solution.py:657
  99.9 2.1 all-gather
  102.0 0.6 slice_bitcast_fusion.1
  105.8 0.6 fusion.20
  106.5 18.8 %shard_map.316 = (f32[3,3,256,256]{3,2,1,0:T(8,128)}, f32[2,3,256,256]{3,2,1,0:T(8,128)}, f32[2,3,256,256]{3,2,1,0:T(8,128)}, bf16[2,3,256,768]{3,2,1,0:T(8,128)...) custom-call(f32[3,256,256]{2,1,0:T(8,128)} %dynamic-slice_multiply_fusion.x0, ...), custom_call_target="tpu_custom_call" | custom-call | tf_op jit(solution)/shard_map/pallas_call | solution.py:496
  125.3 2.3 broadcast_multiply_fusion.1
  127.5 20.3 %shard_map.318 = (f32[3,3,256,256]{3,2,1,0:T(8,128)}, f32[2,3,256,256]{3,2,1,0:T(8,128)}, f32[2,3,256,256]{3,2,1,0:T(8,128)}, bf16[2,3,256,768]{3,2,1,0:T(8,128)...) custom-call(f32[3,256,256]{2,1,0:T(8,128)} %get-tuple-element.116.x0, ...), custom_call_target="tpu_custom_call" | custom-call | tf_op jit(solution)/shard_map/pallas_call | solution.py:496
  147.9 20.5 %shard_map.317 = (f32[3,3,256,256]{3,2,1,0:T(8,128)}, f32[2,3,256,256]{3,2,1,0:T(8,128)}, f32[2,3,256,256]{3,2,1,0:T(8,128)}, bf16[2,3,256,768]{3,2,1,0:T(8,128)...) custom-call(f32[3,256,256]{2,1,0:T(8,128)} %get-tuple-element.116.x0, ...), custom_call_target="tpu_custom_call" | custom-call | tf_op jit(solution)/shard_map/pallas_call | solution.py:496
  168.4 2.7 fusion.7
  171.1 1.6 fusion.10
  172.7 1.0 copy.69
  173.7 21.4 %shard_map.319 = f32[3,256,256]{2,1,0:T(8,128)} custom-call(f32[3,256,256]{2,1,0:T(8,128)} %get-tuple-element.119.refs_0_, bf16[2,6656,256]{2,1,0:T(8,128)(2,1)} %bitcast.82, f32[2,13,256]{2,1,0:T(8,128)} %get-tuple-element.125.small.refs_2_, f32[1024,8]{1,0:T(8,128)} %bitcast.83, f32[3,3,256,256]{3,2,1,0:T(8,128)} %get-tuple-element.65.refs_4_, ...), custom_call_target="tpu_custom_call" | custom-call | tf_op jit(solution)/shard_map/pallas_call | solution.py:514
  195.2 22.1 %shard_map.320 = f32[3,256,256]{2,1,0:T(8,128)} custom-call(f32[3,256,256]{2,1,0:T(8,128)} %get-tuple-element.118.refs_0_, bf16[2,6656,256]{2,1,0:T(8,128)(2,1)} %bitcast.77, f32[2,13,256]{2,1,0:T(8,128)} %get-tuple-element.127.small.refs_2_, f32[1024,8]{1,0:T(8,128)} %bitcast.84, f32[3,3,256,256]{3,2,1,0:T(8,128)} %get-tuple-element.67.refs_4_, ...), custom_call_target="tpu_custom_call" | custom-call | tf_op jit(solution)/shard_map/pallas_call | solution.py:514
  217.2 2.4 add_multiply_fusion.refs_0_
  219.7 1.0 copy.70
  220.7 25.8 %shard_map.321 = (f32[3,256,256]{2,1,0:T(8,128)}, bf16[2,6656,256]{2,1,0:T(8,128)(2,1)}, f32[2,16,256]{2,1,0:T(8,128)}) custom-call(f32[3,256,256]{2,1,0:T(8,128)} %add_multiply_fusion.refs_0_, bf16[2,6656,256]{2,1,0:T(8,128)(2,1)} %bitcast.80, f32[2,13,256]{2,1,0:T(8,128)} %get-tuple-element.126.small.refs_2_, f32[1024,8]{1,0:T(8,128)} %bitcast.88, ...), custom_call_target="tpu_custom_call" | custom-call | tf_op jit(solution)/shard_map/pallas_call | solution.py:514
  246.5 26.1 %shard_map.322 = (f32[3,256,256]{2,1,0:T(8,128)}, bf16[2,6656,256]{2,1,0:T(8,128)(2,1)}, f32[2,16,256]{2,1,0:T(8,128)}) custom-call(f32[3,256,256]{2,1,0:T(8,128)} %get-tuple-element.120.refs_0_, bf16[2,6656,256]{2,1,0:T(8,128)(2,1)} %bitcast.78, f32[2,13,256]{2,1,0:T(8,128)} %get-tuple-element.127.small.refs_2_, f32[1024,8]{1,0:T(8,128)} %bitcast.85, ...), custom_call_target="tpu_custom_call" | custom-call | tf_op jit(solution)/shard_map/pallas_call | solution.py:514
  272.6 2.0 pad_maximum_fusion.8
  274.6 1.5 pad_maximum_fusion.refs_2_
  276.1 90.4 %shard_map.323 = (f32[2,416,256]{2,1,0:T(8,128)}, f32[32,256]{1,0:T(8,128)}, f32[8,128]{1,0:T(8,128)}) custom-call(bf16[13312,256]{1,0:T(8,128)(2,1)} %bitcast.86, bf16[13312,256]{1,0:T(8,128)(2,1)} %bitcast.87, f32[2,32,256]{2,1,0:T(8,128)} %pad_maximum_fusion.refs_2_), custom_call_target="tpu_custom_call" | custom-call | tf_op jit(solution)/shard_map/pallas_call | solution.py:849
  366.5 4.6 %shard_map.324 = (f32[1,416,256]{2,1,0:T(8,128)}, f32[1,416,256]{2,1,0:T(8,128)}, f32[1,416,256]{2,1,0:T(8,128)}, f32[1,416,256]{2,1,0:T(8,128)}, f32[13,1,256]{...) custom-call(f32[2,416,256]{2,1,0:T(8,128)} %get-tuple-element.90.sha, ...), custom_call_target="tpu_custom_call" | custom-call | tf_op jit(solution)/shard_map/pallas_call | solution.py:930
  371.1 1.3 slice_bitcast_fusion.3
  (33 shorter events, 3.1 us)
Async XLA Ops:
  0.6 99.2 %copy-start.6 = (f32[1,13,256]{2,0,1:T(1,128)S(1)}, f32[1,13,256]{2,0,1:T(1,128)}, u32[]{:S(2)}) copy-start(f32[1,13,256]{2,0,1:T(1,128)} %param.39) | copy-start | bytes 39940
  0.7 99.2 %copy-start.3 = (f32[1,13,256]{2,0,1:T(1,128)S(1)}, f32[1,13,256]{2,0,1:T(1,128)}, u32[]{:S(2)}) copy-start(f32[1,13,256]{2,0,1:T(1,128)} %param.35) | copy-start | bytes 39940
  0.7 99.2 %copy-start.4 = (f32[1,13,256]{2,0,1:T(1,128)S(1)}, f32[1,13,256]{2,0,1:T(1,128)}, u32[]{:S(2)}) copy-start(f32[1,13,256]{2,0,1:T(1,128)} %param.28) | copy-start | bytes 39940
  106.5 18.8 %copy-start = (f32[6,256,256]{2,1,0:T(8,128)S(1)}, f32[6,256,256]{2,1,0:T(8,128)}, u32[]{:S(2)}) copy-start(f32[6,256,256]{2,1,0:T(8,128)} %param.20) | copy-start | bytes 4718596
  106.5 18.8 %copy-start.2 = (f32[6,256,256]{2,1,0:T(8,128)S(1)}, f32[6,256,256]{2,1,0:T(8,128)}, u32[]{:S(2)}) copy-start(f32[6,256,256]{2,1,0:T(8,128)} %param.21) | copy-start | bytes 4718596
  195.2 22.1 %copy-start.1 = (f32[3,256,256]{2,1,0:T(8,128)S(1)}, f32[3,256,256]{2,1,0:T(8,128)}, u32[]{:S(2)}) copy-start(f32[3,256,256]{2,1,0:T(8,128)} %shard_map.319) | copy-start | bytes 2359300
  246.5 28.1 %copy-start.5 = (f32[2,16,256]{2,1,0:T(8,128)S(1)}, f32[2,16,256]{2,1,0:T(8,128)}, u32[]{:S(2)}) copy-start(f32[2,16,256]{2,1,0:T(8,128)} %get-tuple-element.88) | copy-start | bytes 98308

commit v4 on v3

--- a/solution.py
+++ b/solution.py
@@ -97,6 +97,33 @@
     return jnp.sum(v, axis=0, keepdims=True)
 
 
+def no_pump(l):
+    pass
+
+
+FORWARD_POINTS, BACKWARD_POINTS = 10, 8
+
+
+class Pump:
+    def __init__(self, steps, points, layers, lo=0.0, hi=1.0):
+        self.table = {l: [[] for _ in range(points)] for l in layers}
+        self.at = 0
+        for k, step in enumerate(steps):
+            place = int((lo + (hi - lo) * (k + 0.5) / len(steps)) * points * len(layers))
+            self.table[layers[place // points]][place % points].append(step)
+
+    def __call__(self, l):
+        for layer, points in self.table.items():
+            if points[self.at]:
+
+                @pl.when(l == layer)
+                def _(todo=points[self.at]):
+                    for step in todo:
+                        step()
+
+        self.at += 1
+
+
 def put_shifted(bufs, i, r, v):
     rows = v.shape[0]
     col = lax.broadcasted_iota(jnp.int32, (rows, C), 0) & (SIDE - 1)
@@ -176,7 +203,7 @@
     return out
 
 
-def layer_forward(l, w, small, eo, xs, h1, y, qkv, att, o, st, bufs, nbuf, qkvw, tmp, staged):
+def layer_forward(l, w, small, eo, xs, h1, y, qkv, att, o, st, bufs, nbuf, qkvw, tmp, staged, pump):
     images = h1.shape[1]
     split_qkv(w, l, qkvw, tmp)
     mod = dot_nn(eo[...], w[l, R_EMB : R_EMB + 4 * C, :])
@@ -265,16 +292,18 @@
     if not staged:
         for step in steps:
             step(range(images))
+            pump(l)
     else:
         for t in range(len(steps) + images - 1):
             for i in range(images):
                 if 0 <= t - i < len(steps):
                     steps[t - i]([i])
+            pump(l)
 
 
 def layer_backward(
     l, w, small, eot, xs, h1, y, qkv, att, o, st, g, bufs, nbuf, qkvw, tmp, dn, dqkv, act_t,
-    grad, sgrad,
+    grad, sgrad, pump,
 ):
     want = grad is not None
     images = h1.shape[1]
@@ -305,7 +334,9 @@
         dqkv[i, :, 0:C] = (dot_nn(ds, qkv[l, i, :, C : 2 * C]) * scale).astype(BF16)
         dqkv[i, :, C : 2 * C] = (dot_tn(ds, qkv[l, i, :, 0:C]) * scale).astype(BF16)
         dqkv[i, :, 2 * C :] = dot_tn(p, nbuf[i]).astype(BF16)
+    pump(l)
     dn[...] = dot_nt(dqkv[...].reshape(flat, 3 * C), qkvw[...]).reshape(images, POS, C)
+    pump(l)
 
     stats = stat(S_M3)
     c1 = rows8([colsum(dn[i]) for i in which])
@@ -326,6 +357,7 @@
             if want:
                 nbuf[i, r : r + CHUNK, :] = (nh * row(8) + row(9)).astype(BF16)
                 db7 = db7 + colsum(gm)
+    pump(l)
     if want:
         sgrad[l, 7:8, :] = db7
         sgrad[l, 8:9, :] = colsum(c2)
@@ -341,6 +373,7 @@
         for h in range(2):
             grad[l, R_QKV : R_QKV + 3 * C, h * HALF : (h + 1) * HALF] = tmp[h].astype(BF16)
     dn[...] = conv_input_grad(bufs, w, l, R_CONV2).reshape(images, POS, C)
+    pump(l)
 
     stats = stat(S_M2)
     gains = [1.0 + st[l, i, S_MA : S_MA + 1, :] for i in which]
@@ -366,6 +399,7 @@
     if want:
         act_t[...] = nbuf[...].reshape(flat, C).T
         conv_weight_grad(act_t, bufs, grad, l, R_CONV2)
+    pump(l)
     full = rows8([row(3) * gains[i] for i in which])
     p18, p28 = rows8(p1), rows8(p2)
     mg = group_mean(full * p18)
@@ -379,6 +413,7 @@
             put_shifted(bufs, i, r, dh)
             if want:
                 db2 = db2 + colsum(dh)
+    pump(l)
     if want:
         modgain = rows8(gains)
         dma = row(3) * p28 + row(4) * p18
@@ -393,6 +428,7 @@
             precision=lax.Precision.HIGHEST, preferred_element_type=F32,
         ).astype(BF16)
     dn[...] = conv_input_grad(bufs, w, l, R_CONV1).reshape(images, POS, C)
+    pump(l)
 
     stats = stat(S_M1)
     p1, p2 = [], []
@@ -415,6 +451,7 @@
     if want:
         act_t[...] = nbuf[...].reshape(flat, C).T
         conv_weight_grad(act_t, bufs, grad, l, R_CONV1)
+    pump(l)
     c1, c2 = rows8(p1), rows8(p2)
     mg = group_mean(row(0) * c1)
     mc = group_mean(row(0) * c2)
@@ -447,7 +484,7 @@
 
     def body(l, _):
         layer_forward(
-            l, w, small, eo, xs, h1, y, qkv, att, o, st, bufs, nbuf, qkvw, tmp, staged
+            l, w, small, eo, xs, h1, y, qkv, att, o, st, bufs, nbuf, qkvw, tmp, staged, no_pump
         )
         return 0
 
@@ -471,7 +508,7 @@
     def body(k, _):
         layer_backward(
             1 - k, w, small, eot, xs, h1, y, qkv, att, o, st, g, bufs, nbuf, qkvw, tmp, dn,
-            dqkv, act_t, grad, sgrad,
+            dqkv, act_t, grad, sgrad, no_pump,
         )
         return 0
 
@@ -566,315 +603,558 @@
 SLOTS = 39
 
 
-def gather_kernel(*refs):
-    nets = (len(refs) - 4) // 2
-    ws, outs = refs[:nets], refs[nets : 2 * nets]
-    stage, local_sem, send_sem, recv_sem = refs[2 * nets :]
-    part = stage.shape[1]
+class Gather:
+    def __init__(self, me, net, stage, local_sem, send_sem, recv_sem):
+        self.me, self.net, self.stage = me, net, stage
+        self.local_sem, self.send_sem, self.recv_sem = local_sem, send_sem, recv_sem
+        self.part = stage.shape[0]
+        self.half = self.part // 2
+
+    def rows(self, plane, y, x, lo, count):
+        at = (plane * PLANE + y * 2 + x) * self.part + lo
+        return self.net.at[self.me.sec, pl.ds(pl.multiple_of(at, 16), count)]
+
+    def own(self, j):
+        return self.rows(self.me.plane(-j), self.me.y, self.me.x, 0, self.part)
+
+    def send(self, slot, piece, target, src=None):
+        src = piece if src is None else src
+        remote(src, piece, self.send_sem.at[slot], self.recv_sem.at[slot], target).start()
+
+    def arrived(self, slot, piece):
+        remote(
+            piece, piece, self.send_sem.at[slot], self.recv_sem.at[slot], self.me.sib
+        ).wait_recv()
+
+    def local(self):
+        return pltpu.make_async_copy(self.stage, self.own(0), self.local_sem)
+
+    def begin(self):
+        me = self.me
+        for j in (1, 2, 3):
+            self.send(Z1 + j - 1, self.own(0), me.zpeer(j), self.stage)
+        for slot, target in ((X1, me.xn), (Y1, me.yn), (S_OWN, me.sib)):
+            self.send(slot, self.own(0), target, self.stage)
+        self.local().start()
+
+    def phase1(self):
+        def step(j):
+            me = self.me
+            self.arrived(Z1 + j - 1, self.own(j))
+            for slot, target in ((X1, me.xn), (Y1, me.yn), (S_OWN, me.sib)):
+                self.send(slot + j, self.own(j), target)
+
+        return [lambda j=j: step(j) for j in (1, 2, 3)]
+
+    def phase2(self):
+        me, part, half = self.me, self.part, self.half
+
+        def step_x(j):
+            plane = me.plane(-j)
+            self.arrived(X1 + j, self.rows(plane, me.y, 1 - me.x, 0, part))
+            self.send(Y2 + j, self.rows(plane, me.y, 1 - me.x, 0, half), me.yn)
+            self.send(S_X + j, self.rows(plane, me.y, 1 - me.x, 0, part), me.sib)
+
+        def step_y(j):
+            plane = me.plane(-j)
+            self.arrived(Y1 + j, self.rows(plane, 1 - me.y, me.x, 0, part))
+            self.send(X2 + j, self.rows(plane, 1 - me.y, me.x, half, half), me.xn)
+            self.send(S_Y + j, self.rows(plane, 1 - me.y, me.x, 0, part), me.sib)
+
+        return [lambda f=f, j=j: f(j) for j in range(PLANES) for f in (step_x, step_y)]
+
+    def phase3(self):
+        def step(j, slot, to, lo):
+            me = self.me
+            where = self.rows(me.plane(-j), 1 - me.y, 1 - me.x, lo, self.half)
+            self.arrived(slot + j, where)
+            self.send(to + j, where, me.sib)
+
+        return [
+            lambda j=j, a=a: step(j, *a)
+            for j in range(PLANES)
+            for a in ((Y2, S_DA, 0), (X2, S_DB, self.half))
+        ]
+
+    def finish(self):
+        def step():
+            for slot in range(S_OWN, SLOTS):
+                count = self.part if slot < S_DA else self.half
+                self.arrived(slot, self.rows(0, 0, 0, 0, count))
+            self.local().wait()
+
+        return [step]
+
+    def drain(self):
+        for slot in range(SLOTS):
+            whole = slot < X2 or S_OWN <= slot < S_DA
+            piece = self.rows(0, 0, 0, 0, self.part if whole else self.half)
+            remote(
+                piece, piece, self.send_sem.at[slot], self.recv_sem.at[slot], self.me.sib
+            ).wait_send()
+
+
+A_SLOT, B_SLOT, C_SLOT, D_SLOT = 0, 4, 20, 28
+R_SLOTS = 31
+
+
+class Reduce:
+    def __init__(self, me, big, shard, sib, rb, rc, rd, ssem, rsem):
+        self.me, self.big, self.shard = me, big, shard
+        self.sib, self.rb, self.rc, self.rd = sib, rb, rc, rd
+        self.ssem, self.rsem = ssem, rsem
+        self.part = shard.shape[0]
+        self.half = self.part // 2
+        self.span = PLANE * self.part
+
+    def zt(self, k):
+        return self.me.plane(1 + k)
+
+    def block(self, k):
+        return pl.ds(pl.multiple_of(self.zt(k) * self.span, 16), self.span)
+
+    def piece(self, k, y, x, lo, count):
+        at = (self.zt(k) * PLANE + y * 2 + x) * self.part + lo
+        return pl.ds(pl.multiple_of(at, 16), count)
+
+    def send(self, src, dst, slot, target):
+        remote(src, dst, self.ssem.at[slot], self.rsem.at[slot], target).start()
+
+    def arrived(self, dst, slot):
+        remote(dst, dst, self.ssem.at[slot], self.rsem.at[slot], self.me.sib).wait_recv()
+
+    def begin(self):
+        for k in range(PLANES):
+            at = self.block(k)
+            self.send(self.big.at[1 - self.me.sec, at], self.sib.at[at], A_SLOT + k, self.me.sib)
+
+    def stage_a(self, k):
+        me, half = self.me, self.half
+        self.arrived(self.sib.at[self.block(k)], A_SLOT + k)
+        base = self.zt(k) * self.span
+
+        def body(i, _):
+            at = pl.ds(pl.multiple_of(base + i * half, 16), half)
+            self.big[me.sec, at, :] = (
+                self.big[me.sec, at, :].astype(F32) + self.sib[at, :].astype(F32)
+            ).astype(BF16)
+            return 0
+
+        lax.fori_loop(0, 2 * PLANE, body, 0)
+        for j in range(2):
+            self.send(
+                self.big.at[me.sec, self.piece(k, 1 - me.y, j, 0, half)], self.rb.at[k, j],
+                B_SLOT + 4 * k + j, me.yn,
+            )
+            self.send(
+                self.big.at[me.sec, self.piece(k, j, 1 - me.x, half, half)], self.rb.at[k, 2 + j],
+                B_SLOT + 4 * k + 2 + j, me.xn,
+            )
+
+    def join(self, where, other):
+        self.big[self.me.sec, where, :] = (
+            self.big[self.me.sec, where, :].astype(F32) + other.astype(F32)
+        ).astype(BF16)
+
+    def stage_c(self, k):
+        me, half = self.me, self.half
+        for j in range(4):
+            self.arrived(self.rb.at[k, j], B_SLOT + 4 * k + j)
+            y, x, lo = (me.y, j, 0) if j < 2 else (j - 2, me.x, half)
+            self.join(self.piece(k, y, x, lo, half), self.rb[k, j])
+        self.send(
+            self.big.at[me.sec, self.piece(k, me.y, 1 - me.x, 0, half)], self.rc.at[k, 0],
+            C_SLOT + 2 * k, me.xn,
+        )
+        self.send(
+            self.big.at[me.sec, self.piece(k, 1 - me.y, me.x, half, half)], self.rc.at[k, 1],
+            C_SLOT + 2 * k + 1, me.yn,
+        )
+
+    def stage_d(self, k):
+        me, half = self.me, self.half
+        for j in range(2):
+            self.arrived(self.rc.at[k, j], C_SLOT + 2 * k + j)
+            where = self.piece(k, me.y, me.x, j * half, half)
+            if k < PLANES - 1:
+                self.join(where, self.rc[k, j])
+            else:
+                self.shard[j * half : (j + 1) * half, :] = (
+                    self.big[me.sec, where, :].astype(F32) + self.rc[k, j].astype(F32)
+                )
+        if k < PLANES - 1:
+            self.send(
+                self.big.at[me.sec, self.piece(k, me.y, me.x, 0, self.part)], self.rd.at[k],
+                D_SLOT + k, me.zpeer(1 + k),
+            )
+
+    def stage_e(self):
+        for k in range(PLANES - 1):
+            self.arrived(self.rd.at[k], D_SLOT + k)
+        self.shard[...] = (
+            self.shard[...]
+            + self.rd[0].astype(F32) + (self.rd[1].astype(F32) + self.rd[2].astype(F32))
+        )
+
+    def steps(self):
+        out = []
+        for t in range(PLANES + 2):
+            for stage, lag in ((self.stage_a, 0), (self.stage_c, 1), (self.stage_d, 2)):
+                if 0 <= t - lag < PLANES:
+                    out.append(lambda stage=stage, k=t - lag: stage(k))
+        return out + [self.stage_e]
+
+    def drain(self):
+        for slot in range(R_SLOTS):
+            if slot < B_SLOT:
+                piece = self.sib.at[pl.ds(0, self.span)]
+            elif slot < D_SLOT:
+                piece = self.rb.at[0, 0]
+            else:
+                piece = self.rd.at[0]
+            remote(piece, piece, self.ssem.at[slot], self.rsem.at[slot], self.me.sib).wait_send()
+
+
+def reduce_scratch(part):
     half = part // 2
+    return [
+        pltpu.VMEM((ROWS, C), BF16),
+        pltpu.VMEM((PLANES, 4, half, C), BF16),
+        pltpu.VMEM((PLANES, 2, half, C), BF16),
+        pltpu.VMEM((PLANES - 1, part, C), BF16),
+        pltpu.SemaphoreType.DMA((R_SLOTS,)),
+        pltpu.SemaphoreType.DMA((R_SLOTS,)),
+    ]
+
+
+class Totals:
+    def __init__(self, me, buf, recv, ssem, rsem):
+        self.me, self.buf, self.recv, self.ssem, self.rsem = me, buf, recv, ssem, rsem
+
+    def send(self, src, dst, slot, target):
+        remote(src, dst, self.ssem.at[slot], self.rsem.at[slot], target).start()
+
+    def arrived(self, dst, slot):
+        remote(dst, dst, self.ssem.at[slot], self.rsem.at[slot], self.me.sib).wait_recv()
+
+    def begin(self, first):
+        self.send(first, self.recv.at[0], 0, self.me.sib)
+
+    def steps(self):
+        me, buf, recv = self.me, self.buf, self.recv
+
+        def one():
+            self.arrived(recv.at[0], 0)
+            buf[1] = buf[0] + recv[0]
+            self.send(buf.at[1], recv.at[1], 1, me.xn)
+
+        def two():
+            self.arrived(recv.at[1], 1)
+            buf[2] = buf[1] + recv[1]
+            self.send(buf.at[2], recv.at[2], 2, me.yn)
+
+        def three():
+            self.arrived(recv.at[2], 2)
+            buf[3] = buf[2] + recv[2]
+            recv[3 + me.z] = buf[3]
+            for j in (1, 2, 3):
+                self.send(buf.at[3], recv.at[3 + me.z], 2 + j, me.zpeer(j))
+
+        return [one, two, three]
+
+    def result(self):
+        for j in (1, 2, 3):
+            self.arrived(self.recv.at[3 + self.me.plane(-j)], 2 + j)
+        return (self.recv[3] + self.recv[4]) + (self.recv[5] + self.recv[6])
+
+    def drain(self):
+        for slot in range(6):
+            piece = self.recv.at[0]
+            remote(piece, piece, self.ssem.at[slot], self.rsem.at[slot], self.me.sib).wait_send()
+
+
+def totals_scratch(shape):
+    return [
+        pltpu.VMEM((4,) + shape, F32),
+        pltpu.VMEM((7,) + shape, F32),
+        pltpu.SemaphoreType.DMA((6,)),
+        pltpu.SemaphoreType.DMA((6,)),
+    ]
+
+
+def saved_scratch(images):
+    return [pltpu.VMEM(a.shape, a.dtype) for a in saved_shapes(images)]
+
+
+def backward_scratch(images):
+    return scratch_forward(images) + [
+        pltpu.VMEM((images, POS, C), F32),
+        pltpu.VMEM((images, POS, 3 * C), BF16),
+        pltpu.VMEM((C, images * POS), BF16),
+    ]
+
+
+GEN_TOTAL = SIGMA_INIT**2 + SIGMA_DATA**2
+GEN_IN = GEN_TOTAL**-0.5
+GEN_SKIP = SIGMA_DATA**2 / GEN_TOTAL
+GEN_OUT = SIGMA_INIT * SIGMA_DATA * GEN_TOTAL**-0.5
+T_IN, T_SKIP, T_OUT, T_SIGMA, T_FACTOR = range(5)
+
+
+def score_kernel(*refs):
+    (
+        z_all, eps_all, gen_w, fake_w, teacher_w, smalls, gen_eo, score_eo, score_eot, tab,
+        gw_out, sv_x, sv_h, sv_y, sv_q, sv_a, sv_o, sv_s, gen_cot, fshard, fsg, sums,
+        *refs,
+    ) = refs
+    gen_out = (sv_x, sv_h, sv_y, sv_q, sv_a, sv_o, sv_s)
+    w_gen, w_fake, w_teach = refs[:3]
+    sv_one, sv_two = refs[3:10], refs[10:17]
+    bufs, nbuf, qkvw, tmp, dn, dqkv, act_t = refs[17:24]
+    zb, eb, g, stage, local_sem, send_sem, recv_sem, copy_sem = refs[24:32]
+    sib, rb, rc, rd, ssem, rsem = refs[32:38]
+    images = zb.shape[0]
     me = Place()
-    for n in range(nets):
-        stage[n] = ws[n][...].astype(BF16)
+    start = me.sec * images
+
+    def mine(ref):
+        return ref.at[pl.ds(start, images)]
+
+    loads = [
+        pltpu.make_async_copy(mine(z_all), zb, copy_sem.at[0]),
+        pltpu.make_async_copy(mine(eps_all), eb, copy_sem.at[1]),
+    ]
+    for copy in loads:
+        copy.start()
+    for n, w in enumerate((gen_w, fake_w, teacher_w)):
+        stage[n] = w[...].astype(BF16)
+    clear_pads(bufs)
+    gathers = [
+        Gather(me, net, stage.at[n], local_sem.at[n], send_sem.at[n], recv_sem.at[n])
+        for n, net in enumerate((w_gen, w_fake, w_teach))
+    ]
     me.meet()
-
-    def rows(plane, y, x, lo, count):
-        at = me.sec * ROWS + (plane * PLANE + y * 2 + x) * part + lo
-        return pl.ds(pl.multiple_of(at, 16), count)
-
-    sends = []
-
-    def send(n, slot, where, target, src=None):
-        piece = outs[n].at[where]
-        copy = remote(
-            piece if src is None else src, piece, send_sem.at[n, slot], recv_sem.at[n, slot], target
-        )
+    for gather in gathers:
+        gather.begin()
+
+    def run(steps):
+        for step in steps:
+            step()
+
+    def forward(n, w, eo, sv, pump):
+        def body(l, _):
+            layer_forward(
+                l, w, smalls.at[n], eo, *sv, bufs, nbuf, qkvw, tmp, True, pump
+            )
+            return 0
+
+        lax.fori_loop(0, 2, body, 0)
+
+    def backward(n, w, sv, cot, grad, sgrad, pump):
+        def body(k, _):
+            layer_backward(
+                1 - k, w, smalls.at[n], score_eot, *sv, cot, bufs, nbuf, qkvw, tmp, dn, dqkv,
+                act_t, grad, sgrad, pump,
+            )
+            return 0
+
+        lax.fori_loop(0, 2, body, 0)
+
+    def each(f):
+        def body(i, carry):
+            return f(i, [tab[start + i, k] for k in range(5)], carry)
+
+        return lax.fori_loop(0, images, body, jnp.zeros((1, C), F32))
+
+    run(gathers[0].phase1() + gathers[0].phase2() + gathers[1].phase1() + gathers[0].phase3())
+    for copy in loads:
+        copy.wait()
+    sv_one[0][0] = zb[...] * (GEN_IN * SIGMA_INIT)
+    run(gathers[0].finish())
+    later = gathers[1].phase2()
+    forward(0, w_gen, gen_eo, sv_one, Pump(later[:5], FORWARD_POINTS, (0, 1)))
+    stores = [pltpu.make_async_copy(w_gen, gw_out, copy_sem.at[2])]
+    for k, (src, dst) in enumerate(zip(sv_one, gen_out)):
+        stores.append(pltpu.make_async_copy(src, dst, copy_sem.at[3 + k]))
+    for copy in stores:
         copy.start()
-        sends.append(copy)
-
-    def arrived(n, slot, where):
-        piece = outs[n].at[where]
-        remote(piece, piece, send_sem.at[n, slot], recv_sem.at[n, slot], me.sib).wait_recv()
-
-    def own(j):
-        return rows(me.plane(-j), me.y, me.x, 0, part)
-
-    def begin(n):
-        for j in (1, 2, 3):
-            send(n, Z1 + j - 1, own(0), me.zpeer(j), stage.at[n])
-        for slot, target in ((X1, me.xn), (Y1, me.yn), (S_OWN, me.sib)):
-            send(n, slot, own(0), target, stage.at[n])
-        copy = pltpu.make_async_copy(stage.at[n], outs[n].at[own(0)], local_sem.at[n])
-        copy.start()
-        return copy
-
-    def phase1(n):
-        for j in (1, 2, 3):
-            arrived(n, Z1 + j - 1, own(j))
-            for slot, target in ((X1, me.xn), (Y1, me.yn), (S_OWN, me.sib)):
-                send(n, slot + j, own(j), target)
-
-    def phase2(n):
-        for j in range(PLANES):
-            plane = me.plane(-j)
-            arrived(n, X1 + j, rows(plane, me.y, 1 - me.x, 0, part))
-            send(n, Y2 + j, rows(plane, me.y, 1 - me.x, 0, half), me.yn)
-            send(n, S_X + j, rows(plane, me.y, 1 - me.x, 0, part), me.sib)
-            arrived(n, Y1 + j, rows(plane, 1 - me.y, me.x, 0, part))
-            send(n, X2 + j, rows(plane, 1 - me.y, me.x, half, half), me.xn)
-            send(n, S_Y + j, rows(plane, 1 - me.y, me.x, 0, part), me.sib)
-
-    def phase3(n):
-        for j in range(PLANES):
-            plane = me.plane(-j)
-            for slot, to, lo in ((Y2, S_DA, 0), (X2, S_DB, half)):
-                where = rows(plane, 1 - me.y, 1 - me.x, lo, half)
-                arrived(n, slot + j, where)
-                send(n, to + j, where, me.sib)
-
-    def finish(n):
-        for slot in range(S_OWN, SLOTS):
-            arrived(n, slot, pl.ds(0, part if slot < S_DA else half))
-
-    locals_ = [begin(n) for n in range(nets)]
-    phase1(0)
-    phase2(0)
-    for n in range(1, nets):
-        phase1(n)
-        phase3(n - 1)
-        phase2(n)
-    phase3(nets - 1)
-    for n in range(nets):
-        finish(n)
-    for copy in locals_:
+
+    def noisy(i, t, carry):
+        zb[i] = zb[i] * (GEN_SKIP * SIGMA_INIT) + GEN_OUT * sv_one[0][2, i]
+        eb[i] = zb[i] + t[T_SIGMA] * eb[i]
+        sv_two[0][0, i] = t[T_IN] * eb[i]
+        return carry
+
+    each(noisy)
+    run(later[5:] + gathers[2].phase1() + gathers[1].phase3() + gathers[1].finish())
+    later = gathers[2].phase2()
+    forward(1, w_fake, score_eo, sv_two, Pump(later[:6], FORWARD_POINTS, (0, 1)))
+    later = later[6:] + gathers[2].phase3()
+
+    def fake_loss(i, t, total):
+        den = t[T_SKIP] * eb[i] + t[T_OUT] * sv_two[0][2, i]
+        sv_two[0][2, i] = den
+        miss = den - zb[i]
+        g[i] = (2.0 * t[T_OUT] * t[T_FACTOR]) * miss
+        return total + t[T_FACTOR] * colsum(miss * miss)
+
+    loss_fake = each(fake_loss)
+    for copy in stores:
         copy.wait()
-    for copy in sends:
-        copy.wait_send()
-
-
-def gather_nets(*ws):
-    part = ws[0].shape[0]
-    nets = len(ws)
-    outs = pl.pallas_call(
-        gather_kernel,
-        out_shape=[jax.ShapeDtypeStruct((2 * ROWS, C), BF16)] * nets,
-        in_specs=vm(nets),
-        out_specs=[pl.BlockSpec(memory_space=pl.ANY)] * nets,
-        scratch_shapes=[
-            pltpu.VMEM((nets, part, C), BF16),
-            pltpu.SemaphoreType.DMA((nets,)),
-            pltpu.SemaphoreType.DMA((nets, SLOTS)),
-            pltpu.SemaphoreType.DMA((nets, SLOTS)),
+    gathers[0].drain()
+    fsg[...] = jnp.zeros(fsg.shape, F32)
+    backward(1, w_fake, sv_two, g, w_gen, fsg, Pump(later, BACKWARD_POINTS, (1, 0)))
+    reduce = Reduce(me, w_gen, fshard, sib, rb, rc, rd, ssem, rsem)
+    reduce.begin()
+    run(gathers[2].finish())
+    later = reduce.steps()
+    sv_one[0][0] = sv_two[0][0]
+    forward(2, w_teach, score_eo, sv_one, Pump(later[:5], FORWARD_POINTS, (0, 1), 0.2))
+
+    def gen_loss(i, t, total):
+        den = t[T_SKIP] * eb[i] + t[T_OUT] * sv_one[0][2, i]
+        miss = sv_two[0][2, i] - zb[i]
+        gap = den - sv_two[0][2, i]
+        scale = t[T_OUT] * t[T_FACTOR]
+        g[i] = scale * ((2.0 * (1.0 - ALPHA_MIX)) * gap + miss)
+        gen_cot[i] = scale * ((1.0 - 2.0 * (1.0 - ALPHA_MIX)) * gap - miss)
+        zb[i] = (t[T_FACTOR] * (t[T_SKIP] - 1.0)) * gap
+        return total + t[T_FACTOR] * colsum(gap * ((1.0 - ALPHA_MIX) * gap + miss))
+
+    loss_gen = each(gen_loss)
+    backward(2, w_teach, sv_one, g, None, None, Pump(later[5:9], BACKWARD_POINTS, (1, 0)))
+    backward(1, w_fake, sv_two, gen_cot, None, None, Pump(later[9:], BACKWARD_POINTS, (1, 0)))
+
+    def gen_gradient(i, t, carry):
+        gen_cot[i] = GEN_OUT * (zb[i] + t[T_IN] * (g[i] + gen_cot[i]))
+        return carry
+
+    each(gen_gradient)
+    sums[...] = jnp.concatenate(
+        [
+            jnp.broadcast_to(jnp.sum(total, axis=1, keepdims=True), (1, C))
+            for total in (loss_gen, loss_fake)
+        ]
+        + [jnp.zeros((6, C), F32)],
+        axis=0,
+    )
+    for gather in gathers[1:]:
+        gather.drain()
+    reduce.drain()
+
+
+def run_score(z, eps, gen_w, fake_w, teacher_w, smalls, gen_eo, score_eo, score_eot, tab):
+    part = gen_w.shape[0]
+    images = z.shape[0] // 2
+    any_ = pl.BlockSpec(memory_space=pl.ANY)
+    saved = saved_shapes(images)
+    return pl.pallas_call(
+        score_kernel,
+        out_shape=[jax.ShapeDtypeStruct((2, ROWS, C), BF16)]
+        + saved
+        + [
+            jax.ShapeDtypeStruct((images, POS, C), F32),
+            jax.ShapeDtypeStruct((part, C), F32),
+            jax.ShapeDtypeStruct((2, 16, C), F32),
+            jax.ShapeDtypeStruct((8, C), F32),
         ],
+        in_specs=[any_] * 2 + vm(7) + [pl.BlockSpec(memory_space=pltpu.SMEM)],
+        out_specs=[any_] * 8 + vm(4),
+        scratch_shapes=[pltpu.VMEM((2, ROWS, C), BF16)] * 3
+        + saved_scratch(images) * 2
+        + backward_scratch(images)
+        + [pltpu.VMEM((images, POS, C), F32)] * 3
+        + [
+            pltpu.VMEM((3, part, C), BF16),
+            pltpu.SemaphoreType.DMA((3,)),
+            pltpu.SemaphoreType.DMA((3, SLOTS)),
+            pltpu.SemaphoreType.DMA((3, SLOTS)),
+            pltpu.SemaphoreType.DMA((10,)),
+        ]
+        + reduce_scratch(part),
         compiler_params=pltpu.CompilerParams(
             collective_id=0, has_side_effects=True, vmem_limit_bytes=VMEM_LIMIT
         ),
-    )(*ws)
-    return [a.reshape(2, ROWS, C) for a in outs]
-
-
-A_SLOT, B_SLOT, C_SLOT, D_SLOT = 0, 4, 20, 28
-R_SLOTS = 31
-
-
-def reduce_kernel(*refs):
-    nets = 2
-    gb, sg = refs[:nets], refs[nets]
-    shard, stot, sqtot = refs[nets + 1 : nets + 4]
-    own, sib, rb, rc, rd, sbuf, srecv, qbuf, qrecv, lsem, ssem, rsem, tsem, urem = refs[nets + 4 :]
-    part = shard.shape[1]
-    half = part // 2
-    span = PLANE * part
+    )(z, eps, gen_w, fake_w, teacher_w, smalls, gen_eo, score_eo, score_eot, tab)
+
+
+def gen_kernel(*refs):
+    (
+        cot, w, small, eot, xs, h1, y, qkv, att, o, st, fsg, sums, fshard,
+        shard, stot, sqtot,
+        big, g, bufs, nbuf, qkvw, tmp, dn, dqkv, act_t, *refs,
+    ) = refs
+    sib, rb, rc, rd, ssem, rsem = refs[:6]
+    small_refs, square_refs = refs[6:10], refs[10:14]
+    sgrad, part_sums = refs[14:16]
     me = Place()
     me.meet()
-    sends = []
-
-    def send(src, dst, s, r, target):
-        copy = remote(src, dst, s, r, target)
-        copy.start()
-        sends.append(copy)
-
-    def arrived(dst, s, r):
-        remote(dst, dst, s, r, me.sib).wait_recv()
-
-    def zt(k):
-        return me.plane(1 + k)
-
-    def block(base, k):
-        return pl.ds(pl.multiple_of(base + zt(k) * span, 16), span)
-
-    def piece(k, y, x, lo, count):
-        at = (zt(k) * PLANE + y * 2 + x) * part + lo
-        return pl.ds(pl.multiple_of(at, 16), count)
-
-    loads = {}
-    for n in range(nets):
-        for k in range(PLANES):
-            there, here = block((1 - me.sec) * ROWS, k), block(me.sec * ROWS, k)
-            slot = A_SLOT + k
-            send(
-                gb[n].at[there], sib.at[n, block(0, k)], ssem.at[n, slot], rsem.at[n, slot], me.sib
-            )
-            copy = pltpu.make_async_copy(gb[n].at[here], own.at[n, block(0, k)], lsem.at[n, k])
-            copy.start()
-            loads[n, k] = copy
-
-    def totals(buf, recv, sem_s, sem_r, base, first):
-        steps = ((0, me.sib), (1, me.xn), (2, me.yn))
-        for slot, target in steps:
-            if slot == 0 and first is not None:
-                src = first
-            else:
-                src = buf.at[slot]
-            send(src, recv.at[slot], sem_s.at[base + slot], sem_r.at[base + slot], target)
-            arrived(recv.at[slot], sem_s.at[base + slot], sem_r.at[base + slot])
-            buf[slot + 1] = buf[slot] + recv[slot]
-        recv[3 + me.z] = buf[3]
-        for j in (1, 2, 3):
-            at = base + 2 + j
-            send(buf.at[3], recv.at[3 + me.z], sem_s.at[at], sem_r.at[at], me.zpeer(j))
-        for j in (1, 2, 3):
-            at = base + 2 + j
-            arrived(recv.at[3 + me.plane(-j)], sem_s.at[at], sem_r.at[at])
-        return (recv[3] + recv[4]) + (recv[5] + recv[6])
-
-    def add_rows(dst, src, n_rows, step):
-        def body(i, _):
-            r = pl.multiple_of(i * step, 16)
-            a, at = dst(r, step)
-            b, bt = src(r, step)
-            a[at] = (a[at].astype(F32) + b[bt].astype(F32)).astype(BF16)
-            return 0
-
-        lax.fori_loop(0, n_rows // step, body, 0)
-
-    def stage_a(n, k):
-        slot = A_SLOT + k
-        loads[n, k].wait()
-        arrived(sib.at[n, block(0, k)], ssem.at[n, slot], rsem.at[n, slot])
-        base = zt(k) * span
-        step = part
-
-        def at(ref):
-            return lambda r, c: (ref, (n, pl.ds(pl.multiple_of(base + r, 16), c), slice(None)))
-
-        add_rows(at(own), at(sib), span, step)
-        for j in range(2):
-            slot = B_SLOT + 4 * k + j
-            send(
-                own.at[n, piece(k, 1 - me.y, j, 0, half)], rb.at[n, k, j],
-                ssem.at[n, slot], rsem.at[n, slot], me.yn,
-            )
-            slot = B_SLOT + 4 * k + 2 + j
-            send(
-                own.at[n, piece(k, j, 1 - me.x, half, half)], rb.at[n, k, 2 + j],
-                ssem.at[n, slot], rsem.at[n, slot], me.xn,
-            )
-
-    def join(n, where, recv_ref, at):
-        own[(n, where, slice(None))] = (
-            own[(n, where, slice(None))].astype(F32) + recv_ref[at].astype(F32)
-        ).astype(BF16)
-
-    def stage_c(n, k):
-        for j in range(4):
-            slot = B_SLOT + 4 * k + j
-            arrived(rb.at[n, k, j], ssem.at[n, slot], rsem.at[n, slot])
-            where = piece(k, me.y, j, 0, half) if j < 2 else piece(k, j - 2, me.x, half, half)
-            join(n, where, rb, (n, k, j))
-        slot = C_SLOT + 2 * k
-        send(
-            own.at[n, piece(k, me.y, 1 - me.x, 0, half)], rc.at[n, k, 0],
-            ssem.at[n, slot], rsem.at[n, slot], me.xn,
+    clear_pads(bufs)
+    g[...] = cot[...]
+    sgrad[...] = jnp.zeros(sgrad.shape, F32)
+    reduce = Reduce(me, big, shard, sib, rb, rc, rd, ssem, rsem)
+
+    def body(k, _):
+        layer_backward(
+            1 - k, w, small, eot, xs, h1, y, qkv, att, o, st, g, bufs, nbuf, qkvw, tmp, dn, dqkv,
+            act_t, big, sgrad, no_pump,
         )
-        slot += 1
-        send(
-            own.at[n, piece(k, 1 - me.y, me.x, half, half)], rc.at[n, k, 1],
-            ssem.at[n, slot], rsem.at[n, slot], me.yn,
-        )
-
-    def stage_d(n, k):
-        for j in range(2):
-            slot = C_SLOT + 2 * k + j
-            arrived(rc.at[n, k, j], ssem.at[n, slot], rsem.at[n, slot])
-            where = piece(k, me.y, me.x, j * half, half)
-            if k < PLANES - 1:
-                join(n, where, rc, (n, k, j))
-            else:
-                shard[n, j * half : (j + 1) * half, :] = (
-                    own[(n, where, slice(None))].astype(F32) + rc[n, k, j].astype(F32)
-                )
-        if k < PLANES - 1:
-            slot = D_SLOT + k
-            send(
-                own.at[n, piece(k, me.y, me.x, 0, part)], rd.at[n, k],
-                ssem.at[n, slot], rsem.at[n, slot], me.zpeer(1 + k),
-            )
-
-    def stage_e(n):
-        for k in range(PLANES - 1):
-            slot = D_SLOT + k
-            arrived(rd.at[n, k], ssem.at[n, slot], rsem.at[n, slot])
-        shard[n] = (
-            shard[n] + rd[n, 0].astype(F32) + (rd[n, 1].astype(F32) + rd[n, 2].astype(F32))
-        )
-
-    order = [(n, k) for n in range(nets) for k in range(PLANES)]
-    lag_c, lag_d = 1, 2
-    for t in range(len(order) + lag_d):
-        if t < len(order):
-            stage_a(*order[t])
-        if 0 <= t - lag_c < len(order):
-            stage_c(*order[t - lag_c])
-        if 0 <= t - lag_d < len(order):
-            stage_d(*order[t - lag_d])
-    sbuf[0] = sg[me.sec]
-    stot[...] = totals(sbuf, srecv, tsem, urem, 0, sg.at[1 - me.sec])
-    for n in range(nets):
-        stage_e(n)
+        return 0
+
+    lax.fori_loop(0, 2, body, 0)
+    reduce.begin()
+    for s in range(2):
+        part_sums[s, 0:16, :] = sgrad[s]
+        part_sums[s, 13:16, :] = sums[0:3, :]
+        part_sums[s, 16:32, :] = fsg[s]
+    small = Totals(me, *small_refs)
+    small_refs[0][0] = part_sums[me.sec]
+    small.begin(part_sums.at[1 - me.sec])
+    steps = reduce.steps()
+    for k, step in enumerate(steps):
+        step()
+        if k in (3, 5, 7):
+            small.steps()[(k - 3) // 2]()
+    stot[...] = small.result()
     lane = lax.broadcasted_iota(jnp.int32, (8, HALF), 1)
     tile = jnp.zeros((8, HALF), F32)
-    for n in range(nets):
-        big = jnp.sum(shard[n] * shard[n])
+    for n, own in enumerate((shard, fshard)):
+        big_sum = jnp.sum(own[...] * own[...])
         low = jnp.sum(stot[16 * n : 16 * n + 13, :] * stot[16 * n : 16 * n + 13, :])
-        tile = jnp.where(lane == n, big + jnp.where(me.d == 0, low, 0.0), tile)
-    qbuf[0] = tile
-    sqtot[...] = totals(qbuf, qrecv, tsem, urem, 6, None)
-    for copy in sends:
-        copy.wait_send()
-
-
-def reduce_nets(bigs, small, part):
-    nets = len(bigs)
-    half = part // 2
+        tile = jnp.where(lane == n, big_sum + jnp.where(me.d == 0, low, 0.0), tile)
+    square = Totals(me, *square_refs)
+    square_refs[0][0] = tile
+    square.begin(square_refs[0].at[0])
+    for step in square.steps():
+        step()
+    sqtot[...] = square.result()
+    reduce.drain()
+    small.drain()
+    square.drain()
+
+
+def run_gen(cot, w, small, eot, saved, fsg, sums, fshard):
+    images = cot.shape[0]
+    part = fshard.shape[0]
     return pl.pallas_call(
-        reduce_kernel,
+        gen_kernel,
         out_shape=[
-            jax.ShapeDtypeStruct((nets, part, C), F32),
-            jax.ShapeDtypeStruct(small.shape[1:], F32),
+            jax.ShapeDtypeStruct((part, C), F32),
+            jax.ShapeDtypeStruct((32, C), F32),
             jax.ShapeDtypeStruct((8, HALF), F32),
         ],
-        in_specs=[pl.BlockSpec(memory_space=pl.ANY)] * nets + vm(1),
+        in_specs=vm(14),
         out_specs=vm(3),
-        scratch_shapes=[
-            pltpu.VMEM((nets, ROWS, C), BF16),
-            pltpu.VMEM((nets, ROWS, C), BF16),
-            pltpu.VMEM((nets, PLANES, 4, half, C), BF16),
-            pltpu.VMEM((nets, PLANES, 2, half, C), BF16),
-            pltpu.VMEM((nets, PLANES - 1, part, C), BF16),
-            pltpu.VMEM((4,) + small.shape[1:], F32),
-            pltpu.VMEM((7,) + small.shape[1:], F32),
-            pltpu.VMEM((4, 8, HALF), F32),
-            pltpu.VMEM((7, 8, HALF), F32),
-            pltpu.SemaphoreType.DMA((nets, PLANES)),
-            pltpu.SemaphoreType.DMA((nets, R_SLOTS)),
-            pltpu.SemaphoreType.DMA((nets, R_SLOTS)),
-            pltpu.SemaphoreType.DMA((12,)),
-            pltpu.SemaphoreType.DMA((12,)),
-        ],
+        scratch_shapes=[pltpu.VMEM((2, ROWS, C), BF16), pltpu.VMEM((images, POS, C), F32)]
+        + backward_scratch(images)
+        + reduce_scratch(part)
+        + totals_scratch((32, C))
+        + totals_scratch((8, HALF))
+        + [pltpu.VMEM((2, 16, C), F32), pltpu.VMEM((2, 32, C), F32)],
         compiler_params=pltpu.CompilerParams(
             collective_id=1, has_side_effects=True, vmem_limit_bytes=VMEM_LIMIT
         ),
-    )(*[b.reshape(2 * ROWS, C) for b in bigs], small)
+    )(cot, w, small, eot, *saved, fsg, sums, fshard)
 
 
 def adam_step(master, first_mom, second_mom, grad):
@@ -892,7 +1172,7 @@
 SMALL_STATES = (4, 5, 6, 7, 11, 12, 13)
 
 
-def update_kernel(shard, stot, sqtot, *refs):
+def update_kernel(gshard, fshard, stot, sqtot, *refs):
     ins, outs = refs[:14], refs[14:]
     nums = outs[14]
     count = stot[15:16, 0:1]
@@ -915,14 +1195,14 @@
         if ema is not None:
             oe[at] = EMA_RATE * ema[at] + (1.0 - EMA_RATE) * new
 
-    one(0, shard[0] * scales[0], *ins[0:4], *outs[0:4])
-    one(0, shard[1] * scales[1], *ins[8:11], None, *outs[8:11], None)
+    one(0, gshard[...] * scales[0], *ins[0:4], *outs[0:4])
+    one(0, fshard[...] * scales[1], *ins[8:11], None, *outs[8:11], None)
     for k in range(13):
         one(k, stot[k : k + 1, :] * scales[0], *ins[4:8], *outs[4:8])
         one(k, stot[16 + k : 17 + k, :] * scales[1], *ins[11:14], None, *outs[11:14], None)
 
 
-def update_nets(shard, stot, sqtot, states):
+def update_nets(gshard, fshard, stot, sqtot, states):
     def turned(arrays):
         return [a.swapaxes(0, 1) if k in SMALL_STATES else a for k, a in enumerate(arrays)]
 
@@ -931,10 +1211,10 @@
         update_kernel,
         out_shape=[jax.ShapeDtypeStruct(a.shape, F32) for a in states]
         + [jax.ShapeDtypeStruct((8, HALF), F32)],
-        in_specs=vm(3 + len(states)),
+        in_specs=vm(4 + len(states)),
         out_specs=vm(len(states) + 1),
         compiler_params=pltpu.CompilerParams(vmem_limit_bytes=VMEM_LIMIT),
-    )(shard, stot, sqtot, *states)
+    )(gshard, fshard, stot, sqtot, *states)
     nums = res[-1]
     return tuple(turned(res[:-1])) + (nums[0, 0:2], nums[0, 2:4])
 
@@ -956,7 +1236,7 @@
         low = jnp.sum(jnp.square(stot[16 * n : 16 * n + 13]))
         squares.append(jnp.sum(own * own) + jnp.where(first, low, 0.0))
     sq = lax.psum(jnp.stack(squares), ("section", "dp"))
-    return jnp.stack(shards_), stot, jnp.zeros((8, HALF), F32).at[:, 0:2].set(sq)
+    return *shards_, stot, jnp.zeros((8, HALF), F32).at[:, 0:2].set(sq)
 
 
 def shards(
@@ -966,70 +1246,38 @@
     teacher_w, teacher_small,
 ):
     section_idx = lax.axis_index("section")
-    sections = lax.axis_size("section")
-    custom = lax.axis_size("dp") == PLANES * PLANE
     per_group = z_noise.shape[0]
-    images = per_group // sections
+    images = per_group // lax.axis_size("section")
     start = section_idx * images
-    elements = POS * C
 
     def mine(a):
         return lax.dynamic_slice_in_dim(a, start, images, 0)
 
-    def wide(a):
-        return a[:, None, None]
-
-    z = mine(z_noise)
-    eps = mine(eps_noise)
-    local_count = counts[0]
-    valid = ((start + jnp.arange(images)) < local_count).astype(F32)
-    sigma = sigma_levels(mine(levels))
-    s_in, s_skip, s_out, s_lam = [wide(t) for t in precondition(sigma)]
-    init = jnp.full((images,), SIGMA_INIT, F32)
-    g_in, g_skip, g_out, _ = [wide(t) for t in precondition(init)]
-    gen_eo, score_eo = spread_embed(init), spread_embed(sigma)
+    valid = (jnp.arange(per_group) < counts[0]).astype(F32)
+    sigma = sigma_levels(levels)
+    s_in, s_skip, s_out, s_lam = precondition(sigma)
+    factor = valid * s_lam / (POS * C)
+    tab = jnp.stack([s_in, s_skip, s_out, sigma, factor] + [jnp.zeros_like(sigma)] * 3, axis=1)
+    gen_eo = spread_embed(jnp.full((images,), SIGMA_INIT, F32))
+    score_eo = spread_embed(mine(sigma))
     gen_eot, score_eot = gen_eo.astype(F32).T, score_eo.astype(F32).T
-
     smalls = lax.all_gather(
-        jnp.concatenate([gen_small, fake_small, teacher_small]), "section", axis=0
+        jnp.concatenate([gen_small, fake_small, teacher_small]), "section", axis=1
     )
-    gs, fs, ts = smalls[:, 0], smalls[:, 1], smalls[:, 2]
-    if custom:
-        gw, fw, tw = gather_nets(gen_w[0], fake_w[0], teacher_w[0])
+    valid_sum = jnp.sum(mine(valid))
+    if lax.axis_size("dp") == PLANES * PLANE:
+        gw, *saved, gen_cot, fshard, fsg, sums = run_score(
+            z_noise, eps_noise, gen_w[0], fake_w[0], teacher_w[0], smalls,
+            gen_eo, score_eo, score_eot, tab,
+        )
+        sums = sums.at[2].set(valid_sum)
+        gshard, stot, sqtot = run_gen(gen_cot, gw, smalls[0], gen_eot, saved, fsg, sums, fshard)
+        reduced = (gshard, fshard, stot, sqtot)
     else:
-        gw, fw, tw = gather_plain(gen_w), gather_plain(fake_w), gather_plain(teacher_w)
-
-    raw = SIGMA_INIT * z
-    gen_saved = run_forward(g_in * raw, gw, gs, gen_eo, True)
-    samples = g_skip * raw + g_out * gen_saved[0][2]
-    noisy = samples + wide(sigma) * eps
-    x0 = s_in * noisy
-    fake_saved = run_forward(x0, fw, fs, score_eo)
-    fake_den = s_skip * noisy + s_out * fake_saved[0][2]
-    factor = wide(valid) * s_lam / elements
-    miss = fake_den - samples
-    _, fake_g, fake_sg = run_backward(s_out * 2.0 * factor * miss, fw, fs, score_eot, fake_saved, True)
-    teacher_saved = run_forward(x0, tw, ts, score_eo)
-    teacher_den = s_skip * noisy + s_out * teacher_saved[0][2]
-    gap = teacher_den - fake_den
-    loss_gen = jnp.sum(factor * ((1.0 - ALPHA_MIX) * gap * gap + gap * miss))
-    loss_fake = jnp.sum(factor * miss * miss)
-    grad_teacher = factor * (2.0 * (1.0 - ALPHA_MIX) * gap + miss)
-    grad_fake = factor * (gap - 2.0 * (1.0 - ALPHA_MIX) * gap - miss)
-    direct = s_skip * (grad_teacher + grad_fake) - factor * gap
-    (back_t,) = run_backward(s_out * grad_teacher, tw, ts, score_eot, teacher_saved, False)
-    (back_f,) = run_backward(s_out * grad_fake, fw, fs, score_eot, fake_saved, False)
-    gen_cot = g_out * (direct + s_in * (back_t + back_f))
-    _, gen_g, gen_sg = run_backward(gen_cot, gw, gs, gen_eot, gen_saved, True)
-
-    scalars = jnp.broadcast_to(jnp.stack([loss_gen, loss_fake, jnp.sum(valid)])[:, None], (3, C))
-    small_sums = jnp.concatenate(
-        [gen_sg[:, :13], jnp.broadcast_to(scalars, (2, 3, C)), fake_sg], axis=1
-    )
-    if custom:
-        reduced = reduce_nets((gen_g, fake_g), small_sums, gen_w.shape[1])
-    else:
-        reduced = reduce_plain((gen_g, fake_g), small_sums)
+        reduced = plain_step(
+            mine(z_noise), mine(eps_noise), gen_w, fake_w, teacher_w, smalls,
+            gen_eo, gen_eot, score_eo, score_eot, mine(tab), valid_sum,
+        )
     return update_nets(
         *reduced,
         (
@@ -1037,6 +1285,42 @@
             fake_w, fake_m, fake_v, fake_small, fake_small_m, fake_small_v,
         ),
     )
+
+
+def plain_step(
+    z, eps, gen_w, fake_w, teacher_w, smalls, gen_eo, gen_eot, score_eo, score_eot, tab, valid_sum
+):
+    gs, fs, ts = smalls[0], smalls[1], smalls[2]
+    gw, fw, tw = gather_plain(gen_w), gather_plain(fake_w), gather_plain(teacher_w)
+    s_in, s_skip, s_out, sigma, factor = [tab[:, k, None, None] for k in range(5)]
+    raw = SIGMA_INIT * z
+    gen_saved = run_forward(GEN_IN * raw, gw, gs, gen_eo)
+    samples = GEN_SKIP * raw + GEN_OUT * gen_saved[0][2]
+    noisy = samples + sigma * eps
+    x0 = s_in * noisy
+    fake_saved = run_forward(x0, fw, fs, score_eo)
+    fake_den = s_skip * noisy + s_out * fake_saved[0][2]
+    miss = fake_den - samples
+    _, fake_g, fake_sg = run_backward(
+        s_out * 2.0 * factor * miss, fw, fs, score_eot, fake_saved, True
+    )
+    teacher_saved = run_forward(x0, tw, ts, score_eo)
+    teacher_den = s_skip * noisy + s_out * teacher_saved[0][2]
+    gap = teacher_den - fake_den
+    loss_gen = jnp.sum(factor * ((1.0 - ALPHA_MIX) * gap * gap + gap * miss))
+    loss_fake = jnp.sum(factor * miss * miss)
+    grad_teacher = factor * (2.0 * (1.0 - ALPHA_MIX) * gap + miss)
+    grad_fake = factor * gap - grad_teacher
+    direct = factor * gap * (s_skip - 1.0)
+    (back_t,) = run_backward(s_out * grad_teacher, tw, ts, score_eot, teacher_saved, False)
+    (back_f,) = run_backward(s_out * grad_fake, fw, fs, score_eot, fake_saved, False)
+    gen_cot = GEN_OUT * (direct + s_in * (back_t + back_f))
+    _, gen_g, gen_sg = run_backward(gen_cot, gw, gs, gen_eot, gen_saved, True)
+    scalars = jnp.broadcast_to(jnp.stack([loss_gen, loss_fake, valid_sum])[:, None], (3, C))
+    small_sums = jnp.concatenate(
+        [gen_sg[:, :13], jnp.broadcast_to(scalars, (2, 3, C)), fake_sg], axis=1
+    )
+    return reduce_plain((gen_g, fake_g), small_sums)
 
 
 def solution(mesh):

time: 378 us -> 270 us (0.71)
  Pallas kernels: 345 us -> 249 us
  other arithmetic: 16.8 us -> 2.38 us
  local copies, waits for them, and re-layouts: 6.9 us -> 10.7 us
    pallas_call x9 -> x2, Pallas kernels: 340 us -> 245 us  [the longest x1 164 us: run_score(): pl.pallas_call(score_kernel, out_shape=[jax.ShapeDtypeStruct((2, ROWS, C)...]
    mul x5 -> x0, other arithmetic: 9.77 us -> none  [the longest x1 2.44 us: shards(): gen_cot = g_out * (direct + s_in * (back_t + back_f))]
where the time goes in v4:
time: 270 us; the launch traced here: 266 us
  Pallas kernels  249 us (92%)
  local copies, waits for them, and re-layouts  10.7 us (4%)
    pallas_call x1, Pallas kernels, run_score(): pl.pallas_call(score_kernel, out_shape=[jax.ShapeDtypeStruct((2, ROWS, C)...  164 us
    pallas_call x1, Pallas kernels, run_gen(): pl.pallas_call(gen_kernel, out_shape=[jax.ShapeDtypeStruct((part, C), F32...  80.6 us

profile of v4, /device:TPU:0, one launch (start us, length us, event | category | flops | bytes accessed | tf_op | source)
XLA Modules:
  0.0 266.1 jit_solution(4103754492545687977)
XLA Ops:
  1.3 0.7 fusion.7
  2.1 0.1 fusion.5
  2.2 0.3 copy.79
  2.6 0.1 broadcast.186.clone
  2.8 0.4 fusion.10
  3.2 0.5 reshape.202
  3.7 0.5 reshape.203
  4.3 0.5 reshape.204
  4.8 0.5 reshape.205
  5.3 0.6 fusion.8
  6.0 1.0 copy.68
  7.0 0.1 copy.69
  7.5 0.7 stack.43.refs_9_
  8.2 2.2 all-gather
  10.4 0.7 copy.75.refs_5_
  11.0 164.0 %shard_map.315 = (bf16[2,6656,256]{2,1,0:T(8,128)(2,1)}, f32[3,3,256,256]{3,2,1,0:T(8,128)}, f32[2,3,256,256]{3,2,1,0:T(8,128)}, f32[2,3,256,256]{3,2,1,0:T(8,12...) custom-call(f32[6,256,256]{2,1,0:T(8,128)} %refs_0_.2, ...), custom_call_target="tpu_custom_call" | custom-call | tf_op jit(solution)/shard_map/pallas_call | solution.py:1051
  175.1 0.7 dynamic-slice_reduce_fusion
  175.7 0.6 broadcast.182
  176.4 1.3 scatter.4.refs_12_
  177.7 1.0 copy.74
  178.8 0.6 squeeze.25.refs_2_
  179.4 80.6 %shard_map.316 = (f32[416,256]{1,0:T(8,128)}, f32[32,256]{1,0:T(8,128)}, f32[8,128]{1,0:T(8,128)}) custom-call(f32[3,256,256]{2,1,0:T(8,128)} %get-tuple-element.58.refs_0_, bf16[2,6656,256]{2,1,0:T(8,128)(2,1)} %get-tuple-element.59.refs_1_, f32[2,13,256]{2,1,0:T(8,128)} %squeeze.25.refs_2_, f32[1024,8]{1,0:T(8,128)} %bitcast.40, ...), custom_call_target="tpu_custom_call" | custom-call | tf_op jit(solution)/shard_map/pallas_call | solution.py:1139
  260.0 4.6 %shard_map.317 = (f32[1,416,256]{2,1,0:T(8,128)}, f32[1,416,256]{2,1,0:T(8,128)}, f32[1,416,256]{2,1,0:T(8,128)}, f32[1,416,256]{2,1,0:T(8,128)}, f32[13,1,256]{...) custom-call(f32[416,256]{1,0:T(8,128)} %get-tuple-element.70.gshard,, ...), custom_call_target="tpu_custom_call" | custom-call | tf_op jit(solution)/shard_map/pallas_call | solution.py:1210
  264.6 1.3 slice_bitcast_fusion
  (23 shorter events, 0.7 us)
Async XLA Ops:
  3.2 4.9 %copy-start = (f32[1,13,256]{2,0,1:T(1,128)S(1)}, f32[1,13,256]{2,0,1:T(1,128)}, u32[]{:S(2)}) copy-start(f32[1,13,256]{2,0,1:T(1,128)} %param.37) | copy-start | bytes 39940
  3.2 4.9 %copy-start.1 = (f32[1,13,256]{2,0,1:T(1,128)S(1)}, f32[1,13,256]{2,0,1:T(1,128)}, u32[]{:S(2)}) copy-start(f32[1,13,256]{2,0,1:T(1,128)} %param.30) | copy-start | bytes 39940
  3.2 4.9 %copy-start.2 = (f32[1,13,256]{2,0,1:T(1,128)S(1)}, f32[1,13,256]{2,0,1:T(1,128)}, u32[]{:S(2)}) copy-start(f32[1,13,256]{2,0,1:T(1,128)} %param.41) | copy-start | bytes 39940
